TPU v7x, 32 devices: a whole 2x2x4 slice. The times are simulated.
32 devices in a mesh: seq: 8 (over z, x), grp: 4 (over y, core).
Axes of the slice: x: 2, y: 2, z: 4, core: 2. Of those that a mesh axis runs over, the one named last changes fastest.
Arguments:
- streams: float32 [3, 2048, 4096], P(None, 'seq', 'grp'), may hold values from -6 to 6
- short_filters: float32 [3, 3, 4096], P(None, None, 'grp'), may hold values from -3.5 to 3.5
- skip_gain: float32 [4096], P('grp'), may hold values from -4 to 4
- long_filter: float32 [2048, 256], P('seq', 'grp'), may hold values from -0.125 to 0.125
Outputs:
- hyena_output: float32 [256, 8, 4096], P('seq', None, 'grp')
All inputs are finite; a program needn't handle non-finite values.
Results may differ from a plain program's by a relative error of at most 0.00011.
Values sent between devices are 32-bit elements; how exact they have to be, the bound alone decides.
No kernel may reach another device: no remote copies, remote signals or barrier semaphores. Data moves between devices by JAX's collectives and lax.ppermute only.
A program may use at most 64 MiB of HBM per device.

v0:
```python
import functools
import math

import jax
import jax.numpy as jnp
import numpy as np
from jax import lax
from jax.experimental import pallas as pl
from jax.experimental.pallas import tpu as pltpu
from jax.sharding import PartitionSpec as P

LANES = 128
ROWS = 8
VMEM_BYTES = 40 * 1024 * 1024


def passed_along(block, axis, distance):
    devices = range(lax.axis_size(axis))
    route = [(i - distance, i) for i in devices if i - distance in devices]
    return lax.ppermute(block, axis, route)


def contract(pattern, matrix, values):
    return jnp.einsum(pattern, matrix, values, precision=lax.Precision.HIGHEST)


def unit_roots(row_index, col_index, period):
    phase_steps = row_index[:, None] * col_index[None, :] % period
    phases = -2.0 * math.pi / period * phase_steps.astype(jnp.float32)
    return (jnp.cos(phases), jnp.sin(phases))


def rotate(real_part, imag_part, cos_part, sin_part):
    return (
        real_part * cos_part - imag_part * sin_part,
        real_part * sin_part + imag_part * cos_part,
    )


def unrotate(real_part, imag_part, cos_part, sin_part):
    return (
        real_part * cos_part + imag_part * sin_part,
        imag_part * cos_part - real_part * sin_part,
    )


def fine_forward(cos_table, sin_table, real_part, imag_part):
    pattern = "km,imc->ikc"
    return (
        contract(pattern, cos_table, real_part) - contract(pattern, sin_table, imag_part),
        contract(pattern, cos_table, imag_part) + contract(pattern, sin_table, real_part),
    )


def fine_inverse(cos_table, sin_table, real_part, imag_part):
    pattern = "km,ikc->imc"
    return (
        contract(pattern, cos_table, real_part) + contract(pattern, sin_table, imag_part),
        contract(pattern, cos_table, imag_part) - contract(pattern, sin_table, real_part),
    )


def narrow_body(streams, short_filters, skip_gain, long_filter):
    panels = lax.axis_size("seq")
    my_panel = lax.axis_index("seq")
    length = streams.shape[1]
    channels = streams.shape[2]
    slice_len = length // panels
    points = 2 * panels * length
    rim_rows = passed_along(streams[:, length - 2 :, :], "seq", 1)
    extended = jnp.concatenate([rim_rows, streams], axis=1)
    featured = (
        short_filters[:, 0:1, :] * extended[:, 2:, :]
        + short_filters[:, 1:2, :] * extended[:, 1 : length + 1, :]
        + short_filters[:, 2:3, :] * extended[:, 0:length, :]
    )
    query_rows = featured[0]
    gated_rows = featured[1] * featured[2]
    query_cols, gated_cols, filter_cols = (
        lax.all_to_all(
            query_rows.reshape(length, 1, channels), "seq", split_axis=0, concat_axis=1, tiled=True
        ),
        lax.all_to_all(
            gated_rows.reshape(length, 1, channels), "seq", split_axis=0, concat_axis=1, tiled=True
        ),
        lax.all_to_all(
            long_filter.reshape(length, 1, long_filter.shape[1]),
            "seq",
            split_axis=0,
            concat_axis=1,
            tiled=True,
        ),
    )
    coarse = jnp.arange(2 * panels, dtype=jnp.int32)
    cross_cos, cross_sin = unit_roots(coarse, jnp.arange(panels, dtype=jnp.int32), 2 * panels)
    fine_index = jnp.arange(length, dtype=jnp.int32)
    local_cos, local_sin = unit_roots(fine_index, fine_index, length)
    own_rows = my_panel * slice_len + jnp.arange(slice_len, dtype=jnp.int32)
    twist_cos, twist_sin = unit_roots(coarse, own_rows, points)
    own_bins = 2 * my_panel + jnp.arange(2, dtype=jnp.int32)
    turn_cos, turn_sin = unit_roots(own_bins, fine_index, points)
    pattern = "kr,mrc->kmc"
    tap_real, tap_imag = rotate(
        contract(pattern, cross_cos, filter_cols),
        contract(pattern, cross_sin, filter_cols),
        twist_cos[:, :, None],
        twist_sin[:, :, None],
    )
    act_real = contract(pattern, cross_cos, gated_cols)
    act_imag = contract(pattern, cross_sin, gated_cols)
    act_real, act_imag = rotate(act_real, act_imag, twist_cos[:, :, None], twist_sin[:, :, None])
    act_real, act_imag, tap_real, tap_imag = (
        lax.all_to_all(act_real, "seq", split_axis=0, concat_axis=1, tiled=True),
        lax.all_to_all(act_imag, "seq", split_axis=0, concat_axis=1, tiled=True),
        lax.all_to_all(tap_real, "seq", split_axis=0, concat_axis=1, tiled=True),
        lax.all_to_all(tap_imag, "seq", split_axis=0, concat_axis=1, tiled=True),
    )
    act_real, act_imag = fine_forward(local_cos, local_sin, act_real, act_imag)
    tap_real, tap_imag = fine_forward(local_cos, local_sin, tap_real, tap_imag)
    tap_real, tap_imag = (
        lax.all_gather(tap_real, "grp", axis=2, tiled=True),
        lax.all_gather(tap_imag, "grp", axis=2, tiled=True),
    )
    filter_count = tap_real.shape[2]
    blocks = act_real.shape[2] // filter_count
    wide_real = act_real.reshape(2, length, blocks, filter_count)
    wide_imag = act_imag.reshape(2, length, blocks, filter_count)
    tap_wide_real = tap_real[:, :, None, :]
    tap_wide_imag = tap_imag[:, :, None, :]
    prod_real = (wide_real * tap_wide_real - wide_imag * tap_wide_imag).reshape(
        2, length, blocks * filter_count
    )
    prod_imag = (wide_real * tap_wide_imag + wide_imag * tap_wide_real).reshape(
        2, length, blocks * filter_count
    )
    back_real, back_imag = fine_inverse(local_cos, local_sin, prod_real, prod_imag)
    back_real, back_imag = unrotate(
        back_real, back_imag, turn_cos[:, :, None], turn_sin[:, :, None]
    )
    back_real, back_imag = (
        lax.all_to_all(back_real, "seq", split_axis=1, concat_axis=0, tiled=True),
        lax.all_to_all(back_imag, "seq", split_axis=1, concat_axis=0, tiled=True),
    )
    inverse_scale = 1.0 / points
    inverse_pattern = "kr,kmc->mrc"
    convolved = (
        contract(inverse_pattern, cross_cos, back_real)
        + contract(inverse_pattern, cross_sin, back_imag)
    ) * inverse_scale
    return query_cols * (convolved + skip_gain * gated_cols)


def split16(values):
    high = values.astype(jnp.bfloat16)
    low = (values - high.astype(jnp.float32)).astype(jnp.bfloat16)
    return high, low


def transform_tables(length):
    bins = np.arange(length, dtype=np.int64)[:, None]
    taps = np.arange(length, dtype=np.int64)[None, :]
    phases = ((2 * bins + 1) * taps % (4 * length)).astype(np.float64) * (math.pi / (2 * length))
    table = np.concatenate([np.cos(phases), -np.sin(phases)], axis=0).astype(np.float32)
    high = table.astype(jnp.bfloat16)
    low = (table - high.astype(np.float32)).astype(jnp.bfloat16)
    forward = np.concatenate([high, high, low], axis=1)
    inverse = np.concatenate([high.T, high.T, low.T], axis=1)
    return forward, inverse


def tile_of(t):
    return slice(t * LANES, (t + 1) * LANES)


def aligned(start, size):
    return pl.ds(pl.multiple_of(start, size), size)


def swap_tiles_and_slots(tiles, width, me, tiles_out):
    count = len(tiles)
    lane = lax.broadcasted_iota(jnp.int32, tiles[0].shape, 1)
    slot = lane // width % count
    mine = slot ^ me
    step = 1
    while step < count:
        upper = (slot & step) != 0
        other = (mine & step) != 0
        first, second = (upper, other) if tiles_out else (other, upper)
        partner = lane ^ (step * width)
        turned = list(tiles)
        for t in range(count):
            if t & step:
                continue
            low, high = tiles[t], tiles[t | step]
            moved = jnp.take_along_axis(jnp.where(first, low, high), partner, axis=1)
            kept = jnp.where(first, high, low)
            turned[t] = jnp.where(second, moved, kept)
            turned[t | step] = jnp.where(second, kept, moved)
        tiles = turned
        step *= 2
    return tiles


def short_filtered(taps, s, columns, now, before):
    shape = now.shape
    row = lax.broadcasted_iota(jnp.int32, shape, 0) % ROWS

    def later(rows):
        mixed = jnp.where(row >= ROWS - rows, before, now)
        blocks = mixed.reshape(shape[0] // ROWS, ROWS, shape[1])
        return pltpu.roll(blocks, rows, 1).reshape(shape)

    return (
        taps[s, 0:1, columns] * now
        + taps[s, 1:2, columns] * later(1)
        + taps[s, 2:3, columns] * later(2)
    )


def in_vmem():
    return pl.BlockSpec(memory_space=pltpu.VMEM)


def in_smem():
    return pl.BlockSpec(memory_space=pltpu.SMEM)


def in_any():
    return pl.BlockSpec(memory_space=pl.ANY)


def params_of(limit=VMEM_BYTES):
    return pltpu.CompilerParams(vmem_limit_bytes=limit)


def far_first(count):
    half = count // 2
    return [half, half + 1] + list(range(half)) + list(range(half + 2, count))


def by_partner(refs):
    ordered = [None] * len(refs)
    for k, ref in zip(far_first(len(refs)), refs):
        ordered[k] = ref
    return ordered


def far_first_operands(messages):
    return [messages[k] for k in far_first(len(messages))]


def gate_kernel(count, width, pieces, me_ref, streams, *rest):
    small, rest = rest[:3], rest[3:]
    messages, rest = rest[:count], rest[count:]
    params, key, value, taps, skip, long_filter, sems = rest
    length = streams.shape[1]
    fetches = [
        pltpu.make_async_copy(source, target, sems.at[2 * pieces + i])
        for i, (source, target) in enumerate(zip(small, (taps, skip, long_filter)))
    ]
    for fetch in fetches:
        fetch.start()
    channels = streams.shape[2]
    me = me_ref[0]
    part = length // pieces
    loads = []
    for piece in range(pieces):
        for s, buffer in ((1, key), (2, value)):
            load = pltpu.make_async_copy(
                streams.at[s, pl.ds(piece * part, part)],
                buffer.at[pl.ds(ROWS + piece * part, part)],
                sems.at[2 * piece + s - 1],
            )
            load.start()
            loads.append(load)
    key[0:ROWS, :] = jnp.zeros((ROWS, channels), jnp.float32)
    value[0:ROWS, :] = jnp.zeros((ROWS, channels), jnp.float32)
    for fetch in fetches:
        fetch.wait()
    rows = jnp.concatenate(
        [taps[1], taps[2], skip[...], jnp.zeros((1, channels), jnp.float32)], axis=0
    )
    tiles = [rows[:, tile_of(t)] for t in range(count)]
    params[...] = swap_tiles_and_slots(tiles, width, me, True)[0]
    for k in range(count):
        for t in range(length // LANES):
            at = length + ROWS + t * width
            messages[k][at : at + width, :] = long_filter[aligned((me ^ k) * width, width), tile_of(t)]
    step = 8 * ROWS

    def block(i, _):
        base = i * step
        tiles = []
        for t in range(count):
            features = []
            for s, buffer in ((1, key), (2, value)):
                now = buffer[pl.ds(pl.multiple_of(base + ROWS, ROWS), step), tile_of(t)]
                before = buffer[aligned(base, step), tile_of(t)]
                features.append(short_filtered(taps, s, tile_of(t), now, before))
            tiles.append(features[0] * features[1])
        tiles = swap_tiles_and_slots(tiles, width, me, True)
        for k in range(count):
            messages[k][aligned(base, step), :] = tiles[k]
        return 0

    for piece in range(pieces):
        loads[2 * piece].wait()
        loads[2 * piece + 1].wait()
        lax.fori_loop(piece * part // step, (piece + 1) * part // step, block, 0)
    rim = jnp.concatenate(
        [
            key[length + ROWS - 2 : length + ROWS, :],
            value[length + ROWS - 2 : length + ROWS, :],
            key[ROWS : ROWS + 2, :],
            value[ROWS : ROWS + 2, :],
        ],
        axis=0,
    )
    tiles = [rim[:, tile_of(t)] for t in range(count)]
    tiles = swap_tiles_and_slots(tiles, width, me, True)
    for k in range(count):
        messages[k][length : length + ROWS, :] = tiles[k]


def gate(me, streams, short_filters, skip_gain, long_filter, count, width):
    length, channels = streams.shape[1], streams.shape[2]
    rows = length + ROWS + width * length // LANES
    message = jax.ShapeDtypeStruct((rows, LANES), jnp.float32)
    pieces = 4
    return pl.pallas_call(
        functools.partial(gate_kernel, count, width, pieces),
        out_shape=[message] * count + [jax.ShapeDtypeStruct((ROWS, LANES), jnp.float32)],
        in_specs=[in_smem()] + [in_any()] * 4,
        out_specs=[in_vmem()] * (count + 1),
        scratch_shapes=[
            pltpu.VMEM((length + ROWS, channels), jnp.float32),
            pltpu.VMEM((length + ROWS, channels), jnp.float32),
            pltpu.VMEM(short_filters.shape, jnp.float32),
            pltpu.VMEM((1, channels), jnp.float32),
            pltpu.VMEM(long_filter.shape[::-1], jnp.float32),
            pltpu.SemaphoreType.DMA((2 * pieces + 3,)),
        ],
        compiler_params=params_of(60 * 1024 * 1024),
        name="gate",
    )(me, streams, short_filters, skip_gain.reshape(1, channels), long_filter.T)


def collect_kernel(count, width, me_ref, *rest):
    messages, out = by_partner(rest[:count]), rest[count]
    me = me_ref[0]
    size = out.shape[1]
    for k in range(count):
        rows = messages[k].shape[0]
        out[me ^ k] = messages[k][rows - size : rows, :]


def collect_taps(me, messages, count, width, length):
    size = width * length // LANES
    return pl.pallas_call(
        functools.partial(collect_kernel, count, width),
        out_shape=jax.ShapeDtypeStruct((count, size, LANES), jnp.float32),
        in_specs=[in_smem()] + [in_vmem()] * count,
        out_specs=in_vmem(),
        compiler_params=params_of(),
        name="collect_taps",
    )(me, *far_first_operands(messages))


def filter_kernel(count, width, group_ref, params, forward, *rest):
    groups = len(rest) - 3
    taps, (out, columns, spectrum) = rest[:groups], rest[groups:]
    length = out.shape[1] // 2
    halves = LANES // (count * width)
    group = group_ref[0]
    for p in range(count):
        for k in range(groups):
            owner = group ^ k
            for turn in range(count * halves // groups):
                at = (owner + turn * groups) // halves + (owner % halves) * count
                for t in range(length // LANES):
                    columns[p, aligned(at * width, width), tile_of(t)] = taps[k][
                        p, t * width : (t + 1) * width, :
                    ]
    for p in range(count):
        high, low = split16(columns[p])
        stacked = jnp.concatenate([high, low, high], axis=1)
        spectrum[p] = lax.dot_general(
            forward[...], stacked, (((1,), (1,)), ((), ())), preferred_element_type=jnp.float32
        )
    parity = lax.broadcasted_iota(jnp.int32, (length, LANES), 0) % 2
    sign = 1.0 - 2.0 * parity.astype(jnp.float32)
    skip = params[6:7, :]
    for d in range(count):
        real = spectrum[d, 0:length, :]
        imag = spectrum[d, length : 2 * length, :]
        if d > 0:
            real = real - sign * spectrum[d - 1, length : 2 * length, :]
            imag = imag + sign * spectrum[d - 1, 0:length, :]
        else:
            real = real + skip
        out[d, 0:length, :] = real
        out[d, length : 2 * length, :] = imag


def filter_spectra(group, params, forward, taps, count, width):
    length = taps[0].shape[1] // width * LANES
    return pl.pallas_call(
        functools.partial(filter_kernel, count, width),
        out_shape=jax.ShapeDtypeStruct((count, 2 * length, LANES), jnp.float32),
        in_specs=[in_smem()] + [in_vmem()] * (2 + len(taps)),
        out_specs=in_vmem(),
        scratch_shapes=[
            pltpu.VMEM((count, LANES, length), jnp.float32),
            pltpu.VMEM((count, 2 * length, LANES), jnp.float32),
        ],
        compiler_params=params_of(),
        name="filter_spectra",
    )(group, params, forward, *taps)


def convolve_kernel(count, length, me_ref, params, forward, inverse, spectra, *rest):
    messages, rest = by_partner(rest[:count]), rest[count:]
    outs, rest = rest[:count], rest[count:]
    rims, bins, halves, result = rest
    me = me_ref[0]
    rims[0] = jnp.zeros((ROWS, LANES), jnp.float32)
    for k in range(count):
        rims[(me ^ k) + 1] = messages[k][length : length + ROWS, :]
    key_taps = [params[a : a + 1, :] for a in range(3)]
    value_taps = [params[3 + a : 4 + a, :] for a in range(3)]

    def feature(taps, now, before, earlier):
        return taps[0] * now + taps[1] * before + taps[2] * earlier

    pair = 2 * ROWS
    row = lax.broadcasted_iota(jnp.int32, (pair, LANES), 0)
    for k in range(count):
        at = aligned((me ^ k) * LANES, LANES)
        past = rims[me ^ k]
        rim = messages[k][length : length + ROWS, :]
        k254, k255, v254, v255 = (past[a : a + 1, :] for a in range(4))
        k0, k1, v0, v1 = (rim[4 + a : 5 + a, :] for a in range(4))
        first = feature(key_taps, k0, k255, k254) * feature(value_taps, v0, v255, v254)
        second = feature(key_taps, k1, k0, k255) * feature(value_taps, v1, v0, v255)
        top = jnp.where(row == 0, first, jnp.where(row == 1, second, messages[k][0:pair, :]))
        for a, b, values in ((0, pair, top), (pair, length, messages[k][pair:length, :])):
            high, low = split16(values)
            halves[a:b, at] = high
            halves[length + a : length + b, at] = low
            halves[2 * length + a : 2 * length + b, at] = high
    for c in range(0, count, 2):
        columns = slice(c * LANES, (c + 2) * LANES)
        bins[:, columns] = jnp.dot(
            forward[...], halves[0 : 3 * length, columns], preferred_element_type=jnp.float32
        )

    def block(i, _):
        start = pl.multiple_of(i * pair, pair)
        rows = []
        for at in (start, start + ROWS):
            real = [bins[pl.ds(at, ROWS), tile_of(r)] for r in range(count)]
            imag = [bins[pl.ds(length + at, ROWS), tile_of(r)] for r in range(count)]
            tap_real = [spectra[d, pl.ds(at, ROWS), :] for d in range(count)]
            tap_imag = [spectra[d, pl.ds(length + at, ROWS), :] for d in range(count)]
            sums = []
            for r in range(count):
                sum_real = real[r] * tap_real[0] - imag[r] * tap_imag[0]
                sum_imag = real[r] * tap_imag[0] + imag[r] * tap_real[0]
                for d in range(1, r + 1):
                    sum_real += real[r - d] * tap_real[d] - imag[r - d] * tap_imag[d]
                    sum_imag += real[r - d] * tap_imag[d] + imag[r - d] * tap_real[d]
                sums.append((sum_real, sum_imag))
            rows.append(sums)
        for r in range(count):
            for part in range(2):
                both = jnp.concatenate([rows[0][r][part], rows[1][r][part]], axis=0)
                high, low = split16(both)
                base = start + part * length
                halves[pl.ds(base, pair), tile_of(r)] = high
                halves[pl.ds(base + 2 * length, pair), tile_of(r)] = low
                halves[pl.ds(base + 4 * length, pair), tile_of(r)] = high
        return 0

    lax.fori_loop(0, length // pair, block, 0)
    for c in range(0, count, 2):
        columns = slice(c * LANES, (c + 2) * LANES)
        result[:, columns] = jnp.dot(
            inverse[...], halves[:, columns], preferred_element_type=jnp.float32
        )
    scale = 1.0 / length
    part = length // count
    for k in range(count):
        for m in range(0, part, ROWS):
            for r in range(count):
                outs[k][pl.ds(m * count + r, ROWS, stride=count), :] = (
                    result[aligned((me ^ k) * part + m, ROWS), tile_of(r)] * scale
                )


def convolve(me, params, forward, inverse, spectra, messages, count):
    length = spectra.shape[1] // 2
    return pl.pallas_call(
        functools.partial(convolve_kernel, count, length),
        out_shape=[jax.ShapeDtypeStruct((length, LANES), jnp.float32)] * count,
        in_specs=[in_smem()] + [in_vmem()] * (4 + count),
        out_specs=[in_vmem()] * count,
        scratch_shapes=[
            pltpu.VMEM((count + 1, ROWS, LANES), jnp.float32),
            pltpu.VMEM((2 * length, count * LANES), jnp.float32),
            pltpu.VMEM((6 * length, count * LANES), jnp.bfloat16),
            pltpu.VMEM((length, count * LANES), jnp.float32),
        ],
        compiler_params=params_of(),
        name="convolve",
    )(me, params, forward, inverse, spectra, *far_first_operands(messages))


def query_kernel(half, me_ref, streams, taps_in, _, near, far, rows, taps, sems):
    length, channels = streams.shape[1:]
    tiles = channels // LANES
    load = pltpu.make_async_copy(streams.at[0], rows.at[pl.ds(ROWS, length)], sems.at[0])
    fetch = pltpu.make_async_copy(taps_in, taps, sems.at[1])
    load.start()
    fetch.start()
    rows[0:ROWS, :] = jnp.zeros((ROWS, channels), jnp.float32)
    side = me_ref[0] // half
    fetch.wait()
    load.wait()
    step = length // (2 * half)
    for out, at in ((far, 1 - side), (near, side)):

        def block(i, _):
            base = pl.multiple_of(at * (length // 2) + i * step, step)
            for t in range(tiles):
                now = rows[pl.ds(pl.multiple_of(base + ROWS, ROWS), step), tile_of(t)]
                before = rows[aligned(base, step), tile_of(t)]
                target = pl.multiple_of((i * tiles + t) * step, step)
                out[pl.ds(target, step), :] = short_filtered(taps, 0, tile_of(t), now, before)
            return 0

        lax.fori_loop(0, half, block, 0)
    last = rows[length + ROWS - 1 : length + ROWS, :]
    last_but_one = rows[length + ROWS - 2 : length + ROWS - 1, :]
    first = taps[0, 1:2, :] * last + taps[0, 2:3, :] * last_but_one
    second = taps[0, 2:3, :] * last
    end = tiles * (length // 2)
    for t in range(tiles):
        both = jnp.concatenate([first[:, tile_of(t)], second[:, tile_of(t)]], axis=0)
        for out in (near, far):
            out[end + 2 * t : end + 2 * t + 2, :] = both


def query(me, streams, short_filters, params, count):
    length, channels = streams.shape[1:]
    tiles = channels // LANES
    rows = jax.ShapeDtypeStruct((tiles * (length // 2 + 2), LANES), jnp.float32)
    return pl.pallas_call(
        functools.partial(query_kernel, count // 2),
        out_shape=[rows, rows],
        in_specs=[in_smem(), in_any(), in_any(), in_any()],
        out_specs=[in_vmem()] * 2,
        scratch_shapes=[
            pltpu.VMEM((length + ROWS, channels), jnp.float32),
            pltpu.VMEM(short_filters.shape, jnp.float32),
            pltpu.SemaphoreType.DMA((2,)),
        ],
        compiler_params=params_of(60 * 1024 * 1024),
        name="query",
    )(me, streams, short_filters, params)


def hold_kernel(*refs):
    del refs


def hold(value, *others):
    return pl.pallas_call(
        hold_kernel,
        out_shape=jax.ShapeDtypeStruct(value.shape, value.dtype),
        in_specs=[in_any()] * (1 + len(others)),
        out_specs=in_any(),
        input_output_aliases={0: 0},
        compiler_params=params_of(),
        name="hold",
    )(value, *others)


def deal_kernel(half, tiles, me_ref, near, far, *rest):
    results, outs = rest[:half], rest[half:]
    share = (near.shape[0] - 2 * tiles) // half
    place = me_ref[0] % half
    for k in range(half):
        start = pl.multiple_of((place ^ k) * share, share)
        outs[k][0:share, :] = near[pl.ds(start, share), :]
        outs[k][share : 2 * share, :] = far[pl.ds(start, share), :]
        at = 2 * share
        for source in (near, far):
            outs[k][at : at + 2 * tiles, :] = source[half * share : half * share + 2 * tiles, :]
            at += 2 * tiles
        outs[k][at : at + results[k].shape[0], :] = results[k][...]


def deal(me, near, far, results, tiles, count):
    half = count // 2
    size = 2 * (near.shape[0] - 2 * tiles) // half + 4 * tiles + results[0].shape[0]
    return pl.pallas_call(
        functools.partial(deal_kernel, half, tiles),
        out_shape=[jax.ShapeDtypeStruct((size, LANES), jnp.float32)] * half,
        in_specs=[in_smem()] + [in_vmem()] * (2 + half),
        out_specs=[in_vmem()] * half,
        compiler_params=params_of(),
        name="deal",
    )(me, near, far, *results[:half])


def arrange_query(count, me, dealt, out, lacking):
    half = count // 2
    tiles, rows = out.shape[:2]
    part = rows // count
    lacking[...] = jnp.zeros(lacking.shape, jnp.float32)
    for k in range(half):
        for i in range(2):
            r = me ^ k ^ (i * half)
            for t in range(tiles):
                for m in range(0, part, ROWS):
                    at = (i * tiles + t) * part + m
                    out[t, pl.ds(m * count + r, ROWS, stride=count), :] = dealt[k][
                        at : at + ROWS, :
                    ]
                at = 2 * tiles * part + (i * tiles + t) * 2
                lacking[t, pl.ds(r + 1, 2, stride=2 * count), :] = dealt[k][at : at + 2, :]
    first = (me == 0).astype(jnp.float32)
    for t in range(tiles):
        for m in range(2):
            at = slice(m * count, (m + 1) * count)
            out[t, at, :] += first * lacking[t, 2 * m * count : (2 * m + 1) * count, :]


def finish_kernel(count, width, pieces, me_ref, *rest):
    messages, (out, rows, query_rows, lacking, sems) = by_partner(rest[:count]), rest[count:]
    me = me_ref[0]
    part = out.shape[0]
    arrange_query(count, me, messages[: count // 2], query_rows, lacking)
    step = 4
    stores = []

    def block(i, _):
        at = aligned(i * step * count, step * count)
        tiles = []
        for message in messages:
            ahead = message.shape[0] - part * count
            start = pl.multiple_of(ahead + i * step * count, step * count)
            tiles.append(message[pl.ds(start, step * count), :])
        tiles = swap_tiles_and_slots(tiles, width, me, False)
        for t in range(count):
            product = query_rows[t, at, :] * tiles[t]
            for m in range(step):
                rows[i * step + m, :, tile_of(t)] = product[m * count : (m + 1) * count]
        return 0

    size = part // pieces
    for piece in range(pieces):
        lax.fori_loop(piece * size // step, (piece + 1) * size // step, block, 0)
        done = pl.ds(piece * size, size)
        store = pltpu.make_async_copy(rows.at[done], out.at[done], sems.at[piece])
        store.start()
        stores.append(store)
    for store in stores:
        store.wait()


def finish(me, messages, tiles, count, width):
    rows = messages[-1].shape[0]
    part = rows // count
    pieces = 4
    return pl.pallas_call(
        functools.partial(finish_kernel, count, width, pieces),
        out_shape=jax.ShapeDtypeStruct((part, count, tiles * LANES), jnp.float32),
        in_specs=[in_smem()] + [in_vmem()] * count,
        out_specs=in_any(),
        scratch_shapes=[
            pltpu.VMEM((part, count, tiles * LANES), jnp.float32),
            pltpu.VMEM((tiles, rows, LANES), jnp.float32),
            pltpu.VMEM((tiles, 4 * count, LANES), jnp.float32),
            pltpu.SemaphoreType.DMA((pieces,)),
        ],
        compiler_params=params_of(),
        name="finish",
    )(me, *far_first_operands(messages))


def swapped(block, axis, k):
    return lax.ppermute(block, axis, [(i, i ^ k) for i in range(lax.axis_size(axis))])


def exchanged(messages, axis):
    received = {0: messages[0]}
    for k in range(1, len(messages)):
        received[k] = swapped(messages[k], axis, k)
    return [received[k] for k in range(len(messages))]


def wide_body(streams, short_filters, skip_gain, long_filter):
    count = lax.axis_size("seq")
    groups = lax.axis_size("grp")
    place = lax.axis_index("seq").astype(jnp.int32)
    me = place.reshape(1)
    group = lax.axis_index("grp").astype(jnp.int32).reshape(1)
    length = streams.shape[1]
    width = long_filter.shape[1] // count
    forward, inverse = (jnp.asarray(table) for table in transform_tables(length))
    *gated, params = gate(me, streams, short_filters, skip_gain, long_filter, count, width)
    gated = exchanged(gated, "seq")
    half = count // 2
    tiles = streams.shape[2] // LANES
    near, far = query(me, streams, short_filters, params, count)
    far = hold(far, *far_first_operands(gated))
    taps = collect_taps(me, gated, count, width, length)
    taps = [taps] + [swapped(taps, "grp", k) for k in range(1, groups)]
    far = swapped(far, "seq", half)
    spectra = filter_spectra(group, params, forward, taps, count, width)
    convolved = convolve(me, params, forward, inverse, spectra, gated, count)
    dealt = exchanged(deal(me, near, far, convolved, tiles, count), "seq")
    convolved = dealt + [swapped(convolved[k], "seq", k) for k in range(half, count)]
    return finish(me, convolved, tiles, count, width)


def body(streams, short_filters, skip_gain, long_filter):
    count = lax.axis_size("seq")
    width = long_filter.shape[1] // count
    one_tile = streams.shape[2] == count * LANES and count == ROWS
    if one_tile and width == ROWS and LANES % (count * width) == 0:
        return wide_body(streams, short_filters, skip_gain, long_filter)
    return narrow_body(streams, short_filters, skip_gain, long_filter)


def solution(mesh):
    return jax.shard_map(
        body,
        mesh=mesh,
        in_specs=(P(None, "seq", "grp"), P(None, None, "grp"), P("grp"), P("seq", "grp")),
        out_specs=P("seq", None, "grp"),
        check_vma=False,
    )
```

profile of v0, /device:TPU:17, one launch (start us, length us, event | category | flops | bytes accessed | tf_op | source)
XLA Modules:
  0.0 99.1 jit_solution(2546913527985555299)
XLA Ops:
  0.0 3.9 %gate.1 = (f32[280,128]{1,0:T(8,128)}, f32[280,128]{1,0:T(8,128)}, f32[280,128]{1,0:T(8,128)}, f32[280,128]{1,0:T(8,128)}, f32[280,128]{1,0:T(8,128)}, /*index=5...) custom-call(s32[1]{0:T(128)} %bitcast.me_ref, f32[3,256,1024]{2,1,0:T(8,128)} %streams.3, ...), custom_call_target="tpu_custom_call" | custom-call | tf_op jit(solution)/shard_map/gate/pallas_call | solution.py:330
  3.9 0.1 collective-permute-start
  4.0 3.3 %collective-permute-start.1 = (f32[280,128]{1,0:T(8,128)}, f32[280,128]{1,0:T(8,128)S(1)}, u32[]{:S(2)}, u32[]{:S(2)}) collective-permute-start(f32[280,128]{1,0:T(8,128)} %get-tuple-element.30), channel_id=1, source_target_pairs={{0,20},{4,16},{8,28},{12,24},{16,4},{20,0},{24,12},{28,8},{1,21},{... | collective-permute-start | bytes 430088 | tf_op jit(solution)/shard_map/ppermute | solution.py:693
  7.3 0.3 collective-permute-start.2
  7.5 1.3 %collective-permute-start.3 = (f32[280,128]{1,0:T(8,128)}, f32[280,128]{1,0:T(8,128)S(1)}, u32[]{:S(2)}, u32[]{:S(2)}) collective-permute-start(f32[280,128]{1,0:T(8,128)} %get-tuple-element.33), channel_id=1, source_target_pairs={{0,8},{4,12},{8,0},{12,4},{16,24},{20,28},{24,16},{28,20},{1,9},{5... | collective-permute-start | bytes 430088 | tf_op jit(solution)/shard_map/ppermute | solution.py:693
  8.8 1.1 %collective-permute-start.4 = (f32[280,128]{1,0:T(8,128)}, f32[280,128]{1,0:T(8,128)S(1)}, u32[]{:S(2)}, u32[]{:S(2)}) collective-permute-start(f32[280,128]{1,0:T(8,128)} %get-tuple-element.34), channel_id=1, source_target_pairs={{0,12},{4,8},{8,4},{12,0},{16,28},{20,24},{24,20},{28,16},{1,13},{... | collective-permute-start | bytes 430088 | tf_op jit(solution)/shard_map/ppermute | solution.py:693
  9.9 2.3 %collective-permute-done.rest_0_.refs_1_ = f32[280,128]{1,0:T(8,128)S(1)} collective-permute-done((f32[280,128]{1,0:T(8,128)}, f32[280,128]{1,0:T(8,128)S(1)}, u32[]{:S(2)}, u32[]{:S(2)}) %collective-permute-start) | collective-permute-done | bytes 143392 | tf_op jit(solution)/shard_map/ppermute | solution.py:693
  12.2 4.1 %collective-permute-start.5 = (f32[280,128]{1,0:T(8,128)}, f32[280,128]{1,0:T(8,128)S(1)}, u32[]{:S(2)}, u32[]{:S(2)}) collective-permute-start(f32[280,128]{1,0:T(8,128)} %get-tuple-element.35), channel_id=1, source_target_pairs={{0,24},{4,28},{8,16},{12,20},{16,8},{20,12},{24,0},{28,4},{1,25},{... | collective-permute-start | bytes 430088 | tf_op jit(solution)/shard_map/ppermute | solution.py:693
  16.3 4.0 %collective-permute-start.6 = (f32[280,128]{1,0:T(8,128)}, f32[280,128]{1,0:T(8,128)S(1)}, u32[]{:S(2)}, u32[]{:S(2)}) collective-permute-start(f32[280,128]{1,0:T(8,128)} %get-tuple-element.36), channel_id=1, source_target_pairs={{0,28},{4,24},{8,20},{12,16},{16,12},{20,8},{24,4},{28,0},{1,29},{... | collective-permute-start | bytes 430088 | tf_op jit(solution)/shard_map/ppermute | solution.py:693
  20.3 2.7 %query.1 = (f32[1040,128]{1,0:T(8,128)}, f32[1040,128]{1,0:T(8,128)}) custom-call(s32[1]{0:T(128)} %bitcast.me_ref, f32[3,256,1024]{2,1,0:T(8,128)} %streams.3, f32[3,3,1024]{2,1,0:T(4,128)} %taps_in.1, f32[8,128]{1,0:T(8,128)} %get-tuple-element.28.params._), custom_call_target="tpu_custom_call" | custom-call | tf_op jit(solution)/shard_map/query/pallas_call | solution.py:557
  23.0 6.2 %collective-permute-done.5.rest_6_.refs_7_ = f32[280,128]{1,0:T(8,128)S(1)} collective-permute-done((f32[280,128]{1,0:T(8,128)}, f32[280,128]{1,0:T(8,128)S(1)}, u32[]{:S(2)}, u32[]{:S(2)}) %collective-permute-start.5) | collective-permute-done | bytes 143392 | tf_op jit(solution)/shard_map/ppermute | solution.py:693
  29.2 4.0 %collective-permute-done.6.rest_7_.refs_8_ = f32[280,128]{1,0:T(8,128)S(1)} collective-permute-done((f32[280,128]{1,0:T(8,128)}, f32[280,128]{1,0:T(8,128)S(1)}, u32[]{:S(2)}, u32[]{:S(2)}) %collective-permute-start.6) | collective-permute-done | bytes 143392 | tf_op jit(solution)/shard_map/ppermute | solution.py:693
  33.3 0.6 collective-permute-start.7
  33.8 1.3 %collective-permute-start.8 = (f32[8,16,128]{2,1,0:T(8,128)S(1)}, f32[8,16,128]{2,1,0:T(8,128)S(1)}, u32[]{:S(2)}, u32[]{:S(2)}) collective-permute-start(f32[8,16,128]{2,1,0:T(8,128)S(1)} %collect_taps.1.rest_0_), channel_id=1, source_target_pairs={{0,2},{1,3},{2,0},{3,1},{4,6},{5,7},{6,4},{7,5},{8,10},{9,11},{10,... | collective-permute-start | bytes 196616 | tf_op jit(solution)/shard_map/ppermute | solution.py:693
  35.1 0.5 collective-permute-start.9
  35.5 2.0 %collective-permute-done.8.rest_2_ = f32[8,16,128]{2,1,0:T(8,128)S(1)} collective-permute-done((f32[8,16,128]{2,1,0:T(8,128)S(1)}, f32[8,16,128]{2,1,0:T(8,128)S(1)}, u32[]{:S(2)}, u32[]{:S(2)}) %collective-permute-start.8) | collective-permute-done | bytes 65568 | tf_op jit(solution)/shard_map/ppermute | solution.py:693
  37.5 1.9 %collective-permute-done.9.rest_3_ = f32[8,16,128]{2,1,0:T(8,128)S(1)} collective-permute-done((f32[8,16,128]{2,1,0:T(8,128)S(1)}, f32[8,16,128]{2,1,0:T(8,128)S(1)}, u32[]{:S(2)}, u32[]{:S(2)}) %collective-permute-start.9) | collective-permute-done | bytes 65568 | tf_op jit(solution)/shard_map/ppermute | solution.py:693
  39.4 2.0 %filter_spectra.1.spectra = f32[8,512,128]{2,1,0:T(8,128)S(1)} custom-call(s32[1]{0:T(128)} %bitcast.3.group_ref, f32[8,128]{1,0:T(8,128)S(1)} %copy-done.4, bf16[512,768]{1,0:T(8,128)(2,1)S(1)} %copy-done, f32[8,16,128]{2,1,0:T(8,128)S(1)} %collect_taps.1.rest_0_, f32[8,16,128]{2,1,0:T(8,128)S(1)} %collective-permute-done.7.rest_1_, ...), custom_call_target="tpu_custom_call" | custom-call | tf_op jit(solution)/shard_map/filter_spectra/pallas_call | solution.py:407
  41.4 0.0 copy-start.3
  41.4 4.6 %convolve.1 = (f32[256,128]{1,0:T(8,128)S(1)}, f32[256,128]{1,0:T(8,128)S(1)}, f32[256,128]{1,0:T(8,128)S(1)}, f32[256,128]{1,0:T(8,128)S(1)}, f32[256,128]{1,0:...) custom-call(s32[1]{0:T(128)} %bitcast.me_ref, f32[8,128]{1,0:T(8,128)S(1)} %copy-done.4, ...), custom_call_target="tpu_custom_call" | custom-call | tf_op jit(solution)/shard_map/convolve/pallas_call | solution.py:502
  46.0 10.2 %collective-permute-done.12.far = f32[1040,128]{1,0:T(8,128)S(1)} collective-permute-done((f32[1040,128]{1,0:T(8,128)}, f32[1040,128]{1,0:T(8,128)S(1)}, u32[]{:S(2)}, u32[]{:S(2)}) %collective-permute-start.12) | collective-permute-done | bytes 532512 | tf_op jit(solution)/shard_map/ppermute | solution.py:693
  56.2 0.1 deal.1
  56.3 0.7 collective-permute-start.13
  57.0 0.9 collective-permute-start.14
  57.9 1.1 %collective-permute-start.15 = (f32[800,128]{1,0:T(8,128)S(1)}, f32[800,128]{1,0:T(8,128)S(1)}, u32[]{:S(2)}, u32[]{:S(2)}) collective-permute-start(f32[800,128]{1,0:T(8,128)S(1)} %get-tuple-element.48), channel_id=1, source_target_pairs={{0,12},{4,8},{8,4},{12,0},{16,28},{20,24},{24,20},{28,16},{1,13},{... | collective-permute-start | bytes 1228808 | tf_op jit(solution)/shard_map/ppermute | solution.py:693
  59.0 3.0 %collective-permute-start.10 = (f32[256,128]{1,0:T(8,128)S(1)}, f32[256,128]{1,0:T(8,128)S(1)}, u32[]{:S(2)}, u32[]{:S(2)}) collective-permute-start(f32[256,128]{1,0:T(8,128)S(1)} %get-tuple-element.37), channel_id=1, source_target_pairs={{0,16},{4,20},{8,24},{12,28},{16,0},{20,4},{24,8},{28,12},{1,17},{... | collective-permute-start | bytes 393224 | tf_op jit(solution)/shard_map/ppermute | solution.py:693
  62.0 0.4 collective-permute-start.11
  62.4 18.0 %collective-permute-done.10.rest_0_ = f32[256,128]{1,0:T(8,128)S(1)} collective-permute-done((f32[256,128]{1,0:T(8,128)S(1)}, f32[256,128]{1,0:T(8,128)S(1)}, u32[]{:S(2)}, u32[]{:S(2)}) %collective-permute-start.10) | collective-permute-done | bytes 131104 | tf_op jit(solution)/shard_map/ppermute | solution.py:693
  80.4 3.7 %collective-permute-done.11.rest_1_ = f32[256,128]{1,0:T(8,128)S(1)} collective-permute-done((f32[256,128]{1,0:T(8,128)S(1)}, f32[256,128]{1,0:T(8,128)S(1)}, u32[]{:S(2)}, u32[]{:S(2)}) %collective-permute-start.11) | collective-permute-done | bytes 131104 | tf_op jit(solution)/shard_map/ppermute | solution.py:693
  84.0 8.7 %collective-permute-done.16.rest_6_ = f32[256,128]{1,0:T(8,128)S(1)} collective-permute-done((f32[256,128]{1,0:T(8,128)S(1)}, f32[256,128]{1,0:T(8,128)S(1)}, u32[]{:S(2)}, u32[]{:S(2)}) %collective-permute-start.16) | collective-permute-done | bytes 131104 | tf_op jit(solution)/shard_map/ppermute | solution.py:693
  92.7 3.4 %collective-permute-done.17.rest_7_ = f32[256,128]{1,0:T(8,128)S(1)} collective-permute-done((f32[256,128]{1,0:T(8,128)S(1)}, f32[256,128]{1,0:T(8,128)S(1)}, u32[]{:S(2)}, u32[]{:S(2)}) %collective-permute-start.17) | collective-permute-done | bytes 131104 | tf_op jit(solution)/shard_map/ppermute | solution.py:693
  96.1 3.0 %finish.1 = f32[32,8,1024]{2,1,0:T(8,128)} custom-call(s32[1]{0:T(128)} %bitcast.me_ref, f32[256,128]{1,0:T(8,128)S(1)} %collective-permute-done.10.rest_0_, f32[256,128]{1,0:T(8,128)S(1)} %collective-permute-done.11.rest_1_, f32[800,128]{1,0:T(8,128)S(1)} %get-tuple-element.45.rest_2_, f32[800,128]{1,0:T(8,128)S(1)} %collective-permute-done.13.rest_3_, ...), custom_call_target="tpu_custom_call" | custom-call | tf_op jit(solution)/shard_map/finish/pallas_call | solution.py:676
  (22 shorter events, 0.1 us)
Async XLA Ops:
  3.9 29.3 %copy-start.1 = (f32[280,128]{1,0:T(8,128)S(1)}, f32[280,128]{1,0:T(8,128)}, u32[]{:S(2)}) copy-start(f32[280,128]{1,0:T(8,128)} %get-tuple-element.31.rest_2_.refs_3_) | copy-start | bytes 430084
  3.9 8.3 %collective-permute-start = (f32[280,128]{1,0:T(8,128)}, f32[280,128]{1,0:T(8,128)S(1)}, u32[]{:S(2)}, u32[]{:S(2)}) collective-permute-start(f32[280,128]{1,0:T(8,128)} %get-tuple-element.29), channel_id=1, source_target_pairs={{0,16},{4,20},{8,24},{12,28},{16,0},{20,4},{24,8},{28,12},{1,17},{... | collective-permute-start | bytes 430088 | tf_op jit(solution)/shard_map/ppermute | solution.py:693
  4.0 12.3 %collective-permute-start.1 = (f32[280,128]{1,0:T(8,128)}, f32[280,128]{1,0:T(8,128)S(1)}, u32[]{:S(2)}, u32[]{:S(2)}) collective-permute-start(f32[280,128]{1,0:T(8,128)} %get-tuple-element.30), channel_id=1, source_target_pairs={{0,20},{4,16},{8,28},{12,24},{16,4},{20,0},{24,12},{28,8},{1,21},{... | collective-permute-start | bytes 430088 | tf_op jit(solution)/shard_map/ppermute | solution.py:693
  7.3 15.7 %collective-permute-start.2 = (f32[280,128]{1,0:T(8,128)}, f32[280,128]{1,0:T(8,128)S(1)}, u32[]{:S(2)}, u32[]{:S(2)}) collective-permute-start(f32[280,128]{1,0:T(8,128)} %get-tuple-element.32), channel_id=1, source_target_pairs={{0,4},{4,0},{8,12},{12,8},{16,20},{20,16},{24,28},{28,24},{1,5},{5... | collective-permute-start | bytes 430088 | tf_op jit(solution)/shard_map/ppermute | solution.py:693
  7.5 15.5 %collective-permute-start.3 = (f32[280,128]{1,0:T(8,128)}, f32[280,128]{1,0:T(8,128)S(1)}, u32[]{:S(2)}, u32[]{:S(2)}) collective-permute-start(f32[280,128]{1,0:T(8,128)} %get-tuple-element.33), channel_id=1, source_target_pairs={{0,8},{4,12},{8,0},{12,4},{16,24},{20,28},{24,16},{28,20},{1,9},{5... | collective-permute-start | bytes 430088 | tf_op jit(solution)/shard_map/ppermute | solution.py:693
  8.8 14.2 %collective-permute-start.4 = (f32[280,128]{1,0:T(8,128)}, f32[280,128]{1,0:T(8,128)S(1)}, u32[]{:S(2)}, u32[]{:S(2)}) collective-permute-start(f32[280,128]{1,0:T(8,128)} %get-tuple-element.34), channel_id=1, source_target_pairs={{0,12},{4,8},{8,4},{12,0},{16,28},{20,24},{24,20},{28,16},{1,13},{... | collective-permute-start | bytes 430088 | tf_op jit(solution)/shard_map/ppermute | solution.py:693
  12.2 17.0 %collective-permute-start.5 = (f32[280,128]{1,0:T(8,128)}, f32[280,128]{1,0:T(8,128)S(1)}, u32[]{:S(2)}, u32[]{:S(2)}) collective-permute-start(f32[280,128]{1,0:T(8,128)} %get-tuple-element.35), channel_id=1, source_target_pairs={{0,24},{4,28},{8,16},{12,20},{16,8},{20,12},{24,0},{28,4},{1,25},{... | collective-permute-start | bytes 430088 | tf_op jit(solution)/shard_map/ppermute | solution.py:693
  16.3 16.9 %collective-permute-start.6 = (f32[280,128]{1,0:T(8,128)}, f32[280,128]{1,0:T(8,128)S(1)}, u32[]{:S(2)}, u32[]{:S(2)}) collective-permute-start(f32[280,128]{1,0:T(8,128)} %get-tuple-element.36), channel_id=1, source_target_pairs={{0,28},{4,24},{8,20},{12,16},{16,12},{20,8},{24,4},{28,0},{1,29},{... | collective-permute-start | bytes 430088 | tf_op jit(solution)/shard_map/ppermute | solution.py:693
  20.3 19.1 %copy-start = (bf16[512,768]{1,0:T(8,128)(2,1)S(1)}, bf16[512,768]{1,0:T(8,128)(2,1)}, u32[]{:S(2)}) copy-start(bf16[512,768]{1,0:T(8,128)(2,1)} %constant.13.clone.forward) | copy-start | bytes 2359300
  20.3 19.1 %copy-start.4 = (f32[8,128]{1,0:T(8,128)S(1)}, f32[8,128]{1,0:T(8,128)}, u32[]{:S(2)}) copy-start(f32[8,128]{1,0:T(8,128)} %get-tuple-element.28.params._) | copy-start | bytes 12292
  33.2 8.2 %copy-start.2 = (bf16[256,1536]{1,0:T(8,128)(2,1)S(1)}, bf16[256,1536]{1,0:T(8,128)(2,1)}, u32[]{:S(2)}) copy-start(bf16[256,1536]{1,0:T(8,128)(2,1)} %constant.14.clone.inverse) | copy-start | bytes 2359300
  33.2 22.9 %collective-permute-start.12 = (f32[1040,128]{1,0:T(8,128)}, f32[1040,128]{1,0:T(8,128)S(1)}, u32[]{:S(2)}, u32[]{:S(2)}) collective-permute-start(f32[1040,128]{1,0:T(8,128)} %hold.1), channel_id=1, source_target_pairs={{0,16},{4,20},{8,24},{12,28},{16,0},{20,4},{24,8},{28,12},{1,17},{... | collective-permute-start | bytes 1597448 | tf_op jit(solution)/shard_map/ppermute | solution.py:693
  33.3 2.3 %collective-permute-start.7 = (f32[8,16,128]{2,1,0:T(8,128)S(1)}, f32[8,16,128]{2,1,0:T(8,128)S(1)}, u32[]{:S(2)}, u32[]{:S(2)}) collective-permute-start(f32[8,16,128]{2,1,0:T(8,128)S(1)} %collect_taps.1.rest_0_), channel_id=1, source_target_pairs={{0,1},{1,0},{2,3},{3,2},{4,5},{5,4},{6,7},{7,6},{8,9},{9,8},{10,11... | collective-permute-start | bytes 196616 | tf_op jit(solution)/shard_map/ppermute | solution.py:693
  33.8 3.7 %collective-permute-start.8 = (f32[8,16,128]{2,1,0:T(8,128)S(1)}, f32[8,16,128]{2,1,0:T(8,128)S(1)}, u32[]{:S(2)}, u32[]{:S(2)}) collective-permute-start(f32[8,16,128]{2,1,0:T(8,128)S(1)} %collect_taps.1.rest_0_), channel_id=1, source_target_pairs={{0,2},{1,3},{2,0},{3,1},{4,6},{5,7},{6,4},{7,5},{8,10},{9,11},{10,... | collective-permute-start | bytes 196616 | tf_op jit(solution)/shard_map/ppermute | solution.py:693
  35.1 4.3 %collective-permute-start.9 = (f32[8,16,128]{2,1,0:T(8,128)S(1)}, f32[8,16,128]{2,1,0:T(8,128)S(1)}, u32[]{:S(2)}, u32[]{:S(2)}) collective-permute-start(f32[8,16,128]{2,1,0:T(8,128)S(1)} %collect_taps.1.rest_0_), channel_id=1, source_target_pairs={{0,3},{1,2},{2,1},{3,0},{4,7},{5,6},{6,5},{7,4},{8,11},{9,10},{10,... | collective-permute-start | bytes 196616 | tf_op jit(solution)/shard_map/ppermute | solution.py:693
  41.4 14.8 %copy-start.3 = (f32[1040,128]{1,0:T(8,128)S(1)}, f32[1040,128]{1,0:T(8,128)}, u32[]{:S(2)}) copy-start(f32[1040,128]{1,0:T(8,128)} %get-tuple-element.39.near) | copy-start | bytes 1597444
  56.3 39.8 %collective-permute-start.13 = (f32[800,128]{1,0:T(8,128)S(1)}, f32[800,128]{1,0:T(8,128)S(1)}, u32[]{:S(2)}, u32[]{:S(2)}) collective-permute-start(f32[800,128]{1,0:T(8,128)S(1)} %get-tuple-element.46), channel_id=1, source_target_pairs={{0,4},{4,0},{8,12},{12,8},{16,20},{20,16},{24,28},{28,24},{1,5},{5... | collective-permute-start | bytes 1228808 | tf_op jit(solution)/shard_map/ppermute | solution.py:693
  57.0 39.1 %collective-permute-start.14 = (f32[800,128]{1,0:T(8,128)S(1)}, f32[800,128]{1,0:T(8,128)S(1)}, u32[]{:S(2)}, u32[]{:S(2)}) collective-permute-start(f32[800,128]{1,0:T(8,128)S(1)} %get-tuple-element.47), channel_id=1, source_target_pairs={{0,8},{4,12},{8,0},{12,4},{16,24},{20,28},{24,16},{28,20},{1,9},{5... | collective-permute-start | bytes 1228808 | tf_op jit(solution)/shard_map/ppermute | solution.py:693
  57.9 38.2 %collective-permute-start.15 = (f32[800,128]{1,0:T(8,128)S(1)}, f32[800,128]{1,0:T(8,128)S(1)}, u32[]{:S(2)}, u32[]{:S(2)}) collective-permute-start(f32[800,128]{1,0:T(8,128)S(1)} %get-tuple-element.48), channel_id=1, source_target_pairs={{0,12},{4,8},{8,4},{12,0},{16,28},{20,24},{24,20},{28,16},{1,13},{... | collective-permute-start | bytes 1228808 | tf_op jit(solution)/shard_map/ppermute | solution.py:693
  59.0 21.4 %collective-permute-start.10 = (f32[256,128]{1,0:T(8,128)S(1)}, f32[256,128]{1,0:T(8,128)S(1)}, u32[]{:S(2)}, u32[]{:S(2)}) collective-permute-start(f32[256,128]{1,0:T(8,128)S(1)} %get-tuple-element.37), channel_id=1, source_target_pairs={{0,16},{4,20},{8,24},{12,28},{16,0},{20,4},{24,8},{28,12},{1,17},{... | collective-permute-start | bytes 393224 | tf_op jit(solution)/shard_map/ppermute | solution.py:693
  62.0 22.0 %collective-permute-start.11 = (f32[256,128]{1,0:T(8,128)S(1)}, f32[256,128]{1,0:T(8,128)S(1)}, u32[]{:S(2)}, u32[]{:S(2)}) collective-permute-start(f32[256,128]{1,0:T(8,128)S(1)} %get-tuple-element.38), channel_id=1, source_target_pairs={{0,20},{4,16},{8,28},{12,24},{16,4},{20,0},{24,12},{28,8},{1,21},{... | collective-permute-start | bytes 393224 | tf_op jit(solution)/shard_map/ppermute | solution.py:693
  80.4 12.4 %collective-permute-start.16 = (f32[256,128]{1,0:T(8,128)S(1)}, f32[256,128]{1,0:T(8,128)S(1)}, u32[]{:S(2)}, u32[]{:S(2)}) collective-permute-start(f32[256,128]{1,0:T(8,128)S(1)} %get-tuple-element.49), channel_id=1, source_target_pairs={{0,24},{4,28},{8,16},{12,20},{16,8},{20,12},{24,0},{28,4},{1,25},{... | collective-permute-start | bytes 393224 | tf_op jit(solution)/shard_map/ppermute | solution.py:693
  84.0 12.0 %collective-permute-start.17 = (f32[256,128]{1,0:T(8,128)S(1)}, f32[256,128]{1,0:T(8,128)S(1)}, u32[]{:S(2)}, u32[]{:S(2)}) collective-permute-start(f32[256,128]{1,0:T(8,128)S(1)} %get-tuple-element.50), channel_id=1, source_target_pairs={{0,28},{4,24},{8,20},{12,16},{16,12},{20,8},{24,4},{28,0},{1,29},{... | collective-permute-start | bytes 393224 | tf_op jit(solution)/shard_map/ppermute | solution.py:693
where the time goes:
time: 99.2 us; the launch traced here: 99.1 us
  waiting for transfers between devices  60.3 us (61%)
  starting transfers between devices  22.4 us (23%)
  Pallas kernels  16.2 us (16%)
    ppermute x18, waiting for transfers between devices, swapped(): lax.ppermute(block, axis, [(i, i ^ k) for i in range(lax.axis_size(axis))])  60.3 us
    ppermute x18, starting transfers between devices, swapped(): lax.ppermute(block, axis, [(i, i ^ k) for i in range(lax.axis_size(axis))])  22.4 us
    pallas_call x1, Pallas kernels, convolve(): pl.pallas_call(functools.partial(convolve_kernel, count, length), out_sha...  4.58 us
    pallas_call x1, Pallas kernels, gate(): pl.pallas_call(functools.partial(gate_kernel, count, width, pieces), out_...  3.88 us
    pallas_call x1, Pallas kernels, finish(): pl.pallas_call(functools.partial(finish_kernel, count, width, pieces), ou...  2.99 us
    pallas_call x1, Pallas kernels, query(): pl.pallas_call(functools.partial(query_kernel, count // 2), out_shape=[ro...  2.67 us
  transfers between devices with their start and end apart: 18, of which 10 were waited for; matrix products, arithmetic and copies ran while one was open for 0% of the time, Pallas kernels for 9%

commit v1 on v0

--- a/solution.py
+++ b/solution.py
@@ -11,7 +11,7 @@
 
 LANES = 128
 ROWS = 8
-VMEM_BYTES = 40 * 1024 * 1024
+VMEM_BYTES = 20 * 1024 * 1024
 
 
 def passed_along(block, axis, distance):
@@ -348,10 +348,9 @@
 def collect_kernel(count, width, me_ref, *rest):
     messages, out = by_partner(rest[:count]), rest[count]
     me = me_ref[0]
-    size = out.shape[1]
+    rows = messages[0].shape[0]
     for k in range(count):
-        rows = messages[k].shape[0]
-        out[me ^ k] = messages[k][rows - size : rows, :]
+        out[me ^ k] = messages[k][rows - out.shape[1] : rows, :]
 
 
 def collect_taps(me, messages, count, width, length):
@@ -515,56 +514,54 @@
     )(me, params, forward, inverse, spectra, *far_first_operands(messages))
 
 
-def query_kernel(half, me_ref, streams, taps_in, _, near, far, rows, taps, sems):
+def query_kernel(count, me_ref, streams, taps_in, _, *rest):
+    evens, (odds, rows, taps, sems) = rest[: count // 2], rest[count // 2 :]
     length, channels = streams.shape[1:]
     tiles = channels // LANES
+    part = length // count
+    size = tiles * (part + 2)
+    me = me_ref[0]
     load = pltpu.make_async_copy(streams.at[0], rows.at[pl.ds(ROWS, length)], sems.at[0])
     fetch = pltpu.make_async_copy(taps_in, taps, sems.at[1])
     load.start()
     fetch.start()
     rows[0:ROWS, :] = jnp.zeros((ROWS, channels), jnp.float32)
-    side = me_ref[0] // half
     fetch.wait()
     load.wait()
-    step = length // (2 * half)
-    for out, at in ((far, 1 - side), (near, side)):
-
-        def block(i, _):
-            base = pl.multiple_of(at * (length // 2) + i * step, step)
-            for t in range(tiles):
-                now = rows[pl.ds(pl.multiple_of(base + ROWS, ROWS), step), tile_of(t)]
-                before = rows[aligned(base, step), tile_of(t)]
-                target = pl.multiple_of((i * tiles + t) * step, step)
-                out[pl.ds(target, step), :] = short_filtered(taps, 0, tile_of(t), now, before)
-            return 0
-
-        lax.fori_loop(0, half, block, 0)
     last = rows[length + ROWS - 1 : length + ROWS, :]
     last_but_one = rows[length + ROWS - 2 : length + ROWS - 1, :]
     first = taps[0, 1:2, :] * last + taps[0, 2:3, :] * last_but_one
     second = taps[0, 2:3, :] * last
-    end = tiles * (length // 2)
-    for t in range(tiles):
-        both = jnp.concatenate([first[:, tile_of(t)], second[:, tile_of(t)]], axis=0)
-        for out in (near, far):
-            out[end + 2 * t : end + 2 * t + 2, :] = both
+    for k in range(count):
+        out, ahead = (odds, k // 2 * size) if k % 2 else (evens[k // 2], 0)
+        base = pl.multiple_of((me ^ k) * part, part)
+        for t in range(tiles):
+            now = rows[pl.ds(pl.multiple_of(base + ROWS, ROWS), part), tile_of(t)]
+            before = rows[aligned(base, part), tile_of(t)]
+            out[ahead + t * part : ahead + (t + 1) * part, :] = short_filtered(
+                taps, 0, tile_of(t), now, before
+            )
+            at = ahead + tiles * part + 2 * t
+            out[at : at + 2, :] = jnp.concatenate(
+                [first[:, tile_of(t)], second[:, tile_of(t)]], axis=0
+            )
 
 
 def query(me, streams, short_filters, params, count):
     length, channels = streams.shape[1:]
-    tiles = channels // LANES
-    rows = jax.ShapeDtypeStruct((tiles * (length // 2 + 2), LANES), jnp.float32)
+    size = channels // LANES * (length // count + 2)
+    sizes = [size] * (count // 2) + [count // 2 * size]
     return pl.pallas_call(
-        functools.partial(query_kernel, count // 2),
-        out_shape=[rows, rows],
+        functools.partial(query_kernel, count),
+        out_shape=[jax.ShapeDtypeStruct((rows, LANES), jnp.float32) for rows in sizes],
         in_specs=[in_smem(), in_any(), in_any(), in_any()],
-        out_specs=[in_vmem()] * 2,
+        out_specs=[in_vmem()] * len(sizes),
         scratch_shapes=[
             pltpu.VMEM((length + ROWS, channels), jnp.float32),
             pltpu.VMEM(short_filters.shape, jnp.float32),
             pltpu.SemaphoreType.DMA((2,)),
         ],
-        compiler_params=params_of(60 * 1024 * 1024),
+        compiler_params=params_of(),
         name="query",
     )(me, streams, short_filters, params)
 
@@ -573,62 +570,50 @@
     del refs
 
 
-def hold(value, *others):
+def hold(values, *others):
     return pl.pallas_call(
         hold_kernel,
-        out_shape=jax.ShapeDtypeStruct(value.shape, value.dtype),
-        in_specs=[in_any()] * (1 + len(others)),
-        out_specs=in_any(),
-        input_output_aliases={0: 0},
+        out_shape=[jax.ShapeDtypeStruct(value.shape, value.dtype) for value in values],
+        in_specs=[in_any()] * (len(values) + len(others)),
+        out_specs=[in_any()] * len(values),
+        input_output_aliases={i: i for i in range(len(values))},
         compiler_params=params_of(),
         name="hold",
-    )(value, *others)
-
-
-def deal_kernel(half, tiles, me_ref, near, far, *rest):
-    results, outs = rest[:half], rest[half:]
-    share = (near.shape[0] - 2 * tiles) // half
-    place = me_ref[0] % half
-    for k in range(half):
-        start = pl.multiple_of((place ^ k) * share, share)
-        outs[k][0:share, :] = near[pl.ds(start, share), :]
-        outs[k][share : 2 * share, :] = far[pl.ds(start, share), :]
-        at = 2 * share
-        for source in (near, far):
-            outs[k][at : at + 2 * tiles, :] = source[half * share : half * share + 2 * tiles, :]
-            at += 2 * tiles
-        outs[k][at : at + results[k].shape[0], :] = results[k][...]
-
-
-def deal(me, near, far, results, tiles, count):
-    half = count // 2
-    size = 2 * (near.shape[0] - 2 * tiles) // half + 4 * tiles + results[0].shape[0]
+    )(*values, *others)
+
+
+def pair_shares_kernel(pairs, *refs):
+    evens, odds, outs = refs[:pairs], refs[pairs], refs[-pairs:]
+    size = evens[0].shape[0]
+    for i in range(pairs):
+        outs[i][0:size, :] = evens[i][...]
+        outs[i][size : 2 * size, :] = odds[(i + 1) * size : (i + 2) * size, :]
+
+
+def pair_shares(evens, odds, *earlier):
+    shape = jax.ShapeDtypeStruct((2 * evens[0].shape[0], LANES), jnp.float32)
     return pl.pallas_call(
-        functools.partial(deal_kernel, half, tiles),
-        out_shape=[jax.ShapeDtypeStruct((size, LANES), jnp.float32)] * half,
-        in_specs=[in_smem()] + [in_vmem()] * (2 + half),
-        out_specs=[in_vmem()] * half,
+        functools.partial(pair_shares_kernel, len(evens)),
+        out_shape=[shape] * len(evens),
+        in_specs=[in_vmem()] * (len(evens) + 1) + [in_any()] * len(earlier),
+        out_specs=[in_vmem()] * len(evens),
         compiler_params=params_of(),
-        name="deal",
-    )(me, near, far, *results[:half])
-
-
-def arrange_query(count, me, dealt, out, lacking):
-    half = count // 2
+        name="pair_shares",
+    )(*evens, odds, *earlier)
+
+
+def arrange_query(count, me, shares, out, lacking):
     tiles, rows = out.shape[:2]
     part = rows // count
     lacking[...] = jnp.zeros(lacking.shape, jnp.float32)
-    for k in range(half):
-        for i in range(2):
-            r = me ^ k ^ (i * half)
-            for t in range(tiles):
-                for m in range(0, part, ROWS):
-                    at = (i * tiles + t) * part + m
-                    out[t, pl.ds(m * count + r, ROWS, stride=count), :] = dealt[k][
-                        at : at + ROWS, :
-                    ]
-                at = 2 * tiles * part + (i * tiles + t) * 2
-                lacking[t, pl.ds(r + 1, 2, stride=2 * count), :] = dealt[k][at : at + 2, :]
+    for k in range(count):
+        r = me ^ k
+        for t in range(tiles):
+            for m in range(0, part, ROWS):
+                at = t * part + m
+                out[t, pl.ds(m * count + r, ROWS, stride=count), :] = shares[k][at : at + ROWS, :]
+            at = tiles * part + t * 2
+            lacking[t, pl.ds(r + 1, 2, stride=2 * count), :] = shares[k][at : at + 2, :]
     first = (me == 0).astype(jnp.float32)
     for t in range(tiles):
         for m in range(2):
@@ -637,20 +622,23 @@
 
 
 def finish_kernel(count, width, pieces, me_ref, *rest):
-    messages, (out, rows, query_rows, lacking, sems) = by_partner(rest[:count]), rest[count:]
+    messages, rest = by_partner(rest[:count]), rest[count:]
+    half = count // 2
+    own, odds, *pairs = rest[: half + 1]
+    out, rows, query_rows, lacking, sems = rest[half + 1 :]
     me = me_ref[0]
     part = out.shape[0]
-    arrange_query(count, me, messages[: count // 2], query_rows, lacking)
+    size = own.shape[0]
+    shares = [own, odds.at[pl.ds(0, size)]]
+    for pair in pairs:
+        shares += [pair.at[pl.ds(0, size)], pair.at[pl.ds(size, size)]]
+    arrange_query(count, me, shares, query_rows, lacking)
     step = 4
     stores = []
 
     def block(i, _):
         at = aligned(i * step * count, step * count)
-        tiles = []
-        for message in messages:
-            ahead = message.shape[0] - part * count
-            start = pl.multiple_of(ahead + i * step * count, step * count)
-            tiles.append(message[pl.ds(start, step * count), :])
+        tiles = [message[at, :] for message in messages]
         tiles = swap_tiles_and_slots(tiles, width, me, False)
         for t in range(count):
             product = query_rows[t, at, :] * tiles[t]
@@ -669,14 +657,13 @@
         store.wait()
 
 
-def finish(me, messages, tiles, count, width):
-    rows = messages[-1].shape[0]
+def finish(me, messages, shares, rows, tiles, count, width):
     part = rows // count
     pieces = 4
     return pl.pallas_call(
         functools.partial(finish_kernel, count, width, pieces),
         out_shape=jax.ShapeDtypeStruct((part, count, tiles * LANES), jnp.float32),
-        in_specs=[in_smem()] + [in_vmem()] * count,
+        in_specs=[in_smem()] + [in_vmem()] * (count + len(shares)),
         out_specs=in_any(),
         scratch_shapes=[
             pltpu.VMEM((part, count, tiles * LANES), jnp.float32),
@@ -686,7 +673,7 @@
         ],
         compiler_params=params_of(),
         name="finish",
-    )(me, *far_first_operands(messages))
+    )(me, *far_first_operands(messages), *shares)
 
 
 def swapped(block, axis, k):
@@ -710,19 +697,25 @@
     width = long_filter.shape[1] // count
     forward, inverse = (jnp.asarray(table) for table in transform_tables(length))
     *gated, params = gate(me, streams, short_filters, skip_gain, long_filter, count, width)
-    gated = exchanged(gated, "seq")
     half = count // 2
     tiles = streams.shape[2] // LANES
-    near, far = query(me, streams, short_filters, params, count)
-    far = hold(far, *far_first_operands(gated))
+    *evens, odds = query(me, streams, short_filters, params, count)
+    odds = swapped(odds, "seq", 1)
+    gated = exchanged(gated, "seq")
+    pairs = pair_shares(evens[1:], odds, *gated[half:half + 2])
     taps = collect_taps(me, gated, count, width, length)
     taps = [taps] + [swapped(taps, "grp", k) for k in range(1, groups)]
-    far = swapped(far, "seq", half)
+    pairs = [swapped(pair, "seq", 2 * i) for i, pair in enumerate(pairs, 1)]
     spectra = filter_spectra(group, params, forward, taps, count, width)
-    convolved = convolve(me, params, forward, inverse, spectra, gated, count)
-    dealt = exchanged(deal(me, near, far, convolved, tiles, count), "seq")
-    convolved = dealt + [swapped(convolved[k], "seq", k) for k in range(half, count)]
-    return finish(me, convolved, tiles, count, width)
+    convolved = list(convolve(me, params, forward, inverse, spectra, gated, count))
+    convolved[1:half] = hold(convolved[1:half], *pairs)
+    first = [swapped(convolved[k], "seq", k) for k in (half, half + 1)]
+    convolved[half + 2 :] = hold(convolved[half + 2 :], *pairs, first[0])
+    convolved = exchanged(convolved[:half], "seq") + first + [
+        swapped(convolved[k], "seq", k) for k in range(half + 2, count)
+    ]
+    shares = [evens[0], odds, *pairs]
+    return finish(me, convolved, shares, length, tiles, count, width)
 
 
 def body(streams, short_filters, skip_gain, long_filter):

time: 99.2 us -> 88.4 us (0.89)
  the two profiles are of different devices: /device:TPU:17 before, /device:TPU:0 now
where the time goes in v1:
time: 88.4 us; the launch traced here: 88.2 us
  starting transfers between devices  44.5 us (50%)
  waiting for transfers between devices  22.7 us (26%)
  Pallas kernels  16.7 us (19%)
  local copies, waits for them, and re-layouts  4.04 us (5%)
    ppermute x21, starting transfers between devices, swapped(): lax.ppermute(block, axis, [(i, i ^ k) for i in range(lax.axis_size(axis))])  44.5 us
    ppermute x21, waiting for transfers between devices, swapped(): lax.ppermute(block, axis, [(i, i ^ k) for i in range(lax.axis_size(axis))])  22.7 us
    pallas_call x1, Pallas kernels, convolve(): pl.pallas_call(functools.partial(convolve_kernel, count, length), out_sha...  4.58 us
    unnamed x54, local copies, waits for them, and re-layouts  4.04 us
    pallas_call x1, Pallas kernels, gate(): pl.pallas_call(functools.partial(gate_kernel, count, width, pieces), out_...  4.02 us
    pallas_call x1, Pallas kernels, finish(): pl.pallas_call(functools.partial(finish_kernel, count, width, pieces), ou...  3 us
    pallas_call x1, Pallas kernels, filter_spectra(): pl.pallas_call(functools.partial(filter_kernel, count, width), out_shape=...  2.94 us
  transfers between devices with their start and end apart: 21, of which 8 were waited for; matrix products, arithmetic and copies ran while one was open for 0% of the time, Pallas kernels for 10%

profile of v1, /device:TPU:0, one launch (start us, length us, event | category | flops | bytes accessed | tf_op | source)
XLA Modules:
  0.0 88.2 jit_solution(11045839961836525193)
XLA Ops:
  0.0 4.0 %gate.1 = (f32[280,128]{1,0:T(8,128)}, f32[280,128]{1,0:T(8,128)}, f32[280,128]{1,0:T(8,128)}, f32[280,128]{1,0:T(8,128)}, f32[280,128]{1,0:T(8,128)}, /*index=5...) custom-call(s32[1]{0:T(128)} %bitcast.me_ref, f32[3,256,1024]{2,1,0:T(8,128)} %streams.3, ...), custom_call_target="tpu_custom_call" | custom-call | tf_op jit(solution)/shard_map/gate/pallas_call | solution.py:330
  4.1 0.7 copy-done.18
  5.4 3.0 %collective-permute-start.12 = (f32[1088,128]{1,0:T(8,128)S(1)}, f32[1088,128]{1,0:T(8,128)S(1)}, u32[]{:S(2)}, u32[]{:S(2)}) collective-permute-start(f32[1088,128]{1,0:T(8,128)S(1)} %get-tuple-element.53), channel_id=1, source_target_pairs={{0,4},{4,0},{8,12},{12,8},{16,20},{20,16},{24,28},{28,24},{1,5},{5... | collective-permute-start | bytes 1671176 | tf_op jit(solution)/shard_map/ppermute | solution.py:680
  8.4 2.6 %collective-permute-start = (f32[280,128]{1,0:T(8,128)S(1)}, f32[280,128]{1,0:T(8,128)S(1)}, u32[]{:S(2)}, u32[]{:S(2)}) collective-permute-start(f32[280,128]{1,0:T(8,128)S(1)} %copy-done.26), channel_id=1, source_target_pairs={{0,16},{4,20},{8,24},{12,28},{16,0},{20,4},{24,8},{28,12},{1,17},{... | collective-permute-start | bytes 430088 | tf_op jit(solution)/shard_map/ppermute | solution.py:680
  11.0 1.8 %collective-permute-start.2 = (f32[280,128]{1,0:T(8,128)S(1)}, f32[280,128]{1,0:T(8,128)S(1)}, u32[]{:S(2)}, u32[]{:S(2)}) collective-permute-start(f32[280,128]{1,0:T(8,128)S(1)} %copy-done.24), channel_id=1, source_target_pairs={{0,4},{4,0},{8,12},{12,8},{16,20},{20,16},{24,28},{28,24},{1,5},{5... | collective-permute-start | bytes 430088 | tf_op jit(solution)/shard_map/ppermute | solution.py:680
  12.8 1.6 %collective-permute-start.3 = (f32[280,128]{1,0:T(8,128)S(1)}, f32[280,128]{1,0:T(8,128)S(1)}, u32[]{:S(2)}, u32[]{:S(2)}) collective-permute-start(f32[280,128]{1,0:T(8,128)S(1)} %copy-done.23), channel_id=1, source_target_pairs={{0,8},{4,12},{8,0},{12,4},{16,24},{20,28},{24,16},{28,20},{1,9},{5... | collective-permute-start | bytes 430088 | tf_op jit(solution)/shard_map/ppermute | solution.py:680
  14.3 7.5 %collective-permute-done.rest_0_.refs_4_ = f32[280,128]{1,0:T(8,128)S(1)} collective-permute-done((f32[280,128]{1,0:T(8,128)S(1)}, f32[280,128]{1,0:T(8,128)S(1)}, u32[]{:S(2)}, u32[]{:S(2)}) %collective-permute-start) | collective-permute-done | bytes 143392 | tf_op jit(solution)/shard_map/ppermute | solution.py:680
  21.8 2.0 %collective-permute-done.1.rest_1_.refs_5_ = f32[280,128]{1,0:T(8,128)S(1)} collective-permute-done((f32[280,128]{1,0:T(8,128)S(1)}, f32[280,128]{1,0:T(8,128)S(1)}, u32[]{:S(2)}, u32[]{:S(2)}) %collective-permute-start.1) | collective-permute-done | bytes 143392 | tf_op jit(solution)/shard_map/ppermute | solution.py:680
  23.8 3.6 %collective-permute-start.5 = (f32[280,128]{1,0:T(8,128)S(1)}, f32[280,128]{1,0:T(8,128)S(1)}, u32[]{:S(2)}, u32[]{:S(2)}) collective-permute-start(f32[280,128]{1,0:T(8,128)S(1)} %copy-done.21), channel_id=1, source_target_pairs={{0,24},{4,28},{8,16},{12,20},{16,8},{20,12},{24,0},{28,4},{1,25},{... | collective-permute-start | bytes 430088 | tf_op jit(solution)/shard_map/ppermute | solution.py:680
  28.0 5.1 %collective-permute-start.6 = (f32[280,128]{1,0:T(8,128)S(1)}, f32[280,128]{1,0:T(8,128)S(1)}, u32[]{:S(2)}, u32[]{:S(2)}) collective-permute-start(f32[280,128]{1,0:T(8,128)S(1)} %copy-done.20), channel_id=1, source_target_pairs={{0,28},{4,24},{8,20},{12,16},{16,12},{20,8},{24,4},{28,0},{1,29},{... | collective-permute-start | bytes 430088 | tf_op jit(solution)/shard_map/ppermute | solution.py:680
  33.1 0.9 %pair_shares.1 = (f32[544,128]{1,0:T(8,128)}, f32[544,128]{1,0:T(8,128)}, f32[544,128]{1,0:T(8,128)}) custom-call(f32[272,128]{1,0:T(8,128)S(1)} %get-tuple-element.50.refs_0_, f32[272,128]{1,0:T(8,128)S(1)} %get-tuple-element.51.refs_1_, f32[272,128]{1,0:T(8,128)S(1)} %get-tuple-element.52.refs_2_, f32[1088,128]{1,0:T(8,128)S(1)} %collective-permute-done.12.refs_3_.rest_9_, ...), custom_call_target="tpu_custom_call" | custom-call | tf_op jit(solution)/shard_map/pair_shares/pallas_call | solution.py:595
  34.0 0.8 collective-permute-start.14
  34.8 3.6 %collective-permute-start.15 = (f32[544,128]{1,0:T(8,128)}, f32[544,128]{1,0:T(8,128)S(1)}, u32[]{:S(2)}, u32[]{:S(2)}) collective-permute-start(f32[544,128]{1,0:T(8,128)} %get-tuple-element.56), channel_id=1, source_target_pairs={{0,24},{4,28},{8,16},{12,20},{16,8},{20,12},{24,0},{28,4},{1,25},{... | collective-permute-start | bytes 835592 | tf_op jit(solution)/shard_map/ppermute | solution.py:680
  38.4 0.7 collect_taps.1.rest_0_
  39.8 1.5 %collective-permute-start.8 = (f32[8,16,128]{2,1,0:T(8,128)}, f32[8,16,128]{2,1,0:T(8,128)}, u32[]{:S(2)}, u32[]{:S(2)}) collective-permute-start(f32[8,16,128]{2,1,0:T(8,128)} %collect_taps.1.rest_0_), channel_id=1, source_target_pairs={{0,2},{1,3},{2,0},{3,1},{4,6},{5,7},{6,4},{7,5},{8,10},{9,11},{10,... | collective-permute-start | bytes 196616 | tf_op jit(solution)/shard_map/ppermute | solution.py:680
  42.0 1.2 %collective-permute-start.9 = (f32[8,16,128]{2,1,0:T(8,128)}, f32[8,16,128]{2,1,0:T(8,128)}, u32[]{:S(2)}, u32[]{:S(2)}) collective-permute-start(f32[8,16,128]{2,1,0:T(8,128)} %collect_taps.1.rest_0_), channel_id=1, source_target_pairs={{0,3},{1,2},{2,1},{3,0},{4,7},{5,6},{6,5},{7,4},{8,11},{9,10},{10,... | collective-permute-start | bytes 196616 | tf_op jit(solution)/shard_map/ppermute | solution.py:680
  43.2 1.5 %collective-permute-done.8.rest_2_ = f32[8,16,128]{2,1,0:T(8,128)} collective-permute-done((f32[8,16,128]{2,1,0:T(8,128)}, f32[8,16,128]{2,1,0:T(8,128)}, u32[]{:S(2)}, u32[]{:S(2)}) %collective-permute-start.8) | collective-permute-done | bytes 65568 | tf_op jit(solution)/shard_map/ppermute | solution.py:680
  44.6 1.7 %collective-permute-done.9.rest_3_ = f32[8,16,128]{2,1,0:T(8,128)} collective-permute-done((f32[8,16,128]{2,1,0:T(8,128)}, f32[8,16,128]{2,1,0:T(8,128)}, u32[]{:S(2)}, u32[]{:S(2)}) %collective-permute-start.9) | collective-permute-done | bytes 65568 | tf_op jit(solution)/shard_map/ppermute | solution.py:680
  46.4 1.1 %copy-done.1 = bf16[512,768]{1,0:T(8,128)(2,1)S(1)} copy-done((bf16[512,768]{1,0:T(8,128)(2,1)S(1)}, bf16[512,768]{1,0:T(8,128)(2,1)}, u32[]{:S(2)}) %copy-start.1) | copy-done | bytes 786456
  47.5 0.8 copy-done.17
  48.3 2.9 %filter_spectra.1.spectra = f32[8,512,128]{2,1,0:T(8,128)S(1)} custom-call(s32[1]{0:T(128)} %bitcast.3.group_ref, f32[8,128]{1,0:T(8,128)S(1)} %copy-done.19, bf16[512,768]{1,0:T(8,128)(2,1)S(1)} %copy-done.1, f32[8,16,128]{2,1,0:T(8,128)} %collect_taps.1.rest_0_, f32[8,16,128]{2,1,0:T(8,128)S(1)} %copy-done.17, ...), custom_call_target="tpu_custom_call" | custom-call | tf_op jit(solution)/shard_map/filter_spectra/pallas_call | solution.py:406
  51.4 4.6 %convolve.1 = (f32[256,128]{1,0:T(8,128)S(1)}, f32[256,128]{1,0:T(8,128)S(1)}, f32[256,128]{1,0:T(8,128)S(1)}, f32[256,128]{1,0:T(8,128)S(1)}, f32[256,128]{1,0:...) custom-call(s32[1]{0:T(128)} %bitcast.me_ref, f32[8,128]{1,0:T(8,128)S(1)} %copy-done.19, ...), custom_call_target="tpu_custom_call" | custom-call | tf_op jit(solution)/shard_map/convolve/pallas_call | solution.py:501
  55.9 2.6 %collective-permute-start.10 = (f32[256,128]{1,0:T(8,128)S(1)}, f32[256,128]{1,0:T(8,128)S(1)}, u32[]{:S(2)}, u32[]{:S(2)}) collective-permute-start(f32[256,128]{1,0:T(8,128)S(1)} %get-tuple-element.44), channel_id=1, source_target_pairs={{0,16},{4,20},{8,24},{12,28},{16,0},{20,4},{24,8},{28,12},{1,17},{... | collective-permute-start | bytes 393224 | tf_op jit(solution)/shard_map/ppermute | solution.py:680
  58.6 1.1 %collective-permute-start.11 = (f32[256,128]{1,0:T(8,128)S(1)}, f32[256,128]{1,0:T(8,128)S(1)}, u32[]{:S(2)}, u32[]{:S(2)}) collective-permute-start(f32[256,128]{1,0:T(8,128)S(1)} %get-tuple-element.45), channel_id=1, source_target_pairs={{0,20},{4,16},{8,28},{12,24},{16,4},{20,0},{24,12},{28,8},{1,21},{... | collective-permute-start | bytes 393224 | tf_op jit(solution)/shard_map/ppermute | solution.py:680
  59.7 0.8 collective-permute-start.16
  60.5 9.3 %collective-permute-start.17 = (f32[256,128]{1,0:T(8,128)S(1)}, f32[256,128]{1,0:T(8,128)S(1)}, u32[]{:S(2)}, u32[]{:S(2)}) collective-permute-start(f32[256,128]{1,0:T(8,128)S(1)} %get-tuple-element.58), channel_id=1, source_target_pairs={{0,8},{4,12},{8,0},{12,4},{16,24},{20,28},{24,16},{28,20},{1,9},{5... | collective-permute-start | bytes 393224 | tf_op jit(solution)/shard_map/ppermute | solution.py:680
  69.8 1.5 %collective-permute-start.18 = (f32[256,128]{1,0:T(8,128)S(1)}, f32[256,128]{1,0:T(8,128)S(1)}, u32[]{:S(2)}, u32[]{:S(2)}) collective-permute-start(f32[256,128]{1,0:T(8,128)S(1)} %get-tuple-element.59), channel_id=1, source_target_pairs={{0,12},{4,8},{8,4},{12,0},{16,28},{20,24},{24,20},{28,16},{1,13},{... | collective-permute-start | bytes 393224 | tf_op jit(solution)/shard_map/ppermute | solution.py:680
  71.3 0.9 collective-permute-done.10.refs_5_.rest_0_
  72.1 1.3 %collective-permute-start.19 = (f32[256,128]{1,0:T(8,128)S(1)}, f32[256,128]{1,0:T(8,128)S(1)}, u32[]{:S(2)}, u32[]{:S(2)}) collective-permute-start(f32[256,128]{1,0:T(8,128)S(1)} %get-tuple-element.62), channel_id=1, source_target_pairs={{0,24},{4,28},{8,16},{12,20},{16,8},{20,12},{24,0},{28,4},{1,25},{... | collective-permute-start | bytes 393224 | tf_op jit(solution)/shard_map/ppermute | solution.py:680
  74.1 3.1 %collective-permute-start.20 = (f32[256,128]{1,0:T(8,128)S(1)}, f32[256,128]{1,0:T(8,128)S(1)}, u32[]{:S(2)}, u32[]{:S(2)}) collective-permute-start(f32[256,128]{1,0:T(8,128)S(1)} %get-tuple-element.63), channel_id=1, source_target_pairs={{0,28},{4,24},{8,20},{12,16},{16,12},{20,8},{24,4},{28,0},{1,29},{... | collective-permute-start | bytes 393224 | tf_op jit(solution)/shard_map/ppermute | solution.py:680
  77.2 8.0 %collective-permute-done.18.rest_5_ = f32[256,128]{1,0:T(8,128)S(1)} collective-permute-done((f32[256,128]{1,0:T(8,128)S(1)}, f32[256,128]{1,0:T(8,128)S(1)}, u32[]{:S(2)}, u32[]{:S(2)}) %collective-permute-start.18) | collective-permute-done | bytes 131104 | tf_op jit(solution)/shard_map/ppermute | solution.py:680
  85.2 3.0 %finish.1 = f32[32,8,1024]{2,1,0:T(8,128)} custom-call(s32[1]{0:T(128)} %bitcast.me_ref, f32[256,128]{1,0:T(8,128)S(1)} %collective-permute-done.10.refs_5_.rest_0_, f32[256,128]{1,0:T(8,128)S(1)} %collective-permute-done.11.rest_1_, f32[256,128]{1,0:T(8,128)S(1)} %get-tuple-element.46.rest_2_, f32[256,128]{1,0:T(8,128)S(1)} %collective-permute-done.16.rest_3_, ...), custom_call_target="tpu_custom_call" | custom-call | tf_op jit(solution)/shard_map/finish/pallas_call | solution.py:663
  (73 shorter events, 3.1 us)
Async XLA Ops:
  4.0 34.4 %copy-start.4 = (f32[280,128]{1,0:T(8,128)S(1)}, f32[280,128]{1,0:T(8,128)}, u32[]{:S(2)}) copy-start(f32[280,128]{1,0:T(8,128)} %get-tuple-element.38.rest_2_) | copy-start | bytes 430084
  4.8 6.2 %copy-start.24 = (f32[280,128]{1,0:T(8,128)S(1)}, f32[280,128]{1,0:T(8,128)}, u32[]{:S(2)}) copy-start(f32[280,128]{1,0:T(8,128)} %get-tuple-element.39) | copy-start | bytes 430084
  4.8 8.0 %copy-start.23 = (f32[280,128]{1,0:T(8,128)S(1)}, f32[280,128]{1,0:T(8,128)}, u32[]{:S(2)}) copy-start(f32[280,128]{1,0:T(8,128)} %get-tuple-element.40) | copy-start | bytes 430084
  4.8 17.0 %copy-start.22 = (f32[280,128]{1,0:T(8,128)S(1)}, f32[280,128]{1,0:T(8,128)}, u32[]{:S(2)}) copy-start(f32[280,128]{1,0:T(8,128)} %get-tuple-element.41) | copy-start | bytes 430084
  4.8 19.0 %copy-start.21 = (f32[280,128]{1,0:T(8,128)S(1)}, f32[280,128]{1,0:T(8,128)}, u32[]{:S(2)}) copy-start(f32[280,128]{1,0:T(8,128)} %get-tuple-element.42) | copy-start | bytes 430084
  4.8 23.1 %copy-start.20 = (f32[280,128]{1,0:T(8,128)S(1)}, f32[280,128]{1,0:T(8,128)}, u32[]{:S(2)}) copy-start(f32[280,128]{1,0:T(8,128)} %get-tuple-element.43) | copy-start | bytes 430084
  4.8 41.5 %copy-start.19 = (f32[8,128]{1,0:T(8,128)S(1)}, f32[8,128]{1,0:T(8,128)}, u32[]{:S(2)}) copy-start(f32[8,128]{1,0:T(8,128)} %get-tuple-element.35.params._) | copy-start | bytes 12292
  5.3 36.0 %copy-start.14 = (f32[272,128]{1,0:T(8,128)}, f32[272,128]{1,0:T(8,128)S(1)}, u32[]{:S(2)}) copy-start(f32[272,128]{1,0:T(8,128)S(1)} %get-tuple-element.64.rest_8_) | copy-start | bytes 417796
  5.3 46.0 %copy-start.2 = (bf16[512,768]{1,0:T(8,128)(2,1)S(1)}, bf16[512,768]{1,0:T(8,128)(2,1)}, u32[]{:S(2)}) copy-start(bf16[512,768]{1,0:T(8,128)(2,1)} %constant.13.clone.forward) | copy-start | bytes 2359300
  5.3 46.0 %copy-start.3 = (bf16[256,1536]{1,0:T(8,128)(2,1)S(1)}, bf16[256,1536]{1,0:T(8,128)(2,1)}, u32[]{:S(2)}) copy-start(bf16[256,1536]{1,0:T(8,128)(2,1)} %constant.14.clone.inverse) | copy-start | bytes 2359300
  5.4 22.6 %collective-permute-start.12 = (f32[1088,128]{1,0:T(8,128)S(1)}, f32[1088,128]{1,0:T(8,128)S(1)}, u32[]{:S(2)}, u32[]{:S(2)}) collective-permute-start(f32[1088,128]{1,0:T(8,128)S(1)} %get-tuple-element.53), channel_id=1, source_target_pairs={{0,4},{4,0},{8,12},{12,8},{16,20},{20,16},{24,28},{28,24},{1,5},{5... | collective-permute-start | bytes 1671176 | tf_op jit(solution)/shard_map/ppermute | solution.py:680
  8.4 13.4 %collective-permute-start = (f32[280,128]{1,0:T(8,128)S(1)}, f32[280,128]{1,0:T(8,128)S(1)}, u32[]{:S(2)}, u32[]{:S(2)}) collective-permute-start(f32[280,128]{1,0:T(8,128)S(1)} %copy-done.26), channel_id=1, source_target_pairs={{0,16},{4,20},{8,24},{12,28},{16,0},{20,4},{24,8},{28,12},{1,17},{... | collective-permute-start | bytes 430088 | tf_op jit(solution)/shard_map/ppermute | solution.py:680
  11.0 12.8 %collective-permute-start.1 = (f32[280,128]{1,0:T(8,128)S(1)}, f32[280,128]{1,0:T(8,128)S(1)}, u32[]{:S(2)}, u32[]{:S(2)}) collective-permute-start(f32[280,128]{1,0:T(8,128)S(1)} %copy-done.25), channel_id=1, source_target_pairs={{0,20},{4,16},{8,28},{12,24},{16,4},{20,0},{24,12},{28,8},{1,21},{... | collective-permute-start | bytes 430088 | tf_op jit(solution)/shard_map/ppermute | solution.py:680
  11.0 23.0 %collective-permute-start.2 = (f32[280,128]{1,0:T(8,128)S(1)}, f32[280,128]{1,0:T(8,128)S(1)}, u32[]{:S(2)}, u32[]{:S(2)}) collective-permute-start(f32[280,128]{1,0:T(8,128)S(1)} %copy-done.24), channel_id=1, source_target_pairs={{0,4},{4,0},{8,12},{12,8},{16,20},{20,16},{24,28},{28,24},{1,5},{5... | collective-permute-start | bytes 430088 | tf_op jit(solution)/shard_map/ppermute | solution.py:680
  12.8 21.3 %collective-permute-start.3 = (f32[280,128]{1,0:T(8,128)S(1)}, f32[280,128]{1,0:T(8,128)S(1)}, u32[]{:S(2)}, u32[]{:S(2)}) collective-permute-start(f32[280,128]{1,0:T(8,128)S(1)} %copy-done.23), channel_id=1, source_target_pairs={{0,8},{4,12},{8,0},{12,4},{16,24},{20,28},{24,16},{28,20},{1,9},{5... | collective-permute-start | bytes 430088 | tf_op jit(solution)/shard_map/ppermute | solution.py:680
  21.8 13.0 %collective-permute-start.4 = (f32[280,128]{1,0:T(8,128)S(1)}, f32[280,128]{1,0:T(8,128)S(1)}, u32[]{:S(2)}, u32[]{:S(2)}) collective-permute-start(f32[280,128]{1,0:T(8,128)S(1)} %copy-done.22), channel_id=1, source_target_pairs={{0,12},{4,8},{8,4},{12,0},{16,28},{20,24},{24,20},{28,16},{1,13},{... | collective-permute-start | bytes 430088 | tf_op jit(solution)/shard_map/ppermute | solution.py:680
  23.8 14.6 %collective-permute-start.5 = (f32[280,128]{1,0:T(8,128)S(1)}, f32[280,128]{1,0:T(8,128)S(1)}, u32[]{:S(2)}, u32[]{:S(2)}) collective-permute-start(f32[280,128]{1,0:T(8,128)S(1)} %copy-done.21), channel_id=1, source_target_pairs={{0,24},{4,28},{8,16},{12,20},{16,8},{20,12},{24,0},{28,4},{1,25},{... | collective-permute-start | bytes 430088 | tf_op jit(solution)/shard_map/ppermute | solution.py:680
  28.0 10.5 %collective-permute-start.6 = (f32[280,128]{1,0:T(8,128)S(1)}, f32[280,128]{1,0:T(8,128)S(1)}, u32[]{:S(2)}, u32[]{:S(2)}) collective-permute-start(f32[280,128]{1,0:T(8,128)S(1)} %copy-done.20), channel_id=1, source_target_pairs={{0,28},{4,24},{8,20},{12,16},{16,12},{20,8},{24,4},{28,0},{1,29},{... | collective-permute-start | bytes 430088 | tf_op jit(solution)/shard_map/ppermute | solution.py:680
  34.0 25.7 %collective-permute-start.13 = (f32[544,128]{1,0:T(8,128)}, f32[544,128]{1,0:T(8,128)S(1)}, u32[]{:S(2)}, u32[]{:S(2)}) collective-permute-start(f32[544,128]{1,0:T(8,128)} %get-tuple-element.54), channel_id=1, source_target_pairs={{0,8},{4,12},{8,0},{12,4},{16,24},{20,28},{24,16},{28,20},{1,9},{5... | collective-permute-start | bytes 835592 | tf_op jit(solution)/shard_map/ppermute | solution.py:680
  34.0 25.7 %collective-permute-start.14 = (f32[544,128]{1,0:T(8,128)}, f32[544,128]{1,0:T(8,128)S(1)}, u32[]{:S(2)}, u32[]{:S(2)}) collective-permute-start(f32[544,128]{1,0:T(8,128)} %get-tuple-element.55), channel_id=1, source_target_pairs={{0,16},{4,20},{8,24},{12,28},{16,0},{20,4},{24,8},{28,12},{1,17},{... | collective-permute-start | bytes 835592 | tf_op jit(solution)/shard_map/ppermute | solution.py:680
  34.8 24.9 %collective-permute-start.15 = (f32[544,128]{1,0:T(8,128)}, f32[544,128]{1,0:T(8,128)S(1)}, u32[]{:S(2)}, u32[]{:S(2)}) collective-permute-start(f32[544,128]{1,0:T(8,128)} %get-tuple-element.56), channel_id=1, source_target_pairs={{0,24},{4,28},{8,16},{12,20},{16,8},{20,12},{24,0},{28,4},{1,25},{... | collective-permute-start | bytes 835592 | tf_op jit(solution)/shard_map/ppermute | solution.py:680
  39.8 1.5 %collective-permute-start.7 = (f32[8,16,128]{2,1,0:T(8,128)}, f32[8,16,128]{2,1,0:T(8,128)S(1)}, u32[]{:S(2)}, u32[]{:S(2)}) collective-permute-start(f32[8,16,128]{2,1,0:T(8,128)} %collect_taps.1.rest_0_), channel_id=1, source_target_pairs={{0,1},{1,0},{2,3},{3,2},{4,5},{5,4},{6,7},{7,6},{8,9},{9,8},{10,11... | collective-permute-start | bytes 196616 | tf_op jit(solution)/shard_map/ppermute | solution.py:680
  39.8 4.8 %collective-permute-start.8 = (f32[8,16,128]{2,1,0:T(8,128)}, f32[8,16,128]{2,1,0:T(8,128)}, u32[]{:S(2)}, u32[]{:S(2)}) collective-permute-start(f32[8,16,128]{2,1,0:T(8,128)} %collect_taps.1.rest_0_), channel_id=1, source_target_pairs={{0,2},{1,3},{2,0},{3,1},{4,6},{5,7},{6,4},{7,5},{8,10},{9,11},{10,... | collective-permute-start | bytes 196616 | tf_op jit(solution)/shard_map/ppermute | solution.py:680
  42.0 4.4 %collective-permute-start.9 = (f32[8,16,128]{2,1,0:T(8,128)}, f32[8,16,128]{2,1,0:T(8,128)}, u32[]{:S(2)}, u32[]{:S(2)}) collective-permute-start(f32[8,16,128]{2,1,0:T(8,128)} %collect_taps.1.rest_0_), channel_id=1, source_target_pairs={{0,3},{1,2},{2,1},{3,0},{4,7},{5,6},{6,5},{7,4},{8,11},{9,10},{10,... | collective-permute-start | bytes 196616 | tf_op jit(solution)/shard_map/ppermute | solution.py:680
  51.4 33.8 %copy-start.15 = (f32[272,128]{1,0:T(8,128)S(1)}, f32[272,128]{1,0:T(8,128)}, u32[]{:S(2)}) copy-start(f32[272,128]{1,0:T(8,128)} %copy-done.14) | copy-start | bytes 417796
  55.9 16.2 %collective-permute-start.10 = (f32[256,128]{1,0:T(8,128)S(1)}, f32[256,128]{1,0:T(8,128)S(1)}, u32[]{:S(2)}, u32[]{:S(2)}) collective-permute-start(f32[256,128]{1,0:T(8,128)S(1)} %get-tuple-element.44), channel_id=1, source_target_pairs={{0,16},{4,20},{8,24},{12,28},{16,0},{20,4},{24,8},{28,12},{1,17},{... | collective-permute-start | bytes 393224 | tf_op jit(solution)/shard_map/ppermute | solution.py:680
  58.6 15.5 %collective-permute-start.11 = (f32[256,128]{1,0:T(8,128)S(1)}, f32[256,128]{1,0:T(8,128)S(1)}, u32[]{:S(2)}, u32[]{:S(2)}) collective-permute-start(f32[256,128]{1,0:T(8,128)S(1)} %get-tuple-element.45), channel_id=1, source_target_pairs={{0,20},{4,16},{8,28},{12,24},{16,4},{20,0},{24,12},{28,8},{1,21},{... | collective-permute-start | bytes 393224 | tf_op jit(solution)/shard_map/ppermute | solution.py:680
  59.7 17.5 %collective-permute-start.16 = (f32[256,128]{1,0:T(8,128)S(1)}, f32[256,128]{1,0:T(8,128)S(1)}, u32[]{:S(2)}, u32[]{:S(2)}) collective-permute-start(f32[256,128]{1,0:T(8,128)S(1)} %get-tuple-element.57), channel_id=1, source_target_pairs={{0,4},{4,0},{8,12},{12,8},{16,20},{20,16},{24,28},{28,24},{1,5},{5... | collective-permute-start | bytes 393224 | tf_op jit(solution)/shard_map/ppermute | solution.py:680
  60.5 16.7 %collective-permute-start.17 = (f32[256,128]{1,0:T(8,128)S(1)}, f32[256,128]{1,0:T(8,128)S(1)}, u32[]{:S(2)}, u32[]{:S(2)}) collective-permute-start(f32[256,128]{1,0:T(8,128)S(1)} %get-tuple-element.58), channel_id=1, source_target_pairs={{0,8},{4,12},{8,0},{12,4},{16,24},{20,28},{24,16},{28,20},{1,9},{5... | collective-permute-start | bytes 393224 | tf_op jit(solution)/shard_map/ppermute | solution.py:680
  69.8 15.4 %collective-permute-start.18 = (f32[256,128]{1,0:T(8,128)S(1)}, f32[256,128]{1,0:T(8,128)S(1)}, u32[]{:S(2)}, u32[]{:S(2)}) collective-permute-start(f32[256,128]{1,0:T(8,128)S(1)} %get-tuple-element.59), channel_id=1, source_target_pairs={{0,12},{4,8},{8,4},{12,0},{16,28},{20,24},{24,20},{28,16},{1,13},{... | collective-permute-start | bytes 393224 | tf_op jit(solution)/shard_map/ppermute | solution.py:680
  72.1 13.0 %collective-permute-start.19 = (f32[256,128]{1,0:T(8,128)S(1)}, f32[256,128]{1,0:T(8,128)S(1)}, u32[]{:S(2)}, u32[]{:S(2)}) collective-permute-start(f32[256,128]{1,0:T(8,128)S(1)} %get-tuple-element.62), channel_id=1, source_target_pairs={{0,24},{4,28},{8,16},{12,20},{16,8},{20,12},{24,0},{28,4},{1,25},{... | collective-permute-start | bytes 393224 | tf_op jit(solution)/shard_map/ppermute | solution.py:680
  74.1 11.1 %collective-permute-start.20 = (f32[256,128]{1,0:T(8,128)S(1)}, f32[256,128]{1,0:T(8,128)S(1)}, u32[]{:S(2)}, u32[]{:S(2)}) collective-permute-start(f32[256,128]{1,0:T(8,128)S(1)} %get-tuple-element.63), channel_id=1, source_target_pairs={{0,28},{4,24},{8,20},{12,16},{16,12},{20,8},{24,4},{28,0},{1,29},{... | collective-permute-start | bytes 393224 | tf_op jit(solution)/shard_map/ppermute | solution.py:680
  (16 other events, 42.5 us)

commit v2 on v1

--- a/solution.py
+++ b/solution.py
@@ -217,6 +217,38 @@
     )
 
 
+def begun(taps, s, head):
+    first = taps[s, 0:1, :] * head[0:1]
+    second = taps[s, 0:1, :] * head[1:2] + taps[s, 1:2, :] * head[0:1]
+    return jnp.concatenate([first, second], axis=0)
+
+
+def lacked(taps, s, end):
+    first = taps[s, 1:2, :] * end[1:2] + taps[s, 2:3, :] * end[0:1]
+    return jnp.concatenate([first, taps[s, 2:3, :] * end[1:2]], axis=0)
+
+
+def upper_half(shape, count, width):
+    lane = lax.broadcasted_iota(jnp.int32, shape, 1)
+    return lane // width % count // (count // 2), lane ^ (count // 2 * width)
+
+
+def packed(low, high, side, count, width):
+    upper, opposite = upper_half(low.shape, count, width)
+    first = side == 0
+    moved = jnp.take_along_axis(jnp.where(first, high, low), opposite, axis=1)
+    return jnp.where(upper == side, jnp.where(first, low, high), moved)
+
+
+def unpacked(tile, side, count, width, fill):
+    upper, opposite = upper_half(tile.shape, count, width)
+    first = side == 0
+    moved = jnp.take_along_axis(tile, opposite, axis=1)
+    low = jnp.where(first, tile, moved)
+    high = jnp.where(first, moved, tile)
+    return jnp.where(upper == side, low, fill), jnp.where(upper == side, high, fill)
+
+
 def in_vmem():
     return pl.BlockSpec(memory_space=pltpu.VMEM)
 
@@ -252,11 +284,13 @@
 def gate_kernel(count, width, pieces, me_ref, streams, *rest):
     small, rest = rest[:3], rest[3:]
     messages, rest = rest[:count], rest[count:]
-    params, key, value, taps, skip, long_filter, sems = rest
+    params, key, value, query_end, taps, skip, long_filter, sems = rest
     length = streams.shape[1]
+    sources = (*small, streams.at[0, pl.ds(length - ROWS, ROWS)])
+    targets = (taps, skip, long_filter, query_end)
     fetches = [
         pltpu.make_async_copy(source, target, sems.at[2 * pieces + i])
-        for i, (source, target) in enumerate(zip(small, (taps, skip, long_filter)))
+        for i, (source, target) in enumerate(zip(sources, targets))
     ]
     for fetch in fetches:
         fetch.start()
@@ -307,19 +341,21 @@
         loads[2 * piece].wait()
         loads[2 * piece + 1].wait()
         lax.fori_loop(piece * part // step, (piece + 1) * part // step, block, 0)
+    key_head, value_head = (
+        begun(taps, s, buffer[ROWS : ROWS + 2, :]) for s, buffer in ((1, key), (2, value))
+    )
+    ends = [buffer[length + ROWS - 2 : length + ROWS, :] for buffer in (key, value)]
     rim = jnp.concatenate(
-        [
-            key[length + ROWS - 2 : length + ROWS, :],
-            value[length + ROWS - 2 : length + ROWS, :],
-            key[ROWS : ROWS + 2, :],
-            value[ROWS : ROWS + 2, :],
-        ],
+        [lacked(taps, 1, ends[0]), lacked(taps, 2, ends[1]), value_head]
+        + [lacked(taps, 0, query_end[ROWS - 2 : ROWS, :])],
         axis=0,
     )
-    tiles = [rim[:, tile_of(t)] for t in range(count)]
-    tiles = swap_tiles_and_slots(tiles, width, me, True)
-    for k in range(count):
-        messages[k][length : length + ROWS, :] = tiles[k]
+    head = jnp.concatenate([key_head, jnp.zeros((ROWS - 2, channels), jnp.float32)], axis=0)
+    for rows, at, size in ((rim, length, ROWS), (head, 0, 2)):
+        tiles = [rows[:, tile_of(t)] for t in range(count)]
+        tiles = swap_tiles_and_slots(tiles, width, me, True)
+        for k in range(count):
+            messages[k][at : at + size, :] = tiles[k][0:size]
 
 
 def gate(me, streams, short_filters, skip_gain, long_filter, count, width):
@@ -335,10 +371,11 @@
         scratch_shapes=[
             pltpu.VMEM((length + ROWS, channels), jnp.float32),
             pltpu.VMEM((length + ROWS, channels), jnp.float32),
+            pltpu.VMEM((ROWS, channels), jnp.float32),
             pltpu.VMEM(short_filters.shape, jnp.float32),
             pltpu.VMEM((1, channels), jnp.float32),
             pltpu.VMEM(long_filter.shape[::-1], jnp.float32),
-            pltpu.SemaphoreType.DMA((2 * pieces + 3,)),
+            pltpu.SemaphoreType.DMA((2 * pieces + 4,)),
         ],
         compiler_params=params_of(60 * 1024 * 1024),
         name="gate",
@@ -419,30 +456,24 @@
 
 def convolve_kernel(count, length, me_ref, params, forward, inverse, spectra, *rest):
     messages, rest = by_partner(rest[:count]), rest[count:]
-    outs, rest = rest[:count], rest[count:]
-    rims, bins, halves, result = rest
+    half = count // 2
+    (own_home, pair, odds), outs, rest = rest[:3], rest[3 : 3 + count], rest[3 + count :]
+    rims, bins, halves, result, query_rows = rest
     me = me_ref[0]
+    side = me // half
     rims[0] = jnp.zeros((ROWS, LANES), jnp.float32)
     for k in range(count):
         rims[(me ^ k) + 1] = messages[k][length : length + ROWS, :]
-    key_taps = [params[a : a + 1, :] for a in range(3)]
-    value_taps = [params[3 + a : 4 + a, :] for a in range(3)]
-
-    def feature(taps, now, before, earlier):
-        return taps[0] * now + taps[1] * before + taps[2] * earlier
-
-    pair = 2 * ROWS
-    row = lax.broadcasted_iota(jnp.int32, (pair, LANES), 0)
+    block_rows = 2 * ROWS
+    row = lax.broadcasted_iota(jnp.int32, (block_rows, LANES), 0)
     for k in range(count):
         at = aligned((me ^ k) * LANES, LANES)
         past = rims[me ^ k]
         rim = messages[k][length : length + ROWS, :]
-        k254, k255, v254, v255 = (past[a : a + 1, :] for a in range(4))
-        k0, k1, v0, v1 = (rim[4 + a : 5 + a, :] for a in range(4))
-        first = feature(key_taps, k0, k255, k254) * feature(value_taps, v0, v255, v254)
-        second = feature(key_taps, k1, k0, k255) * feature(value_taps, v1, v0, v255)
-        top = jnp.where(row == 0, first, jnp.where(row == 1, second, messages[k][0:pair, :]))
-        for a, b, values in ((0, pair, top), (pair, length, messages[k][pair:length, :])):
+        first = (messages[k][0:1, :] + past[0:1]) * (rim[4:5] + past[2:3])
+        second = (messages[k][1:2, :] + past[1:2]) * (rim[5:6] + past[3:4])
+        top = jnp.where(row == 0, first, jnp.where(row == 1, second, messages[k][0:block_rows, :]))
+        for a, b, values in ((0, block_rows, top), (block_rows, length, messages[k][block_rows:length, :])):
             high, low = split16(values)
             halves[a:b, at] = high
             halves[length + a : length + b, at] = low
@@ -454,7 +485,7 @@
         )
 
     def block(i, _):
-        start = pl.multiple_of(i * pair, pair)
+        start = pl.multiple_of(i * block_rows, block_rows)
         rows = []
         for at in (start, start + ROWS):
             real = [bins[pl.ds(at, ROWS), tile_of(r)] for r in range(count)]
@@ -475,12 +506,12 @@
                 both = jnp.concatenate([rows[0][r][part], rows[1][r][part]], axis=0)
                 high, low = split16(both)
                 base = start + part * length
-                halves[pl.ds(base, pair), tile_of(r)] = high
-                halves[pl.ds(base + 2 * length, pair), tile_of(r)] = low
-                halves[pl.ds(base + 4 * length, pair), tile_of(r)] = high
+                halves[pl.ds(base, block_rows), tile_of(r)] = high
+                halves[pl.ds(base + 2 * length, block_rows), tile_of(r)] = low
+                halves[pl.ds(base + 4 * length, block_rows), tile_of(r)] = high
         return 0
 
-    lax.fori_loop(0, length // pair, block, 0)
+    lax.fori_loop(0, length // block_rows, block, 0)
     for c in range(0, count, 2):
         columns = slice(c * LANES, (c + 2) * LANES)
         result[:, columns] = jnp.dot(
@@ -488,39 +519,65 @@
         )
     scale = 1.0 / length
     part = length // count
+    rows = length // 2
+    ahead = pair.shape[0] - 2 * rows
+    behind = odds.shape[0] - 2 * rows
+    homes = [
+        own_home,
+        odds.at[pl.ds(behind, rows)],
+        pair.at[pl.ds(ahead, rows)],
+        pair.at[pl.ds(ahead + rows, rows)],
+    ]
+    index = lax.broadcasted_iota(jnp.int32, (ROWS, LANES), 0)
+    for k in range(half):
+        r = me ^ k
+        query_rows[r] = homes[k][...]
+        query_rows[r ^ half] = jnp.ones((rows, LANES), jnp.float32)
+        past = rims[r]
+        lacking = jnp.where(index == 0, past[6:7], jnp.where(index == 1, past[7:8], 0.0))
+        query_rows[r, 0:ROWS, :] += jnp.where(side == 1, lacking, 0.0)
     for k in range(count):
         for m in range(0, part, ROWS):
             for r in range(count):
-                outs[k][pl.ds(m * count + r, ROWS, stride=count), :] = (
-                    result[aligned((me ^ k) * part + m, ROWS), tile_of(r)] * scale
-                )
-
-
-def convolve(me, params, forward, inverse, spectra, messages, count):
+                values = result[aligned((me ^ k) * part + m, ROWS), tile_of(r)] * scale
+                if k >= half:
+                    values *= query_rows[r, aligned((me ^ k) % half * part + m, ROWS), :]
+                outs[k][pl.ds(m * count + r, ROWS, stride=count), :] = values
+
+
+def convolve(me, params, forward, inverse, spectra, messages, homes, count):
     length = spectra.shape[1] // 2
     return pl.pallas_call(
         functools.partial(convolve_kernel, count, length),
         out_shape=[jax.ShapeDtypeStruct((length, LANES), jnp.float32)] * count,
-        in_specs=[in_smem()] + [in_vmem()] * (4 + count),
+        in_specs=[in_smem()] + [in_vmem()] * (7 + count),
         out_specs=[in_vmem()] * count,
         scratch_shapes=[
             pltpu.VMEM((count + 1, ROWS, LANES), jnp.float32),
             pltpu.VMEM((2 * length, count * LANES), jnp.float32),
             pltpu.VMEM((6 * length, count * LANES), jnp.bfloat16),
             pltpu.VMEM((length, count * LANES), jnp.float32),
+            pltpu.VMEM((count, length // 2, LANES), jnp.float32),
         ],
         compiler_params=params_of(),
         name="convolve",
-    )(me, params, forward, inverse, spectra, *far_first_operands(messages))
-
-
-def query_kernel(count, me_ref, streams, taps_in, _, *rest):
-    evens, (odds, rows, taps, sems) = rest[: count // 2], rest[count // 2 :]
+    )(me, params, forward, inverse, spectra, *far_first_operands(messages), *homes)
+
+
+def share_sizes(count, tiles, part):
+    size = tiles * (part + 2)
+    return [size] * (count // 2) + [size // 2] * (count // 2)
+
+
+def query_kernel(count, width, me_ref, streams, taps_in, gated, *rest):
+    half = count // 2
+    evens, (first_home, second_home, odds, rows, taps, sems) = rest[:half], rest[half:]
     length, channels = streams.shape[1:]
     tiles = channels // LANES
     part = length // count
-    size = tiles * (part + 2)
+    sizes = share_sizes(count, tiles, part)
     me = me_ref[0]
+    other = 1 - me // half
     load = pltpu.make_async_copy(streams.at[0], rows.at[pl.ds(ROWS, length)], sems.at[0])
     fetch = pltpu.make_async_copy(taps_in, taps, sems.at[1])
     load.start()
@@ -528,33 +585,56 @@
     rows[0:ROWS, :] = jnp.zeros((ROWS, channels), jnp.float32)
     fetch.wait()
     load.wait()
-    last = rows[length + ROWS - 1 : length + ROWS, :]
-    last_but_one = rows[length + ROWS - 2 : length + ROWS - 1, :]
-    first = taps[0, 1:2, :] * last + taps[0, 2:3, :] * last_but_one
-    second = taps[0, 2:3, :] * last
+
+    def features(base, size):
+        return [
+            short_filtered(
+                taps,
+                0,
+                tile_of(t),
+                rows[pl.ds(pl.multiple_of(base + ROWS, ROWS), size), tile_of(t)],
+                rows[pl.ds(pl.multiple_of(base, ROWS), size), tile_of(t)],
+            )
+            for t in range(tiles)
+        ]
+
+    ends = lacked(taps, 0, rows[length + ROWS - 2 : length + ROWS, :])
+    ends = [ends[:, tile_of(t)] for t in range(tiles)]
+    at = gated.shape[0]
+    odds[0:at, :] = gated[...]
     for k in range(count):
-        out, ahead = (odds, k // 2 * size) if k % 2 else (evens[k // 2], 0)
-        base = pl.multiple_of((me ^ k) * part, part)
-        for t in range(tiles):
-            now = rows[pl.ds(pl.multiple_of(base + ROWS, ROWS), part), tile_of(t)]
-            before = rows[aligned(base, part), tile_of(t)]
-            out[ahead + t * part : ahead + (t + 1) * part, :] = short_filtered(
-                taps, 0, tile_of(t), now, before
+        out, ahead = (odds, at) if k % 2 else (evens[k // 2], 0)
+        found = features((me ^ k) * part, part)
+        lacking = ends
+        if k >= half:
+            found, lacking = (
+                [packed(a, b, other, count, width) for a, b in zip(one[: tiles // 2], one[tiles // 2 :])]
+                for one in (found, ends)
             )
-            at = ahead + tiles * part + 2 * t
-            out[at : at + 2, :] = jnp.concatenate(
-                [first[:, tile_of(t)], second[:, tile_of(t)]], axis=0
-            )
-
-
-def query(me, streams, short_filters, params, count):
+        for t, (tile, end) in enumerate(zip(found, lacking)):
+            out[ahead + t * part : ahead + (t + 1) * part, :] = tile
+            last = ahead + len(found) * part + 2 * t
+            out[last : last + 2, :] = end
+        if k % 2:
+            at += sizes[k]
+    targets = [(first_home, 0), (odds, at), (second_home, 0), (odds, at + length // 2)]
+    step = 2 * part
+    for i in range(length // 2 // step):
+        found = features(other * (length // 2) + i * step, step)
+        found = swap_tiles_and_slots(found, width, me, True)
+        for k, (out, ahead) in enumerate(targets):
+            out[ahead + i * step : ahead + (i + 1) * step, :] = found[k]
+
+
+def query(me, streams, short_filters, gated, count, width):
     length, channels = streams.shape[1:]
-    size = channels // LANES * (length // count + 2)
-    sizes = [size] * (count // 2) + [count // 2 * size]
+    half = count // 2
+    sizes = share_sizes(count, channels // LANES, length // count)
+    sizes = sizes[0::2] + [length // 2] * 2 + [gated.shape[0] + sum(sizes[1::2]) + length]
     return pl.pallas_call(
-        functools.partial(query_kernel, count),
+        functools.partial(query_kernel, count, width),
         out_shape=[jax.ShapeDtypeStruct((rows, LANES), jnp.float32) for rows in sizes],
-        in_specs=[in_smem(), in_any(), in_any(), in_any()],
+        in_specs=[in_smem(), in_any(), in_any(), in_vmem()],
         out_specs=[in_vmem()] * len(sizes),
         scratch_shapes=[
             pltpu.VMEM((length + ROWS, channels), jnp.float32),
@@ -563,7 +643,7 @@
         ],
         compiler_params=params_of(),
         name="query",
-    )(me, streams, short_filters, params)
+    )(me, streams, short_filters, gated)
 
 
 def hold_kernel(*refs):
@@ -583,38 +663,64 @@
 
 
 def pair_shares_kernel(pairs, *refs):
-    evens, odds, outs = refs[:pairs], refs[pairs], refs[-pairs:]
-    size = evens[0].shape[0]
-    for i in range(pairs):
-        outs[i][0:size, :] = evens[i][...]
-        outs[i][size : 2 * size, :] = odds[(i + 1) * size : (i + 2) * size, :]
-
-
-def pair_shares(evens, odds, *earlier):
-    shape = jax.ShapeDtypeStruct((2 * evens[0].shape[0], LANES), jnp.float32)
+    evens, home, odds, outs = refs[:pairs], refs[pairs], refs[pairs + 1], refs[-pairs:]
+    rows = home.shape[0]
+    shares = evens[0].shape[0] + sum(even.shape[0] for even in evens)
+    at = odds.shape[0] - 2 * rows - shares + evens[0].shape[0]
+    for even, out in zip(evens, outs):
+        size = even.shape[0]
+        out[0:size, :] = even[...]
+        out[size : 2 * size, :] = odds[at : at + size, :]
+        at += size
+    at = odds.shape[0] - rows
+    behind = 2 * evens[0].shape[0]
+    outs[0][behind : behind + rows, :] = home[...]
+    outs[0][behind + rows : behind + 2 * rows, :] = odds[at : at + rows, :]
+
+
+def pair_shares(evens, home, odds, *earlier):
+    sizes = [2 * even.shape[0] for even in evens]
+    sizes[0] += 2 * home.shape[0]
     return pl.pallas_call(
         functools.partial(pair_shares_kernel, len(evens)),
-        out_shape=[shape] * len(evens),
-        in_specs=[in_vmem()] * (len(evens) + 1) + [in_any()] * len(earlier),
+        out_shape=[jax.ShapeDtypeStruct((size, LANES), jnp.float32) for size in sizes],
+        in_specs=[in_vmem()] * (len(evens) + 2) + [in_any()] * len(earlier),
         out_specs=[in_vmem()] * len(evens),
         compiler_params=params_of(),
         name="pair_shares",
-    )(*evens, odds, *earlier)
-
-
-def arrange_query(count, me, shares, out, lacking):
+    )(*evens, home, odds, *earlier)
+
+
+def arrange_query(count, width, me, shares, out, lacking):
+    half = count // 2
     tiles, rows = out.shape[:2]
     part = rows // count
+    side = me // half
     lacking[...] = jnp.zeros(lacking.shape, jnp.float32)
+
+    def put(t, r, tile, ends):
+        for m in range(0, part, ROWS):
+            out[t, pl.ds(m * count + r, ROWS, stride=count), :] = tile[m : m + ROWS]
+        lacking[t, pl.ds(r + 1, 2, stride=2 * count), :] = ends
+
     for k in range(count):
         r = me ^ k
-        for t in range(tiles):
-            for m in range(0, part, ROWS):
-                at = t * part + m
-                out[t, pl.ds(m * count + r, ROWS, stride=count), :] = shares[k][at : at + ROWS, :]
-            at = tiles * part + t * 2
-            lacking[t, pl.ds(r + 1, 2, stride=2 * count), :] = shares[k][at : at + 2, :]
-    first = (me == 0).astype(jnp.float32)
+        near = k < half
+        given = tiles if near else tiles // 2
+        for t in range(given):
+            tile = shares[k][t * part : (t + 1) * part, :]
+            at = given * part + t * 2
+            ends = shares[k][at : at + 2, :]
+            if near:
+                put(t, r, tile, ends)
+            else:
+                tile = unpacked(tile, side, count, width, 1.0)
+                ends = unpacked(ends, side, count, width, 0.0)
+                for i in range(2):
+                    put(t + i * given, r, tile[i], ends[i])
+    panel = lax.broadcasted_iota(jnp.int32, (count, LANES), 0)
+    upper, _ = upper_half((count, LANES), count, width)
+    first = jnp.where((me == 0) & ((panel < half) | (upper == 0)), 1.0, 0.0)
     for t in range(tiles):
         for m in range(2):
             at = slice(m * count, (m + 1) * count)
@@ -628,11 +734,14 @@
     out, rows, query_rows, lacking, sems = rest[half + 1 :]
     me = me_ref[0]
     part = out.shape[0]
-    size = own.shape[0]
-    shares = [own, odds.at[pl.ds(0, size)]]
-    for pair in pairs:
+    length = part * count
+    sizes = share_sizes(count, query_rows.shape[0], part)
+    start = odds.shape[0] - length - sum(sizes[1::2])
+    shares = [own, odds.at[pl.ds(start, sizes[1])]]
+    for i, pair in enumerate(pairs, 1):
+        size = sizes[2 * i]
         shares += [pair.at[pl.ds(0, size)], pair.at[pl.ds(size, size)]]
-    arrange_query(count, me, shares, query_rows, lacking)
+    arrange_query(count, width, me, shares, query_rows, lacking)
     step = 4
     stores = []
 
@@ -699,15 +808,19 @@
     *gated, params = gate(me, streams, short_filters, skip_gain, long_filter, count, width)
     half = count // 2
     tiles = streams.shape[2] // LANES
-    *evens, odds = query(me, streams, short_filters, params, count)
-    odds = swapped(odds, "seq", 1)
+    *evens, own_home, next_home, odds = query(
+        me, streams, short_filters, gated[1], count, width
+    )
+    gated[1] = odds
     gated = exchanged(gated, "seq")
-    pairs = pair_shares(evens[1:], odds, *gated[half:half + 2])
+    odds = gated[1]
+    pairs = pair_shares(evens[1:], next_home, odds, *gated[2:])
     taps = collect_taps(me, gated, count, width, length)
     taps = [taps] + [swapped(taps, "grp", k) for k in range(1, groups)]
     pairs = [swapped(pair, "seq", 2 * i) for i, pair in enumerate(pairs, 1)]
     spectra = filter_spectra(group, params, forward, taps, count, width)
-    convolved = list(convolve(me, params, forward, inverse, spectra, gated, count))
+    homes = (own_home, pairs[0], odds)
+    convolved = list(convolve(me, params, forward, inverse, spectra, gated, homes, count))
     convolved[1:half] = hold(convolved[1:half], *pairs)
     first = [swapped(convolved[k], "seq", k) for k in (half, half + 1)]
     convolved[half + 2 :] = hold(convolved[half + 2 :], *pairs, first[0])

time: 88.4 us -> 85 us (0.962)
  the two profiles are of different devices: /device:TPU:0 before, /device:TPU:20 now
where the time goes in v2:
time: 85 us; the launch traced here: 84.8 us
  waiting for transfers between devices  36.4 us (43%)
  starting transfers between devices  29.4 us (35%)
  Pallas kernels  16.4 us (19%)
  local copies, waits for them, and re-layouts  2.44 us (3%)
    ppermute x20, waiting for transfers between devices, swapped(): lax.ppermute(block, axis, [(i, i ^ k) for i in range(lax.axis_size(axis))])  36.4 us
    ppermute x20, starting transfers between devices, swapped(): lax.ppermute(block, axis, [(i, i ^ k) for i in range(lax.axis_size(axis))])  29.4 us
    pallas_call x1, Pallas kernels, convolve(): pl.pallas_call(functools.partial(convolve_kernel, count, length), out_sha...  4.59 us
    pallas_call x1, Pallas kernels, gate(): pl.pallas_call(functools.partial(gate_kernel, count, width, pieces), out_...  4.05 us
    pallas_call x1, Pallas kernels, finish(): pl.pallas_call(functools.partial(finish_kernel, count, width, pieces), ou...  3.02 us
    pallas_call x1, Pallas kernels, filter_spectra(): pl.pallas_call(functools.partial(filter_kernel, count, width), out_shape=...  2.83 us
    unnamed x30, local copies, waits for them, and re-layouts  2.44 us
  transfers between devices with their start and end apart: 20, of which 12 were waited for; matrix products, arithmetic and copies ran while one was open for 0% of the time, Pallas kernels for 9%

profile of v2, /device:TPU:20, one launch (start us, length us, event | category | flops | bytes accessed | tf_op | source)
XLA Modules:
  0.0 84.8 jit_solution(8789900175374660281)
XLA Ops:
  0.0 4.0 %gate.1 = (f32[280,128]{1,0:T(8,128)}, f32[280,128]{1,0:T(8,128)}, f32[280,128]{1,0:T(8,128)}, f32[280,128]{1,0:T(8,128)}, f32[280,128]{1,0:T(8,128)}, /*index=5...) custom-call(s32[1]{0:T(128)} %bitcast.me_ref, f32[3,256,1024]{2,1,0:T(8,128)} %streams.3, ...), custom_call_target="tpu_custom_call" | custom-call | tf_op jit(solution)/shard_map/gate/pallas_call | solution.py:366
  4.1 0.9 %copy-done.5 = f32[280,128]{1,0:T(8,128)S(1)} copy-done((f32[280,128]{1,0:T(8,128)S(1)}, f32[280,128]{1,0:T(8,128)}, u32[]{:S(2)}) %copy-start.5) | copy-done | bytes 143384
  5.1 1.0 %query.1 = (f32[272,128]{1,0:T(8,128)S(1)}, f32[272,128]{1,0:T(8,128)S(1)}, f32[136,128]{1,0:T(8,128)S(1)}, f32[136,128]{1,0:T(8,128)S(1)}, f32[128,128]{1,0:T(8...) custom-call(s32[1]{0:T(128)} %bitcast.me_ref, f32[3,256,1024]{2,1,0:T(8,128)S(1)} %copy-done, ...), custom_call_target="tpu_custom_call" | custom-call | tf_op jit(solution)/shard_map/query/pallas_call | solution.py:634
  6.1 1.6 %collective-permute-start.2 = (f32[1352,128]{1,0:T(8,128)S(1)}, f32[1352,128]{1,0:T(8,128)S(1)}, u32[]{:S(2)}, u32[]{:S(2)}) collective-permute-start(f32[1352,128]{1,0:T(8,128)S(1)} %get-tuple-element.42), channel_id=1, source_target_pairs={{0,4},{4,0},{8,12},{12,8},{16,20},{20,16},{24,28},{28,24},{1,5},{5... | collective-permute-start | bytes 2076680 | tf_op jit(solution)/shard_map/ppermute | solution.py:789
  8.0 2.6 %collective-permute-start.1 = (f32[280,128]{1,0:T(8,128)S(1)}, f32[280,128]{1,0:T(8,128)S(1)}, u32[]{:S(2)}, u32[]{:S(2)}) collective-permute-start(f32[280,128]{1,0:T(8,128)S(1)} %copy-done.13), channel_id=1, source_target_pairs={{0,20},{4,16},{8,28},{12,24},{16,4},{20,0},{24,12},{28,8},{1,21},{... | collective-permute-start | bytes 430088 | tf_op jit(solution)/shard_map/ppermute | solution.py:789
  10.6 1.6 %collective-permute-start.3 = (f32[280,128]{1,0:T(8,128)S(1)}, f32[280,128]{1,0:T(8,128)S(1)}, u32[]{:S(2)}, u32[]{:S(2)}) collective-permute-start(f32[280,128]{1,0:T(8,128)S(1)} %copy-done.12), channel_id=1, source_target_pairs={{0,8},{4,12},{8,0},{12,4},{16,24},{20,28},{24,16},{28,20},{1,9},{5... | collective-permute-start | bytes 430088 | tf_op jit(solution)/shard_map/ppermute | solution.py:789
  12.1 1.4 %collective-permute-start.4 = (f32[280,128]{1,0:T(8,128)S(1)}, f32[280,128]{1,0:T(8,128)S(1)}, u32[]{:S(2)}, u32[]{:S(2)}) collective-permute-start(f32[280,128]{1,0:T(8,128)S(1)} %copy-done.11), channel_id=1, source_target_pairs={{0,12},{4,8},{8,4},{12,0},{16,28},{20,24},{24,20},{28,16},{1,13},{... | collective-permute-start | bytes 430088 | tf_op jit(solution)/shard_map/ppermute | solution.py:789
  13.5 4.6 %collective-permute-done.rest_0_.refs_7_ = f32[280,128]{1,0:T(8,128)S(1)} collective-permute-done((f32[280,128]{1,0:T(8,128)S(1)}, f32[280,128]{1,0:T(8,128)S(1)}, u32[]{:S(2)}, u32[]{:S(2)}) %collective-permute-start) | collective-permute-done | bytes 143392 | tf_op jit(solution)/shard_map/ppermute | solution.py:789
  18.1 1.5 %collective-permute-start.5 = (f32[280,128]{1,0:T(8,128)S(1)}, f32[280,128]{1,0:T(8,128)S(1)}, u32[]{:S(2)}, u32[]{:S(2)}) collective-permute-start(f32[280,128]{1,0:T(8,128)S(1)} %copy-done.10), channel_id=1, source_target_pairs={{0,24},{4,28},{8,16},{12,20},{16,8},{20,12},{24,0},{28,4},{1,25},{... | collective-permute-start | bytes 430088 | tf_op jit(solution)/shard_map/ppermute | solution.py:789
  20.3 2.4 %collective-permute-start.6 = (f32[280,128]{1,0:T(8,128)S(1)}, f32[280,128]{1,0:T(8,128)S(1)}, u32[]{:S(2)}, u32[]{:S(2)}) collective-permute-start(f32[280,128]{1,0:T(8,128)S(1)} %copy-done.9), channel_id=1, source_target_pairs={{0,28},{4,24},{8,20},{12,16},{16,12},{20,8},{24,4},{28,0},{1,29},{... | collective-permute-start | bytes 430088 | tf_op jit(solution)/shard_map/ppermute | solution.py:789
  22.7 0.9 %collective-permute-done.4.rest_5_.refs_6_ = f32[280,128]{1,0:T(8,128)S(1)} collective-permute-done((f32[280,128]{1,0:T(8,128)S(1)}, f32[280,128]{1,0:T(8,128)S(1)}, u32[]{:S(2)}, u32[]{:S(2)}) %collective-permute-start.4) | collective-permute-done | bytes 143392 | tf_op jit(solution)/shard_map/ppermute | solution.py:789
  23.6 8.8 %collective-permute-done.5.rest_6_.refs_9_ = f32[280,128]{1,0:T(8,128)S(1)} collective-permute-done((f32[280,128]{1,0:T(8,128)S(1)}, f32[280,128]{1,0:T(8,128)S(1)}, u32[]{:S(2)}, u32[]{:S(2)}) %collective-permute-start.5) | collective-permute-done | bytes 143392 | tf_op jit(solution)/shard_map/ppermute | solution.py:789
  32.4 2.9 %collective-permute-done.6.rest_7_.refs_10_ = f32[280,128]{1,0:T(8,128)S(1)} collective-permute-done((f32[280,128]{1,0:T(8,128)S(1)}, f32[280,128]{1,0:T(8,128)S(1)}, u32[]{:S(2)}, u32[]{:S(2)}) %collective-permute-start.6) | collective-permute-done | bytes 143392 | tf_op jit(solution)/shard_map/ppermute | solution.py:789
  35.4 0.9 %pair_shares.1 = (f32[800,128]{1,0:T(8,128)}, f32[272,128]{1,0:T(8,128)}, f32[272,128]{1,0:T(8,128)}) custom-call(f32[272,128]{1,0:T(8,128)S(1)} %get-tuple-element.48.refs_0_, f32[136,128]{1,0:T(8,128)S(1)} %get-tuple-element.49.refs_1_, f32[136,128]{1,0:T(8,128)S(1)} %get-tuple-element.50.refs_2_, f32[128,128]{1,0:T(8,128)S(1)} %get-tuple-element.51.refs_3_, ...), custom_call_target="tpu_custom_call" | custom-call | tf_op jit(solution)/shard_map/pair_shares/pallas_call | solution.py:684
  36.2 1.0 %collective-permute-start.13 = (f32[272,128]{1,0:T(8,128)}, f32[272,128]{1,0:T(8,128)S(1)}, u32[]{:S(2)}, u32[]{:S(2)}) collective-permute-start(f32[272,128]{1,0:T(8,128)} %get-tuple-element.59), channel_id=1, source_target_pairs={{0,16},{4,20},{8,24},{12,28},{16,0},{20,4},{24,8},{28,12},{1,17},{... | collective-permute-start | bytes 417800 | tf_op jit(solution)/shard_map/ppermute | solution.py:789
  37.3 2.4 %collective-permute-start.14 = (f32[272,128]{1,0:T(8,128)}, f32[272,128]{1,0:T(8,128)S(1)}, u32[]{:S(2)}, u32[]{:S(2)}) collective-permute-start(f32[272,128]{1,0:T(8,128)} %get-tuple-element.60), channel_id=1, source_target_pairs={{0,24},{4,28},{8,16},{12,20},{16,8},{20,12},{24,0},{28,4},{1,25},{... | collective-permute-start | bytes 417800 | tf_op jit(solution)/shard_map/ppermute | solution.py:789
  39.8 0.8 collective-permute-start.8
  40.6 3.1 %collective-permute-done.9.rest_3_ = f32[8,16,128]{2,1,0:T(8,128)S(1)} collective-permute-done((f32[8,16,128]{2,1,0:T(8,128)S(1)}, f32[8,16,128]{2,1,0:T(8,128)S(1)}, u32[]{:S(2)}, u32[]{:S(2)}) %collective-permute-start.9) | collective-permute-done | bytes 65568 | tf_op jit(solution)/shard_map/ppermute | solution.py:789
  44.9 0.8 collective-permute-done.7.rest_1_
  45.7 0.8 copy-done.7
  46.6 2.8 %filter_spectra.1.spectra = f32[8,512,128]{2,1,0:T(8,128)S(1)} custom-call(s32[1]{0:T(128)} %bitcast.3.group_ref, f32[8,128]{1,0:T(8,128)S(1)} %copy-done.8, bf16[512,768]{1,0:T(8,128)(2,1)S(1)} %copy-done.1, f32[8,16,128]{2,1,0:T(8,128)S(1)} %collect_taps.1.rest_0_, f32[8,16,128]{2,1,0:T(8,128)} %collective-permute-done.7.rest_1_, ...), custom_call_target="tpu_custom_call" | custom-call | tf_op jit(solution)/shard_map/filter_spectra/pallas_call | solution.py:443
  49.4 4.6 %convolve.1 = (f32[256,128]{1,0:T(8,128)S(1)}, f32[256,128]{1,0:T(8,128)S(1)}, f32[256,128]{1,0:T(8,128)S(1)}, f32[256,128]{1,0:T(8,128)S(1)}, f32[256,128]{1,0:...) custom-call(s32[1]{0:T(128)} %bitcast.me_ref, f32[8,128]{1,0:T(8,128)S(1)} %copy-done.8, ...), custom_call_target="tpu_custom_call" | custom-call | tf_op jit(solution)/shard_map/convolve/pallas_call | solution.py:550
  54.0 1.4 %collective-permute-start.11 = (f32[256,128]{1,0:T(8,128)S(1)}, f32[256,128]{1,0:T(8,128)S(1)}, u32[]{:S(2)}, u32[]{:S(2)}) collective-permute-start(f32[256,128]{1,0:T(8,128)S(1)} %get-tuple-element.53), channel_id=1, source_target_pairs={{0,16},{4,20},{8,24},{12,28},{16,0},{20,4},{24,8},{28,12},{1,17},{... | collective-permute-start | bytes 393224 | tf_op jit(solution)/shard_map/ppermute | solution.py:789
  55.4 2.6 %collective-permute-start.15 = (f32[256,128]{1,0:T(8,128)S(1)}, f32[256,128]{1,0:T(8,128)S(1)}, u32[]{:S(2)}, u32[]{:S(2)}) collective-permute-start(f32[256,128]{1,0:T(8,128)S(1)} %get-tuple-element.61), channel_id=1, source_target_pairs={{0,4},{4,0},{8,12},{12,8},{16,20},{20,16},{24,28},{28,24},{1,5},{5... | collective-permute-start | bytes 393224 | tf_op jit(solution)/shard_map/ppermute | solution.py:789
  58.0 2.3 %collective-permute-start.16 = (f32[256,128]{1,0:T(8,128)S(1)}, f32[256,128]{1,0:T(8,128)S(1)}, u32[]{:S(2)}, u32[]{:S(2)}) collective-permute-start(f32[256,128]{1,0:T(8,128)S(1)} %get-tuple-element.62), channel_id=1, source_target_pairs={{0,8},{4,12},{8,0},{12,4},{16,24},{20,28},{24,16},{28,20},{1,9},{5... | collective-permute-start | bytes 393224 | tf_op jit(solution)/shard_map/ppermute | solution.py:789
  60.4 3.7 %collective-permute-start.12 = (f32[256,128]{1,0:T(8,128)S(1)}, f32[256,128]{1,0:T(8,128)S(1)}, u32[]{:S(2)}, u32[]{:S(2)}) collective-permute-start(f32[256,128]{1,0:T(8,128)S(1)} %get-tuple-element.54), channel_id=1, source_target_pairs={{0,20},{4,16},{8,28},{12,24},{16,4},{20,0},{24,12},{28,8},{1,21},{... | collective-permute-start | bytes 393224 | tf_op jit(solution)/shard_map/ppermute | solution.py:789
  64.7 3.0 %collective-permute-start.19 = (f32[256,128]{1,0:T(8,128)S(1)}, f32[256,128]{1,0:T(8,128)S(1)}, u32[]{:S(2)}, u32[]{:S(2)}) collective-permute-start(f32[256,128]{1,0:T(8,128)S(1)} %get-tuple-element.67), channel_id=1, source_target_pairs={{0,28},{4,24},{8,20},{12,16},{16,12},{20,8},{24,4},{28,0},{1,29},{... | collective-permute-start | bytes 393224 | tf_op jit(solution)/shard_map/ppermute | solution.py:789
  67.7 3.0 %collective-permute-done.17.rest_5_ = f32[256,128]{1,0:T(8,128)S(1)} collective-permute-done((f32[256,128]{1,0:T(8,128)S(1)}, f32[256,128]{1,0:T(8,128)S(1)}, u32[]{:S(2)}, u32[]{:S(2)}) %collective-permute-start.17) | collective-permute-done | bytes 131104 | tf_op jit(solution)/shard_map/ppermute | solution.py:789
  70.7 4.3 %collective-permute-done.12.rest_1_ = f32[256,128]{1,0:T(8,128)S(1)} collective-permute-done((f32[256,128]{1,0:T(8,128)S(1)}, f32[256,128]{1,0:T(8,128)S(1)}, u32[]{:S(2)}, u32[]{:S(2)}) %collective-permute-start.12) | collective-permute-done | bytes 131104 | tf_op jit(solution)/shard_map/ppermute | solution.py:789
  75.0 3.6 %collective-permute-done.18.rest_6_ = f32[256,128]{1,0:T(8,128)S(1)} collective-permute-done((f32[256,128]{1,0:T(8,128)S(1)}, f32[256,128]{1,0:T(8,128)S(1)}, u32[]{:S(2)}, u32[]{:S(2)}) %collective-permute-start.18) | collective-permute-done | bytes 131104 | tf_op jit(solution)/shard_map/ppermute | solution.py:789
  78.7 3.1 %collective-permute-done.19.rest_7_ = f32[256,128]{1,0:T(8,128)S(1)} collective-permute-done((f32[256,128]{1,0:T(8,128)S(1)}, f32[256,128]{1,0:T(8,128)S(1)}, u32[]{:S(2)}, u32[]{:S(2)}) %collective-permute-start.19) | collective-permute-done | bytes 131104 | tf_op jit(solution)/shard_map/ppermute | solution.py:789
  81.8 3.0 %finish.1 = f32[32,8,1024]{2,1,0:T(8,128)} custom-call(s32[1]{0:T(128)} %bitcast.me_ref, f32[256,128]{1,0:T(8,128)S(1)} %collective-permute-done.11.refs_5_.rest_0_, f32[256,128]{1,0:T(8,128)S(1)} %collective-permute-done.12.rest_1_, f32[256,128]{1,0:T(8,128)S(1)} %get-tuple-element.55.rest_2_, f32[256,128]{1,0:T(8,128)S(1)} %collective-permute-done.15.rest_3_, ...), custom_call_target="tpu_custom_call" | custom-call | tf_op jit(solution)/shard_map/finish/pallas_call | solution.py:772
  (47 shorter events, 3.0 us)
Async XLA Ops:
  0.0 4.1 %copy-start.4 = (f32[3,3,1024]{2,1,0:T(4,128)S(1)}, f32[3,3,1024]{2,1,0:T(4,128)}, u32[]{:S(2)}) copy-start(f32[3,3,1024]{2,1,0:T(4,128)} %taps_in.1) | copy-start | bytes 110596
  0.0 4.1 %copy-start = (f32[3,256,1024]{2,1,0:T(8,128)S(1)}, f32[3,256,1024]{2,1,0:T(8,128)}, u32[]{:S(2)}) copy-start(f32[3,256,1024]{2,1,0:T(8,128)} %streams.3) | copy-start | bytes 9437188
  4.1 35.7 %copy-start.3 = (f32[280,128]{1,0:T(8,128)S(1)}, f32[280,128]{1,0:T(8,128)}, u32[]{:S(2)}) copy-start(f32[280,128]{1,0:T(8,128)} %get-tuple-element.40.rest_2_) | copy-start | bytes 430084
  5.0 2.6 %copy-start.14 = (f32[280,128]{1,0:T(8,128)S(1)}, f32[280,128]{1,0:T(8,128)}, u32[]{:S(2)}) copy-start(f32[280,128]{1,0:T(8,128)} %get-tuple-element.38) | copy-start | bytes 430084
  5.0 3.0 %copy-start.13 = (f32[280,128]{1,0:T(8,128)S(1)}, f32[280,128]{1,0:T(8,128)}, u32[]{:S(2)}) copy-start(f32[280,128]{1,0:T(8,128)} %get-tuple-element.39) | copy-start | bytes 430084
  5.0 5.5 %copy-start.12 = (f32[280,128]{1,0:T(8,128)S(1)}, f32[280,128]{1,0:T(8,128)}, u32[]{:S(2)}) copy-start(f32[280,128]{1,0:T(8,128)} %get-tuple-element.43) | copy-start | bytes 430084
  5.0 7.1 %copy-start.11 = (f32[280,128]{1,0:T(8,128)S(1)}, f32[280,128]{1,0:T(8,128)}, u32[]{:S(2)}) copy-start(f32[280,128]{1,0:T(8,128)} %get-tuple-element.44) | copy-start | bytes 430084
  5.0 13.0 %copy-start.10 = (f32[280,128]{1,0:T(8,128)S(1)}, f32[280,128]{1,0:T(8,128)}, u32[]{:S(2)}) copy-start(f32[280,128]{1,0:T(8,128)} %get-tuple-element.45) | copy-start | bytes 430084
  5.1 15.2 %copy-start.9 = (f32[280,128]{1,0:T(8,128)S(1)}, f32[280,128]{1,0:T(8,128)}, u32[]{:S(2)}) copy-start(f32[280,128]{1,0:T(8,128)} %get-tuple-element.46) | copy-start | bytes 430084
  5.1 40.7 %copy-start.8 = (f32[8,128]{1,0:T(8,128)S(1)}, f32[8,128]{1,0:T(8,128)}, u32[]{:S(2)}) copy-start(f32[8,128]{1,0:T(8,128)} %get-tuple-element.37.params) | copy-start | bytes 12292
  6.1 39.6 %copy-start.1 = (bf16[512,768]{1,0:T(8,128)(2,1)S(1)}, bf16[512,768]{1,0:T(8,128)(2,1)}, u32[]{:S(2)}) copy-start(bf16[512,768]{1,0:T(8,128)(2,1)} %constant.13.clone.forward) | copy-start | bytes 2359300
  6.1 29.2 %collective-permute-start.2 = (f32[1352,128]{1,0:T(8,128)S(1)}, f32[1352,128]{1,0:T(8,128)S(1)}, u32[]{:S(2)}, u32[]{:S(2)}) collective-permute-start(f32[1352,128]{1,0:T(8,128)S(1)} %get-tuple-element.42), channel_id=1, source_target_pairs={{0,4},{4,0},{8,12},{12,8},{16,20},{20,16},{24,28},{28,24},{1,5},{5... | collective-permute-start | bytes 2076680 | tf_op jit(solution)/shard_map/ppermute | solution.py:789
  7.7 10.4 %collective-permute-start = (f32[280,128]{1,0:T(8,128)S(1)}, f32[280,128]{1,0:T(8,128)S(1)}, u32[]{:S(2)}, u32[]{:S(2)}) collective-permute-start(f32[280,128]{1,0:T(8,128)S(1)} %copy-done.14), channel_id=1, source_target_pairs={{0,16},{4,20},{8,24},{12,28},{16,0},{20,4},{24,8},{28,12},{1,17},{... | collective-permute-start | bytes 430088 | tf_op jit(solution)/shard_map/ppermute | solution.py:789
  8.0 12.3 %collective-permute-start.1 = (f32[280,128]{1,0:T(8,128)S(1)}, f32[280,128]{1,0:T(8,128)S(1)}, u32[]{:S(2)}, u32[]{:S(2)}) collective-permute-start(f32[280,128]{1,0:T(8,128)S(1)} %copy-done.13), channel_id=1, source_target_pairs={{0,20},{4,16},{8,28},{12,24},{16,4},{20,0},{24,12},{28,8},{1,21},{... | collective-permute-start | bytes 430088 | tf_op jit(solution)/shard_map/ppermute | solution.py:789
  10.6 12.1 %collective-permute-start.3 = (f32[280,128]{1,0:T(8,128)S(1)}, f32[280,128]{1,0:T(8,128)S(1)}, u32[]{:S(2)}, u32[]{:S(2)}) collective-permute-start(f32[280,128]{1,0:T(8,128)S(1)} %copy-done.12), channel_id=1, source_target_pairs={{0,8},{4,12},{8,0},{12,4},{16,24},{20,28},{24,16},{28,20},{1,9},{5... | collective-permute-start | bytes 430088 | tf_op jit(solution)/shard_map/ppermute | solution.py:789
  12.1 11.4 %collective-permute-start.4 = (f32[280,128]{1,0:T(8,128)S(1)}, f32[280,128]{1,0:T(8,128)S(1)}, u32[]{:S(2)}, u32[]{:S(2)}) collective-permute-start(f32[280,128]{1,0:T(8,128)S(1)} %copy-done.11), channel_id=1, source_target_pairs={{0,12},{4,8},{8,4},{12,0},{16,28},{20,24},{24,20},{28,16},{1,13},{... | collective-permute-start | bytes 430088 | tf_op jit(solution)/shard_map/ppermute | solution.py:789
  18.1 14.3 %collective-permute-start.5 = (f32[280,128]{1,0:T(8,128)S(1)}, f32[280,128]{1,0:T(8,128)S(1)}, u32[]{:S(2)}, u32[]{:S(2)}) collective-permute-start(f32[280,128]{1,0:T(8,128)S(1)} %copy-done.10), channel_id=1, source_target_pairs={{0,24},{4,28},{8,16},{12,20},{16,8},{20,12},{24,0},{28,4},{1,25},{... | collective-permute-start | bytes 430088 | tf_op jit(solution)/shard_map/ppermute | solution.py:789
  20.3 15.1 %collective-permute-start.6 = (f32[280,128]{1,0:T(8,128)S(1)}, f32[280,128]{1,0:T(8,128)S(1)}, u32[]{:S(2)}, u32[]{:S(2)}) collective-permute-start(f32[280,128]{1,0:T(8,128)S(1)} %copy-done.9), channel_id=1, source_target_pairs={{0,28},{4,24},{8,20},{12,16},{16,12},{20,8},{24,4},{28,0},{1,29},{... | collective-permute-start | bytes 430088 | tf_op jit(solution)/shard_map/ppermute | solution.py:789
  36.2 13.2 %collective-permute-start.10 = (f32[800,128]{1,0:T(8,128)}, f32[800,128]{1,0:T(8,128)S(1)}, u32[]{:S(2)}, u32[]{:S(2)}) collective-permute-start(f32[800,128]{1,0:T(8,128)} %get-tuple-element.52), channel_id=1, source_target_pairs={{0,8},{4,12},{8,0},{12,4},{16,24},{20,28},{24,16},{28,20},{1,9},{5... | collective-permute-start | bytes 1228808 | tf_op jit(solution)/shard_map/ppermute | solution.py:789
  36.2 19.1 %collective-permute-start.13 = (f32[272,128]{1,0:T(8,128)}, f32[272,128]{1,0:T(8,128)S(1)}, u32[]{:S(2)}, u32[]{:S(2)}) collective-permute-start(f32[272,128]{1,0:T(8,128)} %get-tuple-element.59), channel_id=1, source_target_pairs={{0,16},{4,20},{8,24},{12,28},{16,0},{20,4},{24,8},{28,12},{1,17},{... | collective-permute-start | bytes 417800 | tf_op jit(solution)/shard_map/ppermute | solution.py:789
  37.3 18.1 %collective-permute-start.14 = (f32[272,128]{1,0:T(8,128)}, f32[272,128]{1,0:T(8,128)S(1)}, u32[]{:S(2)}, u32[]{:S(2)}) collective-permute-start(f32[272,128]{1,0:T(8,128)} %get-tuple-element.60), channel_id=1, source_target_pairs={{0,24},{4,28},{8,16},{12,20},{16,8},{20,12},{24,0},{28,4},{1,25},{... | collective-permute-start | bytes 417800 | tf_op jit(solution)/shard_map/ppermute | solution.py:789
  39.7 4.0 %collective-permute-start.9 = (f32[8,16,128]{2,1,0:T(8,128)S(1)}, f32[8,16,128]{2,1,0:T(8,128)S(1)}, u32[]{:S(2)}, u32[]{:S(2)}) collective-permute-start(f32[8,16,128]{2,1,0:T(8,128)S(1)} %collect_taps.1.rest_0_), channel_id=1, source_target_pairs={{0,3},{1,2},{2,1},{3,0},{4,7},{5,6},{6,5},{7,4},{8,11},{9,10},{10,... | collective-permute-start | bytes 196616 | tf_op jit(solution)/shard_map/ppermute | solution.py:789
  39.8 5.1 %collective-permute-start.8 = (f32[8,16,128]{2,1,0:T(8,128)S(1)}, f32[8,16,128]{2,1,0:T(8,128)}, u32[]{:S(2)}, u32[]{:S(2)}) collective-permute-start(f32[8,16,128]{2,1,0:T(8,128)S(1)} %collect_taps.1.rest_0_), channel_id=1, source_target_pairs={{0,2},{1,3},{2,0},{3,1},{4,6},{5,7},{6,4},{7,5},{8,10},{9,11},{10,... | collective-permute-start | bytes 196616 | tf_op jit(solution)/shard_map/ppermute | solution.py:789
  44.3 1.4 %collective-permute-start.7 = (f32[8,16,128]{2,1,0:T(8,128)S(1)}, f32[8,16,128]{2,1,0:T(8,128)}, u32[]{:S(2)}, u32[]{:S(2)}) collective-permute-start(f32[8,16,128]{2,1,0:T(8,128)S(1)} %collect_taps.1.rest_0_), channel_id=1, source_target_pairs={{0,1},{1,0},{2,3},{3,2},{4,5},{5,4},{6,7},{7,6},{8,9},{9,8},{10,11... | collective-permute-start | bytes 196616 | tf_op jit(solution)/shard_map/ppermute | solution.py:789
  44.3 5.1 %copy-start.2 = (bf16[256,1536]{1,0:T(8,128)(2,1)S(1)}, bf16[256,1536]{1,0:T(8,128)(2,1)}, u32[]{:S(2)}) copy-start(bf16[256,1536]{1,0:T(8,128)(2,1)} %constant.14.clone.inverse) | copy-start | bytes 2359300
  54.0 10.1 %collective-permute-start.11 = (f32[256,128]{1,0:T(8,128)S(1)}, f32[256,128]{1,0:T(8,128)S(1)}, u32[]{:S(2)}, u32[]{:S(2)}) collective-permute-start(f32[256,128]{1,0:T(8,128)S(1)} %get-tuple-element.53), channel_id=1, source_target_pairs={{0,16},{4,20},{8,24},{12,28},{16,0},{20,4},{24,8},{28,12},{1,17},{... | collective-permute-start | bytes 393224 | tf_op jit(solution)/shard_map/ppermute | solution.py:789
  55.4 9.4 %collective-permute-start.15 = (f32[256,128]{1,0:T(8,128)S(1)}, f32[256,128]{1,0:T(8,128)S(1)}, u32[]{:S(2)}, u32[]{:S(2)}) collective-permute-start(f32[256,128]{1,0:T(8,128)S(1)} %get-tuple-element.61), channel_id=1, source_target_pairs={{0,4},{4,0},{8,12},{12,8},{16,20},{20,16},{24,28},{28,24},{1,5},{5... | collective-permute-start | bytes 393224 | tf_op jit(solution)/shard_map/ppermute | solution.py:789
  58.0 9.7 %collective-permute-start.16 = (f32[256,128]{1,0:T(8,128)S(1)}, f32[256,128]{1,0:T(8,128)S(1)}, u32[]{:S(2)}, u32[]{:S(2)}) collective-permute-start(f32[256,128]{1,0:T(8,128)S(1)} %get-tuple-element.62), channel_id=1, source_target_pairs={{0,8},{4,12},{8,0},{12,4},{16,24},{20,28},{24,16},{28,20},{1,9},{5... | collective-permute-start | bytes 393224 | tf_op jit(solution)/shard_map/ppermute | solution.py:789
  60.4 10.4 %collective-permute-start.17 = (f32[256,128]{1,0:T(8,128)S(1)}, f32[256,128]{1,0:T(8,128)S(1)}, u32[]{:S(2)}, u32[]{:S(2)}) collective-permute-start(f32[256,128]{1,0:T(8,128)S(1)} %get-tuple-element.63), channel_id=1, source_target_pairs={{0,12},{4,8},{8,4},{12,0},{16,28},{20,24},{24,20},{28,16},{1,13},{... | collective-permute-start | bytes 393224 | tf_op jit(solution)/shard_map/ppermute | solution.py:789
  60.4 14.7 %collective-permute-start.12 = (f32[256,128]{1,0:T(8,128)S(1)}, f32[256,128]{1,0:T(8,128)S(1)}, u32[]{:S(2)}, u32[]{:S(2)}) collective-permute-start(f32[256,128]{1,0:T(8,128)S(1)} %get-tuple-element.54), channel_id=1, source_target_pairs={{0,20},{4,16},{8,28},{12,24},{16,4},{20,0},{24,12},{28,8},{1,21},{... | collective-permute-start | bytes 393224 | tf_op jit(solution)/shard_map/ppermute | solution.py:789
  64.1 14.6 %collective-permute-start.18 = (f32[256,128]{1,0:T(8,128)S(1)}, f32[256,128]{1,0:T(8,128)S(1)}, u32[]{:S(2)}, u32[]{:S(2)}) collective-permute-start(f32[256,128]{1,0:T(8,128)S(1)} %get-tuple-element.66), channel_id=1, source_target_pairs={{0,24},{4,28},{8,16},{12,20},{16,8},{20,12},{24,0},{28,4},{1,25},{... | collective-permute-start | bytes 393224 | tf_op jit(solution)/shard_map/ppermute | solution.py:789
  64.7 17.0 %collective-permute-start.19 = (f32[256,128]{1,0:T(8,128)S(1)}, f32[256,128]{1,0:T(8,128)S(1)}, u32[]{:S(2)}, u32[]{:S(2)}) collective-permute-start(f32[256,128]{1,0:T(8,128)S(1)} %get-tuple-element.67), channel_id=1, source_target_pairs={{0,28},{4,24},{8,20},{12,16},{16,12},{20,8},{24,4},{28,0},{1,29},{... | collective-permute-start | bytes 393224 | tf_op jit(solution)/shard_map/ppermute | solution.py:789
  (3 other events, 2.4 us)

commit v3 on v2

--- a/solution.py
+++ b/solution.py
@@ -403,8 +403,15 @@
 
 
 def filter_kernel(count, width, group_ref, params, forward, *rest):
-    groups = len(rest) - 3
-    taps, (out, columns, spectrum) = rest[:groups], rest[groups:]
+    groups = len(rest) - 5
+    given, (out, columns, spectrum, taps, sems) = rest[:groups], rest[groups:]
+    loads = [
+        pltpu.make_async_copy(source, taps.at[k], sems.at[k]) for k, source in enumerate(given)
+    ]
+    for load in loads:
+        load.start()
+    for load in loads:
+        load.wait()
     length = out.shape[1] // 2
     halves = LANES // (count * width)
     group = group_ref[0]
@@ -414,8 +421,8 @@
             for turn in range(count * halves // groups):
                 at = (owner + turn * groups) // halves + (owner % halves) * count
                 for t in range(length // LANES):
-                    columns[p, aligned(at * width, width), tile_of(t)] = taps[k][
-                        p, t * width : (t + 1) * width, :
+                    columns[p, aligned(at * width, width), tile_of(t)] = taps[
+                        k, p, t * width : (t + 1) * width, :
                     ]
     for p in range(count):
         high, low = split16(columns[p])
@@ -443,24 +450,22 @@
     return pl.pallas_call(
         functools.partial(filter_kernel, count, width),
         out_shape=jax.ShapeDtypeStruct((count, 2 * length, LANES), jnp.float32),
-        in_specs=[in_smem()] + [in_vmem()] * (2 + len(taps)),
+        in_specs=[in_smem()] + [in_vmem()] * 2 + [in_any()] * len(taps),
         out_specs=in_vmem(),
         scratch_shapes=[
             pltpu.VMEM((count, LANES, length), jnp.float32),
             pltpu.VMEM((count, 2 * length, LANES), jnp.float32),
+            pltpu.VMEM((len(taps), *taps[0].shape), jnp.float32),
+            pltpu.SemaphoreType.DMA((len(taps),)),
         ],
         compiler_params=params_of(),
         name="filter_spectra",
     )(group, params, forward, *taps)
 
 
-def convolve_kernel(count, length, me_ref, params, forward, inverse, spectra, *rest):
-    messages, rest = by_partner(rest[:count]), rest[count:]
-    half = count // 2
-    (own_home, pair, odds), outs, rest = rest[:3], rest[3 : 3 + count], rest[3 + count :]
-    rims, bins, halves, result, query_rows = rest
+def gated_bins_kernel(count, length, me_ref, forward, *rest):
+    messages, (bins, rims, halves) = by_partner(rest[:count]), rest[count:]
     me = me_ref[0]
-    side = me // half
     rims[0] = jnp.zeros((ROWS, LANES), jnp.float32)
     for k in range(count):
         rims[(me ^ k) + 1] = messages[k][length : length + ROWS, :]
@@ -483,6 +488,31 @@
         bins[:, columns] = jnp.dot(
             forward[...], halves[0 : 3 * length, columns], preferred_element_type=jnp.float32
         )
+
+
+def gated_bins(me, forward, messages, count):
+    length = forward.shape[0] // 2
+    return pl.pallas_call(
+        functools.partial(gated_bins_kernel, count, length),
+        out_shape=[
+            jax.ShapeDtypeStruct((2 * length, count * LANES), jnp.float32),
+            jax.ShapeDtypeStruct((count + 1, ROWS, LANES), jnp.float32),
+        ],
+        in_specs=[in_smem()] + [in_vmem()] * (1 + count),
+        out_specs=[in_vmem()] * 2,
+        scratch_shapes=[pltpu.VMEM((3 * length, count * LANES), jnp.bfloat16)],
+        compiler_params=params_of(),
+        name="gated_bins",
+    )(me, forward, *far_first_operands(messages))
+
+
+def convolve_kernel(count, length, me_ref, inverse, spectra, bins, rims, *rest):
+    half = count // 2
+    (own_home, pair, odds), outs, rest = rest[:3], rest[3 : 3 + count], rest[3 + count :]
+    halves, result, query_rows = rest
+    me = me_ref[0]
+    side = me // half
+    block_rows = 2 * ROWS
 
     def block(i, _):
         start = pl.multiple_of(i * block_rows, block_rows)
@@ -545,23 +575,21 @@
                 outs[k][pl.ds(m * count + r, ROWS, stride=count), :] = values
 
 
-def convolve(me, params, forward, inverse, spectra, messages, homes, count):
+def convolve(me, inverse, spectra, bins, rims, homes, count):
     length = spectra.shape[1] // 2
     return pl.pallas_call(
         functools.partial(convolve_kernel, count, length),
         out_shape=[jax.ShapeDtypeStruct((length, LANES), jnp.float32)] * count,
-        in_specs=[in_smem()] + [in_vmem()] * (7 + count),
+        in_specs=[in_smem()] + [in_vmem()] * 7,
         out_specs=[in_vmem()] * count,
         scratch_shapes=[
-            pltpu.VMEM((count + 1, ROWS, LANES), jnp.float32),
-            pltpu.VMEM((2 * length, count * LANES), jnp.float32),
             pltpu.VMEM((6 * length, count * LANES), jnp.bfloat16),
             pltpu.VMEM((length, count * LANES), jnp.float32),
             pltpu.VMEM((count, length // 2, LANES), jnp.float32),
         ],
         compiler_params=params_of(),
         name="convolve",
-    )(me, params, forward, inverse, spectra, *far_first_operands(messages), *homes)
+    )(me, inverse, spectra, bins, rims, *homes)
 
 
 def share_sizes(count, tiles, part):
@@ -814,13 +842,14 @@
     gated[1] = odds
     gated = exchanged(gated, "seq")
     odds = gated[1]
-    pairs = pair_shares(evens[1:], next_home, odds, *gated[2:])
     taps = collect_taps(me, gated, count, width, length)
     taps = [taps] + [swapped(taps, "grp", k) for k in range(1, groups)]
+    pairs = pair_shares(evens[1:], next_home, odds, taps[1])
     pairs = [swapped(pair, "seq", 2 * i) for i, pair in enumerate(pairs, 1)]
     spectra = filter_spectra(group, params, forward, taps, count, width)
     homes = (own_home, pairs[0], odds)
-    convolved = list(convolve(me, params, forward, inverse, spectra, gated, homes, count))
+    bins, rims = gated_bins(me, forward, gated, count)
+    convolved = list(convolve(me, inverse, spectra, bins, rims, homes, count))
     convolved[1:half] = hold(convolved[1:half], *pairs)
     first = [swapped(convolved[k], "seq", k) for k in (half, half + 1)]
     convolved[half + 2 :] = hold(convolved[half + 2 :], *pairs, first[0])

time: 85 us -> 83.4 us (0.981)
  the two profiles are of different devices: /device:TPU:20 before, /device:TPU:0 now
where the time goes in v3:
time: 83.4 us; the launch traced here: 81.9 us
  starting transfers between devices  34.8 us (42%)
  waiting for transfers between devices  29.3 us (35%)
  Pallas kernels  16.6 us (20%)
  local copies, waits for them, and re-layouts  1 us (1%)
    ppermute x20, starting transfers between devices, swapped(): lax.ppermute(block, axis, [(i, i ^ k) for i in range(lax.axis_size(axis))])  34.8 us
    ppermute x20, waiting for transfers between devices, swapped(): lax.ppermute(block, axis, [(i, i ^ k) for i in range(lax.axis_size(axis))])  29.3 us
    pallas_call x1, Pallas kernels, gate(): pl.pallas_call(functools.partial(gate_kernel, count, width, pieces), out_...  4.06 us
    pallas_call x1, Pallas kernels, convolve(): pl.pallas_call(functools.partial(convolve_kernel, count, length), out_sha...  3.12 us
    pallas_call x1, Pallas kernels, finish(): pl.pallas_call(functools.partial(finish_kernel, count, width, pieces), ou...  3.02 us
    pallas_call x1, Pallas kernels, filter_spectra(): pl.pallas_call(functools.partial(filter_kernel, count, width), out_shape=...  3.02 us
  transfers between devices with their start and end apart: 20, of which 12 were waited for; matrix products, arithmetic and copies ran while one was open for 0% of the time, Pallas kernels for 9%

profile of v3, /device:TPU:0, one launch (start us, length us, event | category | flops | bytes accessed | tf_op | source)
XLA Modules:
  0.0 81.9 jit_solution(12767193698413895679)
XLA Ops:
  0.0 4.1 %gate.1 = (f32[280,128]{1,0:T(8,128)}, f32[280,128]{1,0:T(8,128)}, f32[280,128]{1,0:T(8,128)}, f32[280,128]{1,0:T(8,128)}, f32[280,128]{1,0:T(8,128)}, /*index=5...) custom-call(s32[1]{0:T(128)} %bitcast.me_ref, f32[3,256,1024]{2,1,0:T(8,128)} %streams.3, ...), custom_call_target="tpu_custom_call" | custom-call | tf_op jit(solution)/shard_map/gate/pallas_call | solution.py:366
  4.1 0.9 %copy-done.5 = f32[280,128]{1,0:T(8,128)S(1)} copy-done((f32[280,128]{1,0:T(8,128)S(1)}, f32[280,128]{1,0:T(8,128)}, u32[]{:S(2)}) %copy-start.5) | copy-done | bytes 143384
  5.1 1.0 %query.1 = (f32[272,128]{1,0:T(8,128)S(1)}, f32[272,128]{1,0:T(8,128)S(1)}, f32[136,128]{1,0:T(8,128)S(1)}, f32[136,128]{1,0:T(8,128)S(1)}, f32[128,128]{1,0:T(8...) custom-call(s32[1]{0:T(128)} %bitcast.me_ref, f32[3,256,1024]{2,1,0:T(8,128)S(1)} %copy-done, ...), custom_call_target="tpu_custom_call" | custom-call | tf_op jit(solution)/shard_map/query/pallas_call | solution.py:662
  6.1 3.0 %collective-permute-start.2 = (f32[1352,128]{1,0:T(8,128)S(1)}, f32[1352,128]{1,0:T(8,128)S(1)}, u32[]{:S(2)}, u32[]{:S(2)}) collective-permute-start(f32[1352,128]{1,0:T(8,128)S(1)} %get-tuple-element.44), channel_id=1, source_target_pairs={{0,4},{4,0},{8,12},{12,8},{16,20},{20,16},{24,28},{28,24},{1,5},{5... | collective-permute-start | bytes 2076680 | tf_op jit(solution)/shard_map/ppermute | solution.py:817
  9.1 2.6 %collective-permute-start = (f32[280,128]{1,0:T(8,128)S(1)}, f32[280,128]{1,0:T(8,128)S(1)}, u32[]{:S(2)}, u32[]{:S(2)}) collective-permute-start(f32[280,128]{1,0:T(8,128)S(1)} %copy-done.14), channel_id=1, source_target_pairs={{0,16},{4,20},{8,24},{12,28},{16,0},{20,4},{24,8},{28,12},{1,17},{... | collective-permute-start | bytes 430088 | tf_op jit(solution)/shard_map/ppermute | solution.py:817
  11.8 1.8 %collective-permute-start.3 = (f32[280,128]{1,0:T(8,128)S(1)}, f32[280,128]{1,0:T(8,128)S(1)}, u32[]{:S(2)}, u32[]{:S(2)}) collective-permute-start(f32[280,128]{1,0:T(8,128)S(1)} %copy-done.12), channel_id=1, source_target_pairs={{0,8},{4,12},{8,0},{12,4},{16,24},{20,28},{24,16},{28,20},{1,9},{5... | collective-permute-start | bytes 430088 | tf_op jit(solution)/shard_map/ppermute | solution.py:817
  13.6 1.4 %collective-permute-start.4 = (f32[280,128]{1,0:T(8,128)S(1)}, f32[280,128]{1,0:T(8,128)S(1)}, u32[]{:S(2)}, u32[]{:S(2)}) collective-permute-start(f32[280,128]{1,0:T(8,128)S(1)} %copy-done.11), channel_id=1, source_target_pairs={{0,12},{4,8},{8,4},{12,0},{16,28},{20,24},{24,20},{28,16},{1,13},{... | collective-permute-start | bytes 430088 | tf_op jit(solution)/shard_map/ppermute | solution.py:817
  15.0 7.7 %collective-permute-done.rest_0_ = f32[280,128]{1,0:T(8,128)S(1)} collective-permute-done((f32[280,128]{1,0:T(8,128)S(1)}, f32[280,128]{1,0:T(8,128)S(1)}, u32[]{:S(2)}, u32[]{:S(2)}) %collective-permute-start) | collective-permute-done | bytes 143392 | tf_op jit(solution)/shard_map/ppermute | solution.py:817
  22.6 2.4 %collective-permute-start.5 = (f32[280,128]{1,0:T(8,128)S(1)}, f32[280,128]{1,0:T(8,128)S(1)}, u32[]{:S(2)}, u32[]{:S(2)}) collective-permute-start(f32[280,128]{1,0:T(8,128)S(1)} %copy-done.10), channel_id=1, source_target_pairs={{0,24},{4,28},{8,16},{12,20},{16,8},{20,12},{24,0},{28,4},{1,25},{... | collective-permute-start | bytes 430088 | tf_op jit(solution)/shard_map/ppermute | solution.py:817
  25.1 4.0 %collective-permute-start.6 = (f32[280,128]{1,0:T(8,128)S(1)}, f32[280,128]{1,0:T(8,128)S(1)}, u32[]{:S(2)}, u32[]{:S(2)}) collective-permute-start(f32[280,128]{1,0:T(8,128)S(1)} %copy-done.9), channel_id=1, source_target_pairs={{0,28},{4,24},{8,20},{12,16},{16,12},{20,8},{24,4},{28,0},{1,29},{... | collective-permute-start | bytes 430088 | tf_op jit(solution)/shard_map/ppermute | solution.py:817
  29.1 1.1 %collective-permute-done.5.rest_6_ = f32[280,128]{1,0:T(8,128)S(1)} collective-permute-done((f32[280,128]{1,0:T(8,128)S(1)}, f32[280,128]{1,0:T(8,128)S(1)}, u32[]{:S(2)}, u32[]{:S(2)}) %collective-permute-start.5) | collective-permute-done | bytes 143392 | tf_op jit(solution)/shard_map/ppermute | solution.py:817
  30.2 3.0 %collective-permute-done.6.rest_7_ = f32[280,128]{1,0:T(8,128)S(1)} collective-permute-done((f32[280,128]{1,0:T(8,128)S(1)}, f32[280,128]{1,0:T(8,128)S(1)}, u32[]{:S(2)}, u32[]{:S(2)}) %collective-permute-start.6) | collective-permute-done | bytes 143392 | tf_op jit(solution)/shard_map/ppermute | solution.py:817
  34.0 1.2 %collective-permute-done.7.rest_1_.refs_5_ = f32[8,16,128]{2,1,0:T(8,128)S(1)} collective-permute-done((f32[8,16,128]{2,1,0:T(8,128)S(1)}, f32[8,16,128]{2,1,0:T(8,128)S(1)}, u32[]{:S(2)}, u32[]{:S(2)}) %collective-permute-start.7) | collective-permute-done | bytes 65568 | tf_op jit(solution)/shard_map/ppermute | solution.py:817
  35.2 0.9 %pair_shares.1 = (f32[800,128]{1,0:T(8,128)}, f32[272,128]{1,0:T(8,128)}, f32[272,128]{1,0:T(8,128)}) custom-call(f32[272,128]{1,0:T(8,128)S(1)} %get-tuple-element.52.refs_0_, f32[136,128]{1,0:T(8,128)S(1)} %get-tuple-element.53.refs_1_, f32[136,128]{1,0:T(8,128)S(1)} %get-tuple-element.54.refs_2_, f32[128,128]{1,0:T(8,128)S(1)} %get-tuple-element.55.refs_3_, ...), custom_call_target="tpu_custom_call" | custom-call | tf_op jit(solution)/shard_map/pair_shares/pallas_call | solution.py:712
  36.1 3.7 %collective-permute-start.10 = (f32[800,128]{1,0:T(8,128)}, f32[800,128]{1,0:T(8,128)S(1)}, u32[]{:S(2)}, u32[]{:S(2)}) collective-permute-start(f32[800,128]{1,0:T(8,128)} %get-tuple-element.56), channel_id=1, source_target_pairs={{0,8},{4,12},{8,0},{12,4},{16,24},{20,28},{24,16},{28,20},{1,9},{5... | collective-permute-start | bytes 1228808 | tf_op jit(solution)/shard_map/ppermute | solution.py:817
  39.8 1.9 %collective-permute-start.13 = (f32[272,128]{1,0:T(8,128)}, f32[272,128]{1,0:T(8,128)S(1)}, u32[]{:S(2)}, u32[]{:S(2)}) collective-permute-start(f32[272,128]{1,0:T(8,128)} %get-tuple-element.63), channel_id=1, source_target_pairs={{0,16},{4,20},{8,24},{12,28},{16,0},{20,4},{24,8},{28,12},{1,17},{... | collective-permute-start | bytes 417800 | tf_op jit(solution)/shard_map/ppermute | solution.py:817
  41.6 1.5 %collective-permute-start.14 = (f32[272,128]{1,0:T(8,128)}, f32[272,128]{1,0:T(8,128)S(1)}, u32[]{:S(2)}, u32[]{:S(2)}) collective-permute-start(f32[272,128]{1,0:T(8,128)} %get-tuple-element.64), channel_id=1, source_target_pairs={{0,24},{4,28},{8,16},{12,20},{16,8},{20,12},{24,0},{28,4},{1,25},{... | collective-permute-start | bytes 417800 | tf_op jit(solution)/shard_map/ppermute | solution.py:817
  44.7 1.5 %gated_bins.1 = (f32[512,1024]{1,0:T(8,128)S(1)}, f32[9,8,128]{2,1,0:T(8,128)S(1)}) custom-call(s32[1]{0:T(128)} %bitcast.me_ref, bf16[512,768]{1,0:T(8,128)(2,1)S(1)} %copy-done.1, f32[280,128]{1,0:T(8,128)S(1)} %collective-permute-done.rest_0_, f32[280,128]{1,0:T(8,128)S(1)} %collective-permute-done.1.rest_1_, f32[280,128]{1,0:T(8,128)S(1)} %copy-done.3, ...), custom_call_target="tpu_custom_call" | custom-call | tf_op jit(solution)/shard_map/gated_bins/pallas_call | solution.py:495
  46.1 1.4 %collective-permute-done.9.rest_3_ = f32[8,16,128]{2,1,0:T(8,128)} collective-permute-done((f32[8,16,128]{2,1,0:T(8,128)S(1)}, f32[8,16,128]{2,1,0:T(8,128)}, u32[]{:S(2)}, u32[]{:S(2)}) %collective-permute-start.9) | collective-permute-done | bytes 65568 | tf_op jit(solution)/shard_map/ppermute | solution.py:817
  47.5 1.5 %collective-permute-done.8.rest_2_ = f32[8,16,128]{2,1,0:T(8,128)} collective-permute-done((f32[8,16,128]{2,1,0:T(8,128)S(1)}, f32[8,16,128]{2,1,0:T(8,128)}, u32[]{:S(2)}, u32[]{:S(2)}) %collective-permute-start.8) | collective-permute-done | bytes 65568 | tf_op jit(solution)/shard_map/ppermute | solution.py:817
  49.0 3.0 %filter_spectra.1.spectra = f32[8,512,128]{2,1,0:T(8,128)S(1)} custom-call(s32[1]{0:T(128)} %bitcast.1.group_ref, f32[8,128]{1,0:T(8,128)S(1)} %copy-done.8, bf16[512,768]{1,0:T(8,128)(2,1)S(1)} %copy-done.1, f32[8,16,128]{2,1,0:T(8,128)S(1)} %collect_taps.1.rest_0_, f32[8,16,128]{2,1,0:T(8,128)S(1)} %collective-permute-done.7.rest_1_.refs_5_, ...), custom_call_target="tpu_custom_call" | custom-call | tf_op jit(solution)/shard_map/filter_spectra/pallas_call | solution.py:450
  52.7 3.1 %convolve.1 = (f32[256,128]{1,0:T(8,128)S(1)}, f32[256,128]{1,0:T(8,128)S(1)}, f32[256,128]{1,0:T(8,128)S(1)}, f32[256,128]{1,0:T(8,128)S(1)}, f32[256,128]{1,0:...) custom-call(s32[1]{0:T(128)} %bitcast.me_ref, ...), custom_call_target="tpu_custom_call" | custom-call | tf_op jit(solution)/shard_map/convolve/pallas_call | solution.py:580
  55.9 2.0 %collective-permute-start.11 = (f32[256,128]{1,0:T(8,128)S(1)}, f32[256,128]{1,0:T(8,128)S(1)}, u32[]{:S(2)}, u32[]{:S(2)}) collective-permute-start(f32[256,128]{1,0:T(8,128)S(1)} %get-tuple-element.57), channel_id=1, source_target_pairs={{0,16},{4,20},{8,24},{12,28},{16,0},{20,4},{24,8},{28,12},{1,17},{... | collective-permute-start | bytes 393224 | tf_op jit(solution)/shard_map/ppermute | solution.py:817
  57.9 0.9 %collective-permute-done.14.refs_5_.refs_4_.rest_12_ = f32[272,128]{1,0:T(8,128)S(1)} collective-permute-done((f32[272,128]{1,0:T(8,128)}, f32[272,128]{1,0:T(8,128)S(1)}, u32[]{:S(2)}, u32[]{:S(2)}) %collective-permute-start.14) | collective-permute-done | bytes 139296 | tf_op jit(solution)/shard_map/ppermute | solution.py:817
  58.8 1.5 %collective-permute-start.15 = (f32[256,128]{1,0:T(8,128)S(1)}, f32[256,128]{1,0:T(8,128)S(1)}, u32[]{:S(2)}, u32[]{:S(2)}) collective-permute-start(f32[256,128]{1,0:T(8,128)S(1)} %get-tuple-element.65), channel_id=1, source_target_pairs={{0,4},{4,0},{8,12},{12,8},{16,20},{20,16},{24,28},{28,24},{1,5},{5... | collective-permute-start | bytes 393224 | tf_op jit(solution)/shard_map/ppermute | solution.py:817
  60.3 1.8 %collective-permute-start.16 = (f32[256,128]{1,0:T(8,128)S(1)}, f32[256,128]{1,0:T(8,128)S(1)}, u32[]{:S(2)}, u32[]{:S(2)}) collective-permute-start(f32[256,128]{1,0:T(8,128)S(1)} %get-tuple-element.66), channel_id=1, source_target_pairs={{0,8},{4,12},{8,0},{12,4},{16,24},{20,28},{24,16},{28,20},{1,9},{5... | collective-permute-start | bytes 393224 | tf_op jit(solution)/shard_map/ppermute | solution.py:817
  63.1 1.7 %collective-permute-done.11.refs_5_.rest_0_ = f32[256,128]{1,0:T(8,128)S(1)} collective-permute-done((f32[256,128]{1,0:T(8,128)S(1)}, f32[256,128]{1,0:T(8,128)S(1)}, u32[]{:S(2)}, u32[]{:S(2)}) %collective-permute-start.11) | collective-permute-done | bytes 131104 | tf_op jit(solution)/shard_map/ppermute | solution.py:817
  64.8 2.8 %collective-permute-start.18 = (f32[256,128]{1,0:T(8,128)S(1)}, f32[256,128]{1,0:T(8,128)S(1)}, u32[]{:S(2)}, u32[]{:S(2)}) collective-permute-start(f32[256,128]{1,0:T(8,128)S(1)} %get-tuple-element.70), channel_id=1, source_target_pairs={{0,24},{4,28},{8,16},{12,20},{16,8},{20,12},{24,0},{28,4},{1,25},{... | collective-permute-start | bytes 393224 | tf_op jit(solution)/shard_map/ppermute | solution.py:817
  67.6 1.7 %collective-permute-start.19 = (f32[256,128]{1,0:T(8,128)S(1)}, f32[256,128]{1,0:T(8,128)S(1)}, u32[]{:S(2)}, u32[]{:S(2)}) collective-permute-start(f32[256,128]{1,0:T(8,128)S(1)} %get-tuple-element.71), channel_id=1, source_target_pairs={{0,28},{4,24},{8,20},{12,16},{16,12},{20,8},{24,4},{28,0},{1,29},{... | collective-permute-start | bytes 393224 | tf_op jit(solution)/shard_map/ppermute | solution.py:817
  69.3 2.6 %collective-permute-done.17.rest_5_ = f32[256,128]{1,0:T(8,128)S(1)} collective-permute-done((f32[256,128]{1,0:T(8,128)S(1)}, f32[256,128]{1,0:T(8,128)S(1)}, u32[]{:S(2)}, u32[]{:S(2)}) %collective-permute-start.17) | collective-permute-done | bytes 131104 | tf_op jit(solution)/shard_map/ppermute | solution.py:817
  71.9 6.9 %collective-permute-done.12.rest_1_ = f32[256,128]{1,0:T(8,128)S(1)} collective-permute-done((f32[256,128]{1,0:T(8,128)S(1)}, f32[256,128]{1,0:T(8,128)S(1)}, u32[]{:S(2)}, u32[]{:S(2)}) %collective-permute-start.12) | collective-permute-done | bytes 131104 | tf_op jit(solution)/shard_map/ppermute | solution.py:817
  78.8 3.0 %finish.1 = f32[32,8,1024]{2,1,0:T(8,128)} custom-call(s32[1]{0:T(128)} %bitcast.me_ref, f32[256,128]{1,0:T(8,128)S(1)} %collective-permute-done.11.refs_5_.rest_0_, f32[256,128]{1,0:T(8,128)S(1)} %collective-permute-done.12.rest_1_, f32[256,128]{1,0:T(8,128)S(1)} %get-tuple-element.59.rest_2_, f32[256,128]{1,0:T(8,128)S(1)} %collective-permute-done.15.rest_3_, ...), custom_call_target="tpu_custom_call" | custom-call | tf_op jit(solution)/shard_map/finish/pallas_call | solution.py:800
  (48 shorter events, 4.1 us)
Async XLA Ops:
  0.0 4.1 %copy-start = (f32[3,256,1024]{2,1,0:T(8,128)S(1)}, f32[3,256,1024]{2,1,0:T(8,128)}, u32[]{:S(2)}) copy-start(f32[3,256,1024]{2,1,0:T(8,128)} %streams.3) | copy-start | bytes 9437188
  4.1 29.8 %copy-start.3 = (f32[280,128]{1,0:T(8,128)S(1)}, f32[280,128]{1,0:T(8,128)}, u32[]{:S(2)}) copy-start(f32[280,128]{1,0:T(8,128)} %get-tuple-element.42.rest_2_) | copy-start | bytes 430084
  5.1 6.7 %copy-start.13 = (f32[280,128]{1,0:T(8,128)S(1)}, f32[280,128]{1,0:T(8,128)}, u32[]{:S(2)}) copy-start(f32[280,128]{1,0:T(8,128)} %get-tuple-element.41) | copy-start | bytes 430084
  5.1 6.7 %copy-start.12 = (f32[280,128]{1,0:T(8,128)S(1)}, f32[280,128]{1,0:T(8,128)}, u32[]{:S(2)}) copy-start(f32[280,128]{1,0:T(8,128)} %get-tuple-element.45) | copy-start | bytes 430084
  5.1 8.5 %copy-start.11 = (f32[280,128]{1,0:T(8,128)S(1)}, f32[280,128]{1,0:T(8,128)}, u32[]{:S(2)}) copy-start(f32[280,128]{1,0:T(8,128)} %get-tuple-element.46) | copy-start | bytes 430084
  5.1 17.6 %copy-start.10 = (f32[280,128]{1,0:T(8,128)S(1)}, f32[280,128]{1,0:T(8,128)}, u32[]{:S(2)}) copy-start(f32[280,128]{1,0:T(8,128)} %get-tuple-element.47) | copy-start | bytes 430084
  5.1 20.0 %copy-start.9 = (f32[280,128]{1,0:T(8,128)S(1)}, f32[280,128]{1,0:T(8,128)}, u32[]{:S(2)}) copy-start(f32[280,128]{1,0:T(8,128)} %get-tuple-element.48) | copy-start | bytes 430084
  6.1 29.1 %copy-start.6 = (f32[128,128]{1,0:T(8,128)}, f32[128,128]{1,0:T(8,128)S(1)}, u32[]{:S(2)}) copy-start(f32[128,128]{1,0:T(8,128)S(1)} %get-tuple-element.51.rest_0_) | copy-start | bytes 196612
  6.1 38.6 %copy-start.1 = (bf16[512,768]{1,0:T(8,128)(2,1)S(1)}, bf16[512,768]{1,0:T(8,128)(2,1)}, u32[]{:S(2)}) copy-start(bf16[512,768]{1,0:T(8,128)(2,1)} %constant.13.clone.forward) | copy-start | bytes 2359300
  6.1 27.7 %collective-permute-start.2 = (f32[1352,128]{1,0:T(8,128)S(1)}, f32[1352,128]{1,0:T(8,128)S(1)}, u32[]{:S(2)}, u32[]{:S(2)}) collective-permute-start(f32[1352,128]{1,0:T(8,128)S(1)} %get-tuple-element.44), channel_id=1, source_target_pairs={{0,4},{4,0},{8,12},{12,8},{16,20},{20,16},{24,28},{28,24},{1,5},{5... | collective-permute-start | bytes 2076680 | tf_op jit(solution)/shard_map/ppermute | solution.py:817
  9.1 13.5 %collective-permute-start = (f32[280,128]{1,0:T(8,128)S(1)}, f32[280,128]{1,0:T(8,128)S(1)}, u32[]{:S(2)}, u32[]{:S(2)}) collective-permute-start(f32[280,128]{1,0:T(8,128)S(1)} %copy-done.14), channel_id=1, source_target_pairs={{0,16},{4,20},{8,24},{12,28},{16,0},{20,4},{24,8},{28,12},{1,17},{... | collective-permute-start | bytes 430088 | tf_op jit(solution)/shard_map/ppermute | solution.py:817
  11.7 13.4 %collective-permute-start.1 = (f32[280,128]{1,0:T(8,128)S(1)}, f32[280,128]{1,0:T(8,128)S(1)}, u32[]{:S(2)}, u32[]{:S(2)}) collective-permute-start(f32[280,128]{1,0:T(8,128)S(1)} %copy-done.13), channel_id=1, source_target_pairs={{0,20},{4,16},{8,28},{12,24},{16,4},{20,0},{24,12},{28,8},{1,21},{... | collective-permute-start | bytes 430088 | tf_op jit(solution)/shard_map/ppermute | solution.py:817
  11.8 17.3 %collective-permute-start.3 = (f32[280,128]{1,0:T(8,128)S(1)}, f32[280,128]{1,0:T(8,128)S(1)}, u32[]{:S(2)}, u32[]{:S(2)}) collective-permute-start(f32[280,128]{1,0:T(8,128)S(1)} %copy-done.12), channel_id=1, source_target_pairs={{0,8},{4,12},{8,0},{12,4},{16,24},{20,28},{24,16},{28,20},{1,9},{5... | collective-permute-start | bytes 430088 | tf_op jit(solution)/shard_map/ppermute | solution.py:817
  13.6 15.5 %collective-permute-start.4 = (f32[280,128]{1,0:T(8,128)S(1)}, f32[280,128]{1,0:T(8,128)S(1)}, u32[]{:S(2)}, u32[]{:S(2)}) collective-permute-start(f32[280,128]{1,0:T(8,128)S(1)} %copy-done.11), channel_id=1, source_target_pairs={{0,12},{4,8},{8,4},{12,0},{16,28},{20,24},{24,20},{28,16},{1,13},{... | collective-permute-start | bytes 430088 | tf_op jit(solution)/shard_map/ppermute | solution.py:817
  22.6 7.6 %collective-permute-start.5 = (f32[280,128]{1,0:T(8,128)S(1)}, f32[280,128]{1,0:T(8,128)S(1)}, u32[]{:S(2)}, u32[]{:S(2)}) collective-permute-start(f32[280,128]{1,0:T(8,128)S(1)} %copy-done.10), channel_id=1, source_target_pairs={{0,24},{4,28},{8,16},{12,20},{16,8},{20,12},{24,0},{28,4},{1,25},{... | collective-permute-start | bytes 430088 | tf_op jit(solution)/shard_map/ppermute | solution.py:817
  25.1 8.1 %collective-permute-start.6 = (f32[280,128]{1,0:T(8,128)S(1)}, f32[280,128]{1,0:T(8,128)S(1)}, u32[]{:S(2)}, u32[]{:S(2)}) collective-permute-start(f32[280,128]{1,0:T(8,128)S(1)} %copy-done.9), channel_id=1, source_target_pairs={{0,28},{4,24},{8,20},{12,16},{16,12},{20,8},{24,4},{28,0},{1,29},{... | collective-permute-start | bytes 430088 | tf_op jit(solution)/shard_map/ppermute | solution.py:817
  33.9 15.1 %copy-start.8 = (f32[8,128]{1,0:T(8,128)S(1)}, f32[8,128]{1,0:T(8,128)}, u32[]{:S(2)}) copy-start(f32[8,128]{1,0:T(8,128)} %get-tuple-element.39.params) | copy-start | bytes 12292
  33.9 1.3 %collective-permute-start.7 = (f32[8,16,128]{2,1,0:T(8,128)S(1)}, f32[8,16,128]{2,1,0:T(8,128)S(1)}, u32[]{:S(2)}, u32[]{:S(2)}) collective-permute-start(f32[8,16,128]{2,1,0:T(8,128)S(1)} %collect_taps.1.rest_0_), channel_id=1, source_target_pairs={{0,1},{1,0},{2,3},{3,2},{4,5},{5,4},{6,7},{7,6},{8,9},{9,8},{10,11... | collective-permute-start | bytes 196616 | tf_op jit(solution)/shard_map/ppermute | solution.py:817
  36.1 16.6 %collective-permute-start.10 = (f32[800,128]{1,0:T(8,128)}, f32[800,128]{1,0:T(8,128)S(1)}, u32[]{:S(2)}, u32[]{:S(2)}) collective-permute-start(f32[800,128]{1,0:T(8,128)} %get-tuple-element.56), channel_id=1, source_target_pairs={{0,8},{4,12},{8,0},{12,4},{16,24},{20,28},{24,16},{28,20},{1,9},{5... | collective-permute-start | bytes 1228808 | tf_op jit(solution)/shard_map/ppermute | solution.py:817
  39.8 18.2 %collective-permute-start.13 = (f32[272,128]{1,0:T(8,128)}, f32[272,128]{1,0:T(8,128)S(1)}, u32[]{:S(2)}, u32[]{:S(2)}) collective-permute-start(f32[272,128]{1,0:T(8,128)} %get-tuple-element.63), channel_id=1, source_target_pairs={{0,16},{4,20},{8,24},{12,28},{16,0},{20,4},{24,8},{28,12},{1,17},{... | collective-permute-start | bytes 417800 | tf_op jit(solution)/shard_map/ppermute | solution.py:817
  41.6 17.1 %collective-permute-start.14 = (f32[272,128]{1,0:T(8,128)}, f32[272,128]{1,0:T(8,128)S(1)}, u32[]{:S(2)}, u32[]{:S(2)}) collective-permute-start(f32[272,128]{1,0:T(8,128)} %get-tuple-element.64), channel_id=1, source_target_pairs={{0,24},{4,28},{8,16},{12,20},{16,8},{20,12},{24,0},{28,4},{1,25},{... | collective-permute-start | bytes 417800 | tf_op jit(solution)/shard_map/ppermute | solution.py:817
  43.1 4.4 %collective-permute-start.9 = (f32[8,16,128]{2,1,0:T(8,128)S(1)}, f32[8,16,128]{2,1,0:T(8,128)}, u32[]{:S(2)}, u32[]{:S(2)}) collective-permute-start(f32[8,16,128]{2,1,0:T(8,128)S(1)} %collect_taps.1.rest_0_), channel_id=1, source_target_pairs={{0,3},{1,2},{2,1},{3,0},{4,7},{5,6},{6,5},{7,4},{8,11},{9,10},{10,... | collective-permute-start | bytes 196616 | tf_op jit(solution)/shard_map/ppermute | solution.py:817
  43.8 5.2 %collective-permute-start.8 = (f32[8,16,128]{2,1,0:T(8,128)S(1)}, f32[8,16,128]{2,1,0:T(8,128)}, u32[]{:S(2)}, u32[]{:S(2)}) collective-permute-start(f32[8,16,128]{2,1,0:T(8,128)S(1)} %collect_taps.1.rest_0_), channel_id=1, source_target_pairs={{0,2},{1,3},{2,0},{3,1},{4,6},{5,7},{6,4},{7,5},{8,10},{9,11},{10,... | collective-permute-start | bytes 196616 | tf_op jit(solution)/shard_map/ppermute | solution.py:817
  46.1 6.6 %copy-start.2 = (bf16[256,1536]{1,0:T(8,128)(2,1)S(1)}, bf16[256,1536]{1,0:T(8,128)(2,1)}, u32[]{:S(2)}) copy-start(bf16[256,1536]{1,0:T(8,128)(2,1)} %constant.14.clone.inverse) | copy-start | bytes 2359300
  46.1 6.6 %copy-start.7 = (f32[128,128]{1,0:T(8,128)S(1)}, f32[128,128]{1,0:T(8,128)}, u32[]{:S(2)}) copy-start(f32[128,128]{1,0:T(8,128)} %copy-done.6) | copy-start | bytes 196612
  55.9 8.9 %collective-permute-start.11 = (f32[256,128]{1,0:T(8,128)S(1)}, f32[256,128]{1,0:T(8,128)S(1)}, u32[]{:S(2)}, u32[]{:S(2)}) collective-permute-start(f32[256,128]{1,0:T(8,128)S(1)} %get-tuple-element.57), channel_id=1, source_target_pairs={{0,16},{4,20},{8,24},{12,28},{16,0},{20,4},{24,8},{28,12},{1,17},{... | collective-permute-start | bytes 393224 | tf_op jit(solution)/shard_map/ppermute | solution.py:817
  58.8 8.8 %collective-permute-start.15 = (f32[256,128]{1,0:T(8,128)S(1)}, f32[256,128]{1,0:T(8,128)S(1)}, u32[]{:S(2)}, u32[]{:S(2)}) collective-permute-start(f32[256,128]{1,0:T(8,128)S(1)} %get-tuple-element.65), channel_id=1, source_target_pairs={{0,4},{4,0},{8,12},{12,8},{16,20},{20,16},{24,28},{28,24},{1,5},{5... | collective-permute-start | bytes 393224 | tf_op jit(solution)/shard_map/ppermute | solution.py:817
  60.3 9.1 %collective-permute-start.16 = (f32[256,128]{1,0:T(8,128)S(1)}, f32[256,128]{1,0:T(8,128)S(1)}, u32[]{:S(2)}, u32[]{:S(2)}) collective-permute-start(f32[256,128]{1,0:T(8,128)S(1)} %get-tuple-element.66), channel_id=1, source_target_pairs={{0,8},{4,12},{8,0},{12,4},{16,24},{20,28},{24,16},{28,20},{1,9},{5... | collective-permute-start | bytes 393224 | tf_op jit(solution)/shard_map/ppermute | solution.py:817
  62.1 9.8 %collective-permute-start.17 = (f32[256,128]{1,0:T(8,128)S(1)}, f32[256,128]{1,0:T(8,128)S(1)}, u32[]{:S(2)}, u32[]{:S(2)}) collective-permute-start(f32[256,128]{1,0:T(8,128)S(1)} %get-tuple-element.67), channel_id=1, source_target_pairs={{0,12},{4,8},{8,4},{12,0},{16,28},{20,24},{24,20},{28,16},{1,13},{... | collective-permute-start | bytes 393224 | tf_op jit(solution)/shard_map/ppermute | solution.py:817
  62.3 16.5 %collective-permute-start.12 = (f32[256,128]{1,0:T(8,128)S(1)}, f32[256,128]{1,0:T(8,128)S(1)}, u32[]{:S(2)}, u32[]{:S(2)}) collective-permute-start(f32[256,128]{1,0:T(8,128)S(1)} %get-tuple-element.58), channel_id=1, source_target_pairs={{0,20},{4,16},{8,28},{12,24},{16,4},{20,0},{24,12},{28,8},{1,21},{... | collective-permute-start | bytes 393224 | tf_op jit(solution)/shard_map/ppermute | solution.py:817
  64.8 14.0 %collective-permute-start.18 = (f32[256,128]{1,0:T(8,128)S(1)}, f32[256,128]{1,0:T(8,128)S(1)}, u32[]{:S(2)}, u32[]{:S(2)}) collective-permute-start(f32[256,128]{1,0:T(8,128)S(1)} %get-tuple-element.70), channel_id=1, source_target_pairs={{0,24},{4,28},{8,16},{12,20},{16,8},{20,12},{24,0},{28,4},{1,25},{... | collective-permute-start | bytes 393224 | tf_op jit(solution)/shard_map/ppermute | solution.py:817
  67.6 11.2 %collective-permute-start.19 = (f32[256,128]{1,0:T(8,128)S(1)}, f32[256,128]{1,0:T(8,128)S(1)}, u32[]{:S(2)}, u32[]{:S(2)}) collective-permute-start(f32[256,128]{1,0:T(8,128)S(1)} %get-tuple-element.71), channel_id=1, source_target_pairs={{0,28},{4,24},{8,20},{12,16},{16,12},{20,8},{24,4},{28,0},{1,29},{... | collective-permute-start | bytes 393224 | tf_op jit(solution)/shard_map/ppermute | solution.py:817
  (3 other events, 9.1 us)

commit v4 on v3

--- a/solution.py
+++ b/solution.py
@@ -424,12 +424,14 @@
                     columns[p, aligned(at * width, width), tile_of(t)] = taps[
                         k, p, t * width : (t + 1) * width, :
                     ]
-    for p in range(count):
-        high, low = split16(columns[p])
+    for p in range(0, count, 2):
+        high, low = split16(columns[p : p + 2].reshape(2 * LANES, length))
         stacked = jnp.concatenate([high, low, high], axis=1)
-        spectrum[p] = lax.dot_general(
+        both = lax.dot_general(
             forward[...], stacked, (((1,), (1,)), ((), ())), preferred_element_type=jnp.float32
         )
+        spectrum[p] = both[:, 0:LANES]
+        spectrum[p + 1] = both[:, LANES : 2 * LANES]
     parity = lax.broadcasted_iota(jnp.int32, (length, LANES), 0) % 2
     sign = 1.0 - 2.0 * parity.astype(jnp.float32)
     skip = params[6:7, :]
@@ -755,21 +757,35 @@
             out[t, at, :] += first * lacking[t, 2 * m * count : (2 * m + 1) * count, :]
 
 
-def finish_kernel(count, width, pieces, me_ref, *rest):
-    messages, rest = by_partner(rest[:count]), rest[count:]
-    half = count // 2
-    own, odds, *pairs = rest[: half + 1]
-    out, rows, query_rows, lacking, sems = rest[half + 1 :]
-    me = me_ref[0]
-    part = out.shape[0]
-    length = part * count
-    sizes = share_sizes(count, query_rows.shape[0], part)
+def arrange_kernel(count, width, me_ref, *rest):
+    (own, odds, *pairs), (out, lacking) = rest[: count // 2 + 1], rest[count // 2 + 1 :]
+    tiles, length = out.shape[:2]
+    sizes = share_sizes(count, tiles, length // count)
     start = odds.shape[0] - length - sum(sizes[1::2])
     shares = [own, odds.at[pl.ds(start, sizes[1])]]
     for i, pair in enumerate(pairs, 1):
         size = sizes[2 * i]
         shares += [pair.at[pl.ds(0, size)], pair.at[pl.ds(size, size)]]
-    arrange_query(count, width, me, shares, query_rows, lacking)
+    arrange_query(count, width, me_ref[0], shares, out, lacking)
+
+
+def arrange(me, shares, rows, tiles, count, width):
+    return pl.pallas_call(
+        functools.partial(arrange_kernel, count, width),
+        out_shape=jax.ShapeDtypeStruct((tiles, rows, LANES), jnp.float32),
+        in_specs=[in_smem()] + [in_vmem()] * len(shares),
+        out_specs=in_vmem(),
+        scratch_shapes=[pltpu.VMEM((tiles, 4 * count, LANES), jnp.float32)],
+        compiler_params=params_of(),
+        name="arrange",
+    )(me, *shares)
+
+
+def finish_kernel(count, width, pieces, me_ref, *rest):
+    messages, rest = by_partner(rest[:count]), rest[count:]
+    query_rows, out, rows, sems = rest
+    me = me_ref[0]
+    part = out.shape[0]
     step = 4
     stores = []
 
@@ -794,23 +810,22 @@
         store.wait()
 
 
-def finish(me, messages, shares, rows, tiles, count, width):
+def finish(me, messages, query_rows, count, width):
+    tiles, rows = query_rows.shape[:2]
     part = rows // count
-    pieces = 4
+    pieces = 8
     return pl.pallas_call(
         functools.partial(finish_kernel, count, width, pieces),
         out_shape=jax.ShapeDtypeStruct((part, count, tiles * LANES), jnp.float32),
-        in_specs=[in_smem()] + [in_vmem()] * (count + len(shares)),
+        in_specs=[in_smem()] + [in_vmem()] * (count + 1),
         out_specs=in_any(),
         scratch_shapes=[
             pltpu.VMEM((part, count, tiles * LANES), jnp.float32),
-            pltpu.VMEM((tiles, rows, LANES), jnp.float32),
-            pltpu.VMEM((tiles, 4 * count, LANES), jnp.float32),
             pltpu.SemaphoreType.DMA((pieces,)),
         ],
         compiler_params=params_of(),
         name="finish",
-    )(me, *far_first_operands(messages), *shares)
+    )(me, *far_first_operands(messages), query_rows)
 
 
 def swapped(block, axis, k):
@@ -856,8 +871,8 @@
     convolved = exchanged(convolved[:half], "seq") + first + [
         swapped(convolved[k], "seq", k) for k in range(half + 2, count)
     ]
-    shares = [evens[0], odds, *pairs]
-    return finish(me, convolved, shares, length, tiles, count, width)
+    query_rows = arrange(me, [evens[0], odds, *pairs], length, tiles, count, width)
+    return finish(me, convolved, query_rows, count, width)
 
 
 def body(streams, short_filters, skip_gain, long_filter):

time: 83.4 us -> 82.6 us (level); the launches traced: 81.9 us -> 82.4 us
  waiting for transfers between devices: 29.3 us -> 31.3 us
  Pallas kernels: 16.6 us -> 15.4 us
    ppermute x20, waiting for transfers between devices: 29.3 us -> 31.3 us  [swapped(): lax.ppermute(block, axis, [(i, i ^ k) for i in range(lax.axis_size(axis))])]
    pallas_call x1, Pallas kernels: 3.02 us -> 2.18 us  [finish(): pl.pallas_call(functools.partial(finish_kernel, count, width, pieces), ou...]
  transfers between devices with their start and end apart: 20 -> 20, of which waited for: 12 -> 10; matrix products, arithmetic and copies ran while one was open for 0% -> 0% of each run, Pallas kernels for 9% -> 9%
where the time goes in v4:
time: 82.6 us; the launch traced here: 82.4 us
  starting transfers between devices  34.5 us (42%)
  waiting for transfers between devices  31.3 us (38%)
  Pallas kernels  15.4 us (19%)
  local copies, waits for them, and re-layouts  1 us (1%)
    ppermute x20, starting transfers between devices, swapped(): lax.ppermute(block, axis, [(i, i ^ k) for i in range(lax.axis_size(axis))])  34.5 us
    ppermute x20, waiting for transfers between devices, swapped(): lax.ppermute(block, axis, [(i, i ^ k) for i in range(lax.axis_size(axis))])  31.3 us
    pallas_call x1, Pallas kernels, gate(): pl.pallas_call(functools.partial(gate_kernel, count, width, pieces), out_...  4.06 us
    pallas_call x1, Pallas kernels, convolve(): pl.pallas_call(functools.partial(convolve_kernel, count, length), out_sha...  3.12 us
    pallas_call x1, Pallas kernels, filter_spectra(): pl.pallas_call(functools.partial(filter_kernel, count, width), out_shape=...  2.32 us
    pallas_call x1, Pallas kernels, finish(): pl.pallas_call(functools.partial(finish_kernel, count, width, pieces), ou...  2.18 us
  transfers between devices with their start and end apart: 20, of which 10 were waited for; matrix products, arithmetic and copies ran while one was open for 0% of the time, Pallas kernels for 9%

profile of v4, /device:TPU:0, one launch (start us, length us, event | category | flops | bytes accessed | tf_op | source)
XLA Modules:
  0.0 82.4 jit_solution(3594542394980513470)
XLA Ops:
  0.0 4.1 %gate.1 = (f32[280,128]{1,0:T(8,128)}, f32[280,128]{1,0:T(8,128)}, f32[280,128]{1,0:T(8,128)}, f32[280,128]{1,0:T(8,128)}, f32[280,128]{1,0:T(8,128)}, /*index=5...) custom-call(s32[1]{0:T(128)} %bitcast.me_ref, f32[3,256,1024]{2,1,0:T(8,128)} %streams.3, ...), custom_call_target="tpu_custom_call" | custom-call | tf_op jit(solution)/shard_map/gate/pallas_call | solution.py:366
  4.1 0.9 %copy-done.5 = f32[280,128]{1,0:T(8,128)S(1)} copy-done((f32[280,128]{1,0:T(8,128)S(1)}, f32[280,128]{1,0:T(8,128)}, u32[]{:S(2)}) %copy-start.5) | copy-done | bytes 143384
  5.1 1.0 %query.1 = (f32[272,128]{1,0:T(8,128)S(1)}, f32[272,128]{1,0:T(8,128)S(1)}, f32[136,128]{1,0:T(8,128)S(1)}, f32[136,128]{1,0:T(8,128)S(1)}, f32[128,128]{1,0:T(8...) custom-call(s32[1]{0:T(128)} %bitcast.me_ref, f32[3,256,1024]{2,1,0:T(8,128)S(1)} %copy-done, ...), custom_call_target="tpu_custom_call" | custom-call | tf_op jit(solution)/shard_map/query/pallas_call | solution.py:664
  6.1 3.0 %collective-permute-start.2 = (f32[1352,128]{1,0:T(8,128)S(1)}, f32[1352,128]{1,0:T(8,128)S(1)}, u32[]{:S(2)}, u32[]{:S(2)}) collective-permute-start(f32[1352,128]{1,0:T(8,128)S(1)} %get-tuple-element.44), channel_id=1, source_target_pairs={{0,4},{4,0},{8,12},{12,8},{16,20},{20,16},{24,28},{28,24},{1,5},{5... | collective-permute-start | bytes 2076680 | tf_op jit(solution)/shard_map/ppermute | solution.py:832
  9.1 2.6 %collective-permute-start = (f32[280,128]{1,0:T(8,128)S(1)}, f32[280,128]{1,0:T(8,128)S(1)}, u32[]{:S(2)}, u32[]{:S(2)}) collective-permute-start(f32[280,128]{1,0:T(8,128)S(1)} %copy-done.14), channel_id=1, source_target_pairs={{0,16},{4,20},{8,24},{12,28},{16,0},{20,4},{24,8},{28,12},{1,17},{... | collective-permute-start | bytes 430088 | tf_op jit(solution)/shard_map/ppermute | solution.py:832
  11.8 1.8 %collective-permute-start.3 = (f32[280,128]{1,0:T(8,128)S(1)}, f32[280,128]{1,0:T(8,128)S(1)}, u32[]{:S(2)}, u32[]{:S(2)}) collective-permute-start(f32[280,128]{1,0:T(8,128)S(1)} %copy-done.12), channel_id=1, source_target_pairs={{0,8},{4,12},{8,0},{12,4},{16,24},{20,28},{24,16},{28,20},{1,9},{5... | collective-permute-start | bytes 430088 | tf_op jit(solution)/shard_map/ppermute | solution.py:832
  13.6 1.4 %collective-permute-start.4 = (f32[280,128]{1,0:T(8,128)S(1)}, f32[280,128]{1,0:T(8,128)S(1)}, u32[]{:S(2)}, u32[]{:S(2)}) collective-permute-start(f32[280,128]{1,0:T(8,128)S(1)} %copy-done.11), channel_id=1, source_target_pairs={{0,12},{4,8},{8,4},{12,0},{16,28},{20,24},{24,20},{28,16},{1,13},{... | collective-permute-start | bytes 430088 | tf_op jit(solution)/shard_map/ppermute | solution.py:832
  15.0 7.7 %collective-permute-done.rest_0_ = f32[280,128]{1,0:T(8,128)S(1)} collective-permute-done((f32[280,128]{1,0:T(8,128)S(1)}, f32[280,128]{1,0:T(8,128)S(1)}, u32[]{:S(2)}, u32[]{:S(2)}) %collective-permute-start) | collective-permute-done | bytes 143392 | tf_op jit(solution)/shard_map/ppermute | solution.py:832
  22.6 2.4 %collective-permute-start.5 = (f32[280,128]{1,0:T(8,128)S(1)}, f32[280,128]{1,0:T(8,128)S(1)}, u32[]{:S(2)}, u32[]{:S(2)}) collective-permute-start(f32[280,128]{1,0:T(8,128)S(1)} %copy-done.10), channel_id=1, source_target_pairs={{0,24},{4,28},{8,16},{12,20},{16,8},{20,12},{24,0},{28,4},{1,25},{... | collective-permute-start | bytes 430088 | tf_op jit(solution)/shard_map/ppermute | solution.py:832
  25.1 4.0 %collective-permute-start.6 = (f32[280,128]{1,0:T(8,128)S(1)}, f32[280,128]{1,0:T(8,128)S(1)}, u32[]{:S(2)}, u32[]{:S(2)}) collective-permute-start(f32[280,128]{1,0:T(8,128)S(1)} %copy-done.9), channel_id=1, source_target_pairs={{0,28},{4,24},{8,20},{12,16},{16,12},{20,8},{24,4},{28,0},{1,29},{... | collective-permute-start | bytes 430088 | tf_op jit(solution)/shard_map/ppermute | solution.py:832
  29.1 1.1 %collective-permute-done.5.rest_6_ = f32[280,128]{1,0:T(8,128)S(1)} collective-permute-done((f32[280,128]{1,0:T(8,128)S(1)}, f32[280,128]{1,0:T(8,128)S(1)}, u32[]{:S(2)}, u32[]{:S(2)}) %collective-permute-start.5) | collective-permute-done | bytes 143392 | tf_op jit(solution)/shard_map/ppermute | solution.py:832
  30.2 3.0 %collective-permute-done.6.rest_7_ = f32[280,128]{1,0:T(8,128)S(1)} collective-permute-done((f32[280,128]{1,0:T(8,128)S(1)}, f32[280,128]{1,0:T(8,128)S(1)}, u32[]{:S(2)}, u32[]{:S(2)}) %collective-permute-start.6) | collective-permute-done | bytes 143392 | tf_op jit(solution)/shard_map/ppermute | solution.py:832
  34.0 1.2 %collective-permute-done.7.rest_1_.refs_5_ = f32[8,16,128]{2,1,0:T(8,128)S(1)} collective-permute-done((f32[8,16,128]{2,1,0:T(8,128)S(1)}, f32[8,16,128]{2,1,0:T(8,128)S(1)}, u32[]{:S(2)}, u32[]{:S(2)}) %collective-permute-start.7) | collective-permute-done | bytes 65568 | tf_op jit(solution)/shard_map/ppermute | solution.py:832
  36.1 3.7 %collective-permute-start.10 = (f32[800,128]{1,0:T(8,128)}, f32[800,128]{1,0:T(8,128)S(1)}, u32[]{:S(2)}, u32[]{:S(2)}) collective-permute-start(f32[800,128]{1,0:T(8,128)} %get-tuple-element.56), channel_id=1, source_target_pairs={{0,8},{4,12},{8,0},{12,4},{16,24},{20,28},{24,16},{28,20},{1,9},{5... | collective-permute-start | bytes 1228808 | tf_op jit(solution)/shard_map/ppermute | solution.py:832
  39.8 1.5 %collective-permute-start.8 = (f32[8,16,128]{2,1,0:T(8,128)S(1)}, f32[8,16,128]{2,1,0:T(8,128)}, u32[]{:S(2)}, u32[]{:S(2)}) collective-permute-start(f32[8,16,128]{2,1,0:T(8,128)S(1)} %collect_taps.1.rest_0_), channel_id=1, source_target_pairs={{0,2},{1,3},{2,0},{3,1},{4,6},{5,7},{6,4},{7,5},{8,10},{9,11},{10,... | collective-permute-start | bytes 196616 | tf_op jit(solution)/shard_map/ppermute | solution.py:832
  41.3 1.9 %collective-permute-start.13 = (f32[272,128]{1,0:T(8,128)}, f32[272,128]{1,0:T(8,128)S(1)}, u32[]{:S(2)}, u32[]{:S(2)}) collective-permute-start(f32[272,128]{1,0:T(8,128)} %get-tuple-element.63), channel_id=1, source_target_pairs={{0,16},{4,20},{8,24},{12,28},{16,0},{20,4},{24,8},{28,12},{1,17},{... | collective-permute-start | bytes 417800 | tf_op jit(solution)/shard_map/ppermute | solution.py:832
  43.2 1.4 %collective-permute-start.14 = (f32[272,128]{1,0:T(8,128)}, f32[272,128]{1,0:T(8,128)S(1)}, u32[]{:S(2)}, u32[]{:S(2)}) collective-permute-start(f32[272,128]{1,0:T(8,128)} %get-tuple-element.64), channel_id=1, source_target_pairs={{0,24},{4,28},{8,16},{12,20},{16,8},{20,12},{24,0},{28,4},{1,25},{... | collective-permute-start | bytes 417800 | tf_op jit(solution)/shard_map/ppermute | solution.py:832
  44.6 1.5 %gated_bins.1 = (f32[512,1024]{1,0:T(8,128)S(1)}, f32[9,8,128]{2,1,0:T(8,128)S(1)}) custom-call(s32[1]{0:T(128)} %bitcast.me_ref, bf16[512,768]{1,0:T(8,128)(2,1)S(1)} %copy-done.1, f32[280,128]{1,0:T(8,128)S(1)} %collective-permute-done.rest_0_, f32[280,128]{1,0:T(8,128)S(1)} %collective-permute-done.1.rest_1_, f32[280,128]{1,0:T(8,128)S(1)} %copy-done.3, ...), custom_call_target="tpu_custom_call" | custom-call | tf_op jit(solution)/shard_map/gated_bins/pallas_call | solution.py:497
  46.1 2.3 %filter_spectra.1.spectra = f32[8,512,128]{2,1,0:T(8,128)S(1)} custom-call(s32[1]{0:T(128)} %bitcast.1.group_ref, f32[8,128]{1,0:T(8,128)S(1)} %copy-done.8, bf16[512,768]{1,0:T(8,128)(2,1)S(1)} %copy-done.1, f32[8,16,128]{2,1,0:T(8,128)S(1)} %collect_taps.1.rest_0_, f32[8,16,128]{2,1,0:T(8,128)S(1)} %collective-permute-done.7.rest_1_.refs_5_, ...), custom_call_target="tpu_custom_call" | custom-call | tf_op jit(solution)/shard_map/filter_spectra/pallas_call | solution.py:452
  48.5 4.3 %collective-permute-done.10.rest_1_.refs_3_.refs_2_.rest_2_ = f32[800,128]{1,0:T(8,128)S(1)} collective-permute-done((f32[800,128]{1,0:T(8,128)}, f32[800,128]{1,0:T(8,128)S(1)}, u32[]{:S(2)}, u32[]{:S(2)}) %collective-permute-start.10) | collective-permute-done | bytes 409632 | tf_op jit(solution)/shard_map/ppermute | solution.py:832
  52.7 3.1 %convolve.1 = (f32[256,128]{1,0:T(8,128)S(1)}, f32[256,128]{1,0:T(8,128)S(1)}, f32[256,128]{1,0:T(8,128)S(1)}, f32[256,128]{1,0:T(8,128)S(1)}, f32[256,128]{1,0:...) custom-call(s32[1]{0:T(128)} %bitcast.me_ref, ...), custom_call_target="tpu_custom_call" | custom-call | tf_op jit(solution)/shard_map/convolve/pallas_call | solution.py:582
  55.9 1.9 %collective-permute-start.11 = (f32[256,128]{1,0:T(8,128)S(1)}, f32[256,128]{1,0:T(8,128)S(1)}, u32[]{:S(2)}, u32[]{:S(2)}) collective-permute-start(f32[256,128]{1,0:T(8,128)S(1)} %get-tuple-element.57), channel_id=1, source_target_pairs={{0,16},{4,20},{8,24},{12,28},{16,0},{20,4},{24,8},{28,12},{1,17},{... | collective-permute-start | bytes 393224 | tf_op jit(solution)/shard_map/ppermute | solution.py:832
  57.8 1.8 %collective-permute-start.12 = (f32[256,128]{1,0:T(8,128)S(1)}, f32[256,128]{1,0:T(8,128)S(1)}, u32[]{:S(2)}, u32[]{:S(2)}) collective-permute-start(f32[256,128]{1,0:T(8,128)S(1)} %get-tuple-element.58), channel_id=1, source_target_pairs={{0,20},{4,16},{8,28},{12,24},{16,4},{20,0},{24,12},{28,8},{1,21},{... | collective-permute-start | bytes 393224 | tf_op jit(solution)/shard_map/ppermute | solution.py:832
  60.3 1.8 %collective-permute-start.16 = (f32[256,128]{1,0:T(8,128)S(1)}, f32[256,128]{1,0:T(8,128)S(1)}, u32[]{:S(2)}, u32[]{:S(2)}) collective-permute-start(f32[256,128]{1,0:T(8,128)S(1)} %get-tuple-element.66), channel_id=1, source_target_pairs={{0,8},{4,12},{8,0},{12,4},{16,24},{20,28},{24,16},{28,20},{1,9},{5... | collective-permute-start | bytes 393224 | tf_op jit(solution)/shard_map/ppermute | solution.py:832
  62.1 1.0 %collective-permute-start.17 = (f32[256,128]{1,0:T(8,128)S(1)}, f32[256,128]{1,0:T(8,128)S(1)}, u32[]{:S(2)}, u32[]{:S(2)}) collective-permute-start(f32[256,128]{1,0:T(8,128)S(1)} %get-tuple-element.67), channel_id=1, source_target_pairs={{0,12},{4,8},{8,4},{12,0},{16,28},{20,24},{24,20},{28,16},{1,13},{... | collective-permute-start | bytes 393224 | tf_op jit(solution)/shard_map/ppermute | solution.py:832
  63.1 5.3 %collective-permute-done.11.refs_5_.rest_0_ = f32[256,128]{1,0:T(8,128)S(1)} collective-permute-done((f32[256,128]{1,0:T(8,128)S(1)}, f32[256,128]{1,0:T(8,128)S(1)}, u32[]{:S(2)}, u32[]{:S(2)}) %collective-permute-start.11) | collective-permute-done | bytes 131104 | tf_op jit(solution)/shard_map/ppermute | solution.py:832
  68.4 1.9 %collective-permute-start.18 = (f32[256,128]{1,0:T(8,128)S(1)}, f32[256,128]{1,0:T(8,128)S(1)}, u32[]{:S(2)}, u32[]{:S(2)}) collective-permute-start(f32[256,128]{1,0:T(8,128)S(1)} %get-tuple-element.70), channel_id=1, source_target_pairs={{0,24},{4,28},{8,16},{12,20},{16,8},{20,12},{24,0},{28,4},{1,25},{... | collective-permute-start | bytes 393224 | tf_op jit(solution)/shard_map/ppermute | solution.py:832
  70.3 2.2 %collective-permute-done.12.rest_1_ = f32[256,128]{1,0:T(8,128)S(1)} collective-permute-done((f32[256,128]{1,0:T(8,128)S(1)}, f32[256,128]{1,0:T(8,128)S(1)}, u32[]{:S(2)}, u32[]{:S(2)}) %collective-permute-start.12) | collective-permute-done | bytes 131104 | tf_op jit(solution)/shard_map/ppermute | solution.py:832
  72.5 1.4 %collective-permute-start.19 = (f32[256,128]{1,0:T(8,128)S(1)}, f32[256,128]{1,0:T(8,128)S(1)}, u32[]{:S(2)}, u32[]{:S(2)}) collective-permute-start(f32[256,128]{1,0:T(8,128)S(1)} %get-tuple-element.71), channel_id=1, source_target_pairs={{0,28},{4,24},{8,20},{12,16},{16,12},{20,8},{24,4},{28,0},{1,29},{... | collective-permute-start | bytes 393224 | tf_op jit(solution)/shard_map/ppermute | solution.py:832
  74.4 1.0 %collective-permute-done.18.rest_6_ = f32[256,128]{1,0:T(8,128)S(1)} collective-permute-done((f32[256,128]{1,0:T(8,128)S(1)}, f32[256,128]{1,0:T(8,128)S(1)}, u32[]{:S(2)}, u32[]{:S(2)}) %collective-permute-start.18) | collective-permute-done | bytes 131104 | tf_op jit(solution)/shard_map/ppermute | solution.py:832
  75.4 4.9 %collective-permute-done.19.rest_7_ = f32[256,128]{1,0:T(8,128)S(1)} collective-permute-done((f32[256,128]{1,0:T(8,128)S(1)}, f32[256,128]{1,0:T(8,128)S(1)}, u32[]{:S(2)}, u32[]{:S(2)}) %collective-permute-start.19) | collective-permute-done | bytes 131104 | tf_op jit(solution)/shard_map/ppermute | solution.py:832
  80.3 2.2 %finish.1 = f32[32,8,1024]{2,1,0:T(8,128)} custom-call(s32[1]{0:T(128)} %bitcast.me_ref, f32[256,128]{1,0:T(8,128)S(1)} %collective-permute-done.11.refs_5_.rest_0_, f32[256,128]{1,0:T(8,128)S(1)} %collective-permute-done.12.rest_1_, f32[256,128]{1,0:T(8,128)S(1)} %get-tuple-element.59.rest_2_, f32[256,128]{1,0:T(8,128)S(1)} %collective-permute-done.15.rest_3_, ...), custom_call_target="tpu_custom_call" | custom-call | tf_op jit(solution)/shard_map/finish/pallas_call | solution.py:817
  (49 shorter events, 2.9 us)
Async XLA Ops:
  0.0 4.1 %copy-start.4 = (f32[3,3,1024]{2,1,0:T(4,128)S(1)}, f32[3,3,1024]{2,1,0:T(4,128)}, u32[]{:S(2)}) copy-start(f32[3,3,1024]{2,1,0:T(4,128)} %taps_in.1) | copy-start | bytes 110596
  4.1 29.8 %copy-start.3 = (f32[280,128]{1,0:T(8,128)S(1)}, f32[280,128]{1,0:T(8,128)}, u32[]{:S(2)}) copy-start(f32[280,128]{1,0:T(8,128)} %get-tuple-element.42.rest_2_) | copy-start | bytes 430084
  5.1 6.7 %copy-start.13 = (f32[280,128]{1,0:T(8,128)S(1)}, f32[280,128]{1,0:T(8,128)}, u32[]{:S(2)}) copy-start(f32[280,128]{1,0:T(8,128)} %get-tuple-element.41) | copy-start | bytes 430084
  5.1 6.7 %copy-start.12 = (f32[280,128]{1,0:T(8,128)S(1)}, f32[280,128]{1,0:T(8,128)}, u32[]{:S(2)}) copy-start(f32[280,128]{1,0:T(8,128)} %get-tuple-element.45) | copy-start | bytes 430084
  5.1 8.5 %copy-start.11 = (f32[280,128]{1,0:T(8,128)S(1)}, f32[280,128]{1,0:T(8,128)}, u32[]{:S(2)}) copy-start(f32[280,128]{1,0:T(8,128)} %get-tuple-element.46) | copy-start | bytes 430084
  5.1 17.6 %copy-start.10 = (f32[280,128]{1,0:T(8,128)S(1)}, f32[280,128]{1,0:T(8,128)}, u32[]{:S(2)}) copy-start(f32[280,128]{1,0:T(8,128)} %get-tuple-element.47) | copy-start | bytes 430084
  5.1 20.0 %copy-start.9 = (f32[280,128]{1,0:T(8,128)S(1)}, f32[280,128]{1,0:T(8,128)}, u32[]{:S(2)}) copy-start(f32[280,128]{1,0:T(8,128)} %get-tuple-element.48) | copy-start | bytes 430084
  6.1 29.1 %copy-start.6 = (f32[128,128]{1,0:T(8,128)}, f32[128,128]{1,0:T(8,128)S(1)}, u32[]{:S(2)}) copy-start(f32[128,128]{1,0:T(8,128)S(1)} %get-tuple-element.51.rest_0_) | copy-start | bytes 196612
  6.1 38.5 %copy-start.1 = (bf16[512,768]{1,0:T(8,128)(2,1)S(1)}, bf16[512,768]{1,0:T(8,128)(2,1)}, u32[]{:S(2)}) copy-start(bf16[512,768]{1,0:T(8,128)(2,1)} %constant.13.clone.forward) | copy-start | bytes 2359300
  6.1 27.7 %collective-permute-start.2 = (f32[1352,128]{1,0:T(8,128)S(1)}, f32[1352,128]{1,0:T(8,128)S(1)}, u32[]{:S(2)}, u32[]{:S(2)}) collective-permute-start(f32[1352,128]{1,0:T(8,128)S(1)} %get-tuple-element.44), channel_id=1, source_target_pairs={{0,4},{4,0},{8,12},{12,8},{16,20},{20,16},{24,28},{28,24},{1,5},{5... | collective-permute-start | bytes 2076680 | tf_op jit(solution)/shard_map/ppermute | solution.py:832
  9.1 13.5 %collective-permute-start = (f32[280,128]{1,0:T(8,128)S(1)}, f32[280,128]{1,0:T(8,128)S(1)}, u32[]{:S(2)}, u32[]{:S(2)}) collective-permute-start(f32[280,128]{1,0:T(8,128)S(1)} %copy-done.14), channel_id=1, source_target_pairs={{0,16},{4,20},{8,24},{12,28},{16,0},{20,4},{24,8},{28,12},{1,17},{... | collective-permute-start | bytes 430088 | tf_op jit(solution)/shard_map/ppermute | solution.py:832
  11.7 13.4 %collective-permute-start.1 = (f32[280,128]{1,0:T(8,128)S(1)}, f32[280,128]{1,0:T(8,128)S(1)}, u32[]{:S(2)}, u32[]{:S(2)}) collective-permute-start(f32[280,128]{1,0:T(8,128)S(1)} %copy-done.13), channel_id=1, source_target_pairs={{0,20},{4,16},{8,28},{12,24},{16,4},{20,0},{24,12},{28,8},{1,21},{... | collective-permute-start | bytes 430088 | tf_op jit(solution)/shard_map/ppermute | solution.py:832
  11.8 17.3 %collective-permute-start.3 = (f32[280,128]{1,0:T(8,128)S(1)}, f32[280,128]{1,0:T(8,128)S(1)}, u32[]{:S(2)}, u32[]{:S(2)}) collective-permute-start(f32[280,128]{1,0:T(8,128)S(1)} %copy-done.12), channel_id=1, source_target_pairs={{0,8},{4,12},{8,0},{12,4},{16,24},{20,28},{24,16},{28,20},{1,9},{5... | collective-permute-start | bytes 430088 | tf_op jit(solution)/shard_map/ppermute | solution.py:832
  13.6 15.5 %collective-permute-start.4 = (f32[280,128]{1,0:T(8,128)S(1)}, f32[280,128]{1,0:T(8,128)S(1)}, u32[]{:S(2)}, u32[]{:S(2)}) collective-permute-start(f32[280,128]{1,0:T(8,128)S(1)} %copy-done.11), channel_id=1, source_target_pairs={{0,12},{4,8},{8,4},{12,0},{16,28},{20,24},{24,20},{28,16},{1,13},{... | collective-permute-start | bytes 430088 | tf_op jit(solution)/shard_map/ppermute | solution.py:832
  22.6 7.6 %collective-permute-start.5 = (f32[280,128]{1,0:T(8,128)S(1)}, f32[280,128]{1,0:T(8,128)S(1)}, u32[]{:S(2)}, u32[]{:S(2)}) collective-permute-start(f32[280,128]{1,0:T(8,128)S(1)} %copy-done.10), channel_id=1, source_target_pairs={{0,24},{4,28},{8,16},{12,20},{16,8},{20,12},{24,0},{28,4},{1,25},{... | collective-permute-start | bytes 430088 | tf_op jit(solution)/shard_map/ppermute | solution.py:832
  25.1 8.1 %collective-permute-start.6 = (f32[280,128]{1,0:T(8,128)S(1)}, f32[280,128]{1,0:T(8,128)S(1)}, u32[]{:S(2)}, u32[]{:S(2)}) collective-permute-start(f32[280,128]{1,0:T(8,128)S(1)} %copy-done.9), channel_id=1, source_target_pairs={{0,28},{4,24},{8,20},{12,16},{16,12},{20,8},{24,4},{28,0},{1,29},{... | collective-permute-start | bytes 430088 | tf_op jit(solution)/shard_map/ppermute | solution.py:832
  33.9 12.3 %copy-start.8 = (f32[8,128]{1,0:T(8,128)S(1)}, f32[8,128]{1,0:T(8,128)}, u32[]{:S(2)}) copy-start(f32[8,128]{1,0:T(8,128)} %get-tuple-element.39.params) | copy-start | bytes 12292
  33.9 1.3 %collective-permute-start.7 = (f32[8,16,128]{2,1,0:T(8,128)S(1)}, f32[8,16,128]{2,1,0:T(8,128)S(1)}, u32[]{:S(2)}, u32[]{:S(2)}) collective-permute-start(f32[8,16,128]{2,1,0:T(8,128)S(1)} %collect_taps.1.rest_0_), channel_id=1, source_target_pairs={{0,1},{1,0},{2,3},{3,2},{4,5},{5,4},{6,7},{7,6},{8,9},{9,8},{10,11... | collective-permute-start | bytes 196616 | tf_op jit(solution)/shard_map/ppermute | solution.py:832
  36.1 16.6 %collective-permute-start.10 = (f32[800,128]{1,0:T(8,128)}, f32[800,128]{1,0:T(8,128)S(1)}, u32[]{:S(2)}, u32[]{:S(2)}) collective-permute-start(f32[800,128]{1,0:T(8,128)} %get-tuple-element.56), channel_id=1, source_target_pairs={{0,8},{4,12},{8,0},{12,4},{16,24},{20,28},{24,16},{28,20},{1,9},{5... | collective-permute-start | bytes 1228808 | tf_op jit(solution)/shard_map/ppermute | solution.py:832
  39.8 6.4 %collective-permute-start.8 = (f32[8,16,128]{2,1,0:T(8,128)S(1)}, f32[8,16,128]{2,1,0:T(8,128)}, u32[]{:S(2)}, u32[]{:S(2)}) collective-permute-start(f32[8,16,128]{2,1,0:T(8,128)S(1)} %collect_taps.1.rest_0_), channel_id=1, source_target_pairs={{0,2},{1,3},{2,0},{3,1},{4,6},{5,7},{6,4},{7,5},{8,10},{9,11},{10,... | collective-permute-start | bytes 196616 | tf_op jit(solution)/shard_map/ppermute | solution.py:832
  41.3 4.8 %collective-permute-start.9 = (f32[8,16,128]{2,1,0:T(8,128)S(1)}, f32[8,16,128]{2,1,0:T(8,128)}, u32[]{:S(2)}, u32[]{:S(2)}) collective-permute-start(f32[8,16,128]{2,1,0:T(8,128)S(1)} %collect_taps.1.rest_0_), channel_id=1, source_target_pairs={{0,3},{1,2},{2,1},{3,0},{4,7},{5,6},{6,5},{7,4},{8,11},{9,10},{10,... | collective-permute-start | bytes 196616 | tf_op jit(solution)/shard_map/ppermute | solution.py:832
  41.3 18.3 %collective-permute-start.13 = (f32[272,128]{1,0:T(8,128)}, f32[272,128]{1,0:T(8,128)S(1)}, u32[]{:S(2)}, u32[]{:S(2)}) collective-permute-start(f32[272,128]{1,0:T(8,128)} %get-tuple-element.63), channel_id=1, source_target_pairs={{0,16},{4,20},{8,24},{12,28},{16,0},{20,4},{24,8},{28,12},{1,17},{... | collective-permute-start | bytes 417800 | tf_op jit(solution)/shard_map/ppermute | solution.py:832
  43.2 16.4 %collective-permute-start.14 = (f32[272,128]{1,0:T(8,128)}, f32[272,128]{1,0:T(8,128)S(1)}, u32[]{:S(2)}, u32[]{:S(2)}) collective-permute-start(f32[272,128]{1,0:T(8,128)} %get-tuple-element.64), channel_id=1, source_target_pairs={{0,24},{4,28},{8,16},{12,20},{16,8},{20,12},{24,0},{28,4},{1,25},{... | collective-permute-start | bytes 417800 | tf_op jit(solution)/shard_map/ppermute | solution.py:832
  46.1 6.6 %copy-start.2 = (bf16[256,1536]{1,0:T(8,128)(2,1)S(1)}, bf16[256,1536]{1,0:T(8,128)(2,1)}, u32[]{:S(2)}) copy-start(bf16[256,1536]{1,0:T(8,128)(2,1)} %constant.14.clone.inverse) | copy-start | bytes 2359300
  46.1 6.6 %copy-start.7 = (f32[128,128]{1,0:T(8,128)S(1)}, f32[128,128]{1,0:T(8,128)}, u32[]{:S(2)}) copy-start(f32[128,128]{1,0:T(8,128)} %copy-done.6) | copy-start | bytes 196612
  55.9 12.5 %collective-permute-start.11 = (f32[256,128]{1,0:T(8,128)S(1)}, f32[256,128]{1,0:T(8,128)S(1)}, u32[]{:S(2)}, u32[]{:S(2)}) collective-permute-start(f32[256,128]{1,0:T(8,128)S(1)} %get-tuple-element.57), channel_id=1, source_target_pairs={{0,16},{4,20},{8,24},{12,28},{16,0},{20,4},{24,8},{28,12},{1,17},{... | collective-permute-start | bytes 393224 | tf_op jit(solution)/shard_map/ppermute | solution.py:832
  57.8 14.7 %collective-permute-start.12 = (f32[256,128]{1,0:T(8,128)S(1)}, f32[256,128]{1,0:T(8,128)S(1)}, u32[]{:S(2)}, u32[]{:S(2)}) collective-permute-start(f32[256,128]{1,0:T(8,128)S(1)} %get-tuple-element.58), channel_id=1, source_target_pairs={{0,20},{4,16},{8,28},{12,24},{16,4},{20,0},{24,12},{28,8},{1,21},{... | collective-permute-start | bytes 393224 | tf_op jit(solution)/shard_map/ppermute | solution.py:832
  59.6 14.7 %collective-permute-start.15 = (f32[256,128]{1,0:T(8,128)S(1)}, f32[256,128]{1,0:T(8,128)S(1)}, u32[]{:S(2)}, u32[]{:S(2)}) collective-permute-start(f32[256,128]{1,0:T(8,128)S(1)} %get-tuple-element.65), channel_id=1, source_target_pairs={{0,4},{4,0},{8,12},{12,8},{16,20},{20,16},{24,28},{28,24},{1,5},{5... | collective-permute-start | bytes 393224 | tf_op jit(solution)/shard_map/ppermute | solution.py:832
  60.3 14.0 %collective-permute-start.16 = (f32[256,128]{1,0:T(8,128)S(1)}, f32[256,128]{1,0:T(8,128)S(1)}, u32[]{:S(2)}, u32[]{:S(2)}) collective-permute-start(f32[256,128]{1,0:T(8,128)S(1)} %get-tuple-element.66), channel_id=1, source_target_pairs={{0,8},{4,12},{8,0},{12,4},{16,24},{20,28},{24,16},{28,20},{1,9},{5... | collective-permute-start | bytes 393224 | tf_op jit(solution)/shard_map/ppermute | solution.py:832
  62.1 12.2 %collective-permute-start.17 = (f32[256,128]{1,0:T(8,128)S(1)}, f32[256,128]{1,0:T(8,128)S(1)}, u32[]{:S(2)}, u32[]{:S(2)}) collective-permute-start(f32[256,128]{1,0:T(8,128)S(1)} %get-tuple-element.67), channel_id=1, source_target_pairs={{0,12},{4,8},{8,4},{12,0},{16,28},{20,24},{24,20},{28,16},{1,13},{... | collective-permute-start | bytes 393224 | tf_op jit(solution)/shard_map/ppermute | solution.py:832
  68.4 7.0 %collective-permute-start.18 = (f32[256,128]{1,0:T(8,128)S(1)}, f32[256,128]{1,0:T(8,128)S(1)}, u32[]{:S(2)}, u32[]{:S(2)}) collective-permute-start(f32[256,128]{1,0:T(8,128)S(1)} %get-tuple-element.70), channel_id=1, source_target_pairs={{0,24},{4,28},{8,16},{12,20},{16,8},{20,12},{24,0},{28,4},{1,25},{... | collective-permute-start | bytes 393224 | tf_op jit(solution)/shard_map/ppermute | solution.py:832
  72.5 7.8 %collective-permute-start.19 = (f32[256,128]{1,0:T(8,128)S(1)}, f32[256,128]{1,0:T(8,128)S(1)}, u32[]{:S(2)}, u32[]{:S(2)}) collective-permute-start(f32[256,128]{1,0:T(8,128)S(1)} %get-tuple-element.71), channel_id=1, source_target_pairs={{0,28},{4,24},{8,20},{12,16},{16,12},{20,8},{24,4},{28,0},{1,29},{... | collective-permute-start | bytes 393224 | tf_op jit(solution)/shard_map/ppermute | solution.py:832
  (3 other events, 9.1 us)

commit v5 on v4

--- a/solution.py
+++ b/solution.py
@@ -292,8 +292,6 @@
         pltpu.make_async_copy(source, target, sems.at[2 * pieces + i])
         for i, (source, target) in enumerate(zip(sources, targets))
     ]
-    for fetch in fetches:
-        fetch.start()
     channels = streams.shape[2]
     me = me_ref[0]
     part = length // pieces
@@ -307,6 +305,9 @@
             )
             load.start()
             loads.append(load)
+        if piece == 0:
+            for fetch in fetches:
+                fetch.start()
     key[0:ROWS, :] = jnp.zeros((ROWS, channels), jnp.float32)
     value[0:ROWS, :] = jnp.zeros((ROWS, channels), jnp.float32)
     for fetch in fetches:

time: 82.6 us -> 82.8 us (level)
  no operation moved by 1% of the time
where the time goes in v5:
time: 82.8 us; the launch traced here: 82.6 us
  starting transfers between devices  34.5 us (42%)
  waiting for transfers between devices  31.4 us (38%)
  Pallas kernels  15.5 us (19%)
  local copies, waits for them, and re-layouts  1 us (1%)
    ppermute x20, starting transfers between devices, swapped(): lax.ppermute(block, axis, [(i, i ^ k) for i in range(lax.axis_size(axis))])  34.5 us
    ppermute x20, waiting for transfers between devices, swapped(): lax.ppermute(block, axis, [(i, i ^ k) for i in range(lax.axis_size(axis))])  31.4 us
    pallas_call x1, Pallas kernels, gate(): pl.pallas_call(functools.partial(gate_kernel, count, width, pieces), out_...  4.2 us
    pallas_call x1, Pallas kernels, convolve(): pl.pallas_call(functools.partial(convolve_kernel, count, length), out_sha...  3.12 us
    pallas_call x1, Pallas kernels, filter_spectra(): pl.pallas_call(functools.partial(filter_kernel, count, width), out_shape=...  2.32 us
    pallas_call x1, Pallas kernels, finish(): pl.pallas_call(functools.partial(finish_kernel, count, width, pieces), ou...  2.18 us
  transfers between devices with their start and end apart: 20, of which 10 were waited for; matrix products, arithmetic and copies ran while one was open for 0% of the time, Pallas kernels for 9%

profile of v5, /device:TPU:0, one launch (start us, length us, event | category | flops | bytes accessed | tf_op | source)
XLA Modules:
  0.0 82.6 jit_solution(14654518656289215718)
XLA Ops:
  0.0 4.2 %gate.1 = (f32[280,128]{1,0:T(8,128)}, f32[280,128]{1,0:T(8,128)}, f32[280,128]{1,0:T(8,128)}, f32[280,128]{1,0:T(8,128)}, f32[280,128]{1,0:T(8,128)}, /*index=5...) custom-call(s32[1]{0:T(128)} %bitcast.me_ref, f32[3,256,1024]{2,1,0:T(8,128)} %streams.3, ...), custom_call_target="tpu_custom_call" | custom-call | tf_op jit(solution)/shard_map/gate/pallas_call | solution.py:367
  4.3 0.9 %copy-done.5 = f32[280,128]{1,0:T(8,128)S(1)} copy-done((f32[280,128]{1,0:T(8,128)S(1)}, f32[280,128]{1,0:T(8,128)}, u32[]{:S(2)}) %copy-start.5) | copy-done | bytes 143384
  5.2 1.0 %query.1 = (f32[272,128]{1,0:T(8,128)S(1)}, f32[272,128]{1,0:T(8,128)S(1)}, f32[136,128]{1,0:T(8,128)S(1)}, f32[136,128]{1,0:T(8,128)S(1)}, f32[128,128]{1,0:T(8...) custom-call(s32[1]{0:T(128)} %bitcast.me_ref, f32[3,256,1024]{2,1,0:T(8,128)S(1)} %copy-done, ...), custom_call_target="tpu_custom_call" | custom-call | tf_op jit(solution)/shard_map/query/pallas_call | solution.py:665
  6.3 3.0 %collective-permute-start.2 = (f32[1352,128]{1,0:T(8,128)S(1)}, f32[1352,128]{1,0:T(8,128)S(1)}, u32[]{:S(2)}, u32[]{:S(2)}) collective-permute-start(f32[1352,128]{1,0:T(8,128)S(1)} %get-tuple-element.44), channel_id=1, source_target_pairs={{0,4},{4,0},{8,12},{12,8},{16,20},{20,16},{24,28},{28,24},{1,5},{5... | collective-permute-start | bytes 2076680 | tf_op jit(solution)/shard_map/ppermute | solution.py:833
  9.3 2.6 %collective-permute-start = (f32[280,128]{1,0:T(8,128)S(1)}, f32[280,128]{1,0:T(8,128)S(1)}, u32[]{:S(2)}, u32[]{:S(2)}) collective-permute-start(f32[280,128]{1,0:T(8,128)S(1)} %copy-done.14), channel_id=1, source_target_pairs={{0,16},{4,20},{8,24},{12,28},{16,0},{20,4},{24,8},{28,12},{1,17},{... | collective-permute-start | bytes 430088 | tf_op jit(solution)/shard_map/ppermute | solution.py:833
  11.9 1.8 %collective-permute-start.3 = (f32[280,128]{1,0:T(8,128)S(1)}, f32[280,128]{1,0:T(8,128)S(1)}, u32[]{:S(2)}, u32[]{:S(2)}) collective-permute-start(f32[280,128]{1,0:T(8,128)S(1)} %copy-done.12), channel_id=1, source_target_pairs={{0,8},{4,12},{8,0},{12,4},{16,24},{20,28},{24,16},{28,20},{1,9},{5... | collective-permute-start | bytes 430088 | tf_op jit(solution)/shard_map/ppermute | solution.py:833
  13.7 1.4 %collective-permute-start.4 = (f32[280,128]{1,0:T(8,128)S(1)}, f32[280,128]{1,0:T(8,128)S(1)}, u32[]{:S(2)}, u32[]{:S(2)}) collective-permute-start(f32[280,128]{1,0:T(8,128)S(1)} %copy-done.11), channel_id=1, source_target_pairs={{0,12},{4,8},{8,4},{12,0},{16,28},{20,24},{24,20},{28,16},{1,13},{... | collective-permute-start | bytes 430088 | tf_op jit(solution)/shard_map/ppermute | solution.py:833
  15.1 7.7 %collective-permute-done.rest_0_ = f32[280,128]{1,0:T(8,128)S(1)} collective-permute-done((f32[280,128]{1,0:T(8,128)S(1)}, f32[280,128]{1,0:T(8,128)S(1)}, u32[]{:S(2)}, u32[]{:S(2)}) %collective-permute-start) | collective-permute-done | bytes 143392 | tf_op jit(solution)/shard_map/ppermute | solution.py:833
  22.8 2.4 %collective-permute-start.5 = (f32[280,128]{1,0:T(8,128)S(1)}, f32[280,128]{1,0:T(8,128)S(1)}, u32[]{:S(2)}, u32[]{:S(2)}) collective-permute-start(f32[280,128]{1,0:T(8,128)S(1)} %copy-done.10), channel_id=1, source_target_pairs={{0,24},{4,28},{8,16},{12,20},{16,8},{20,12},{24,0},{28,4},{1,25},{... | collective-permute-start | bytes 430088 | tf_op jit(solution)/shard_map/ppermute | solution.py:833
  25.2 4.0 %collective-permute-start.6 = (f32[280,128]{1,0:T(8,128)S(1)}, f32[280,128]{1,0:T(8,128)S(1)}, u32[]{:S(2)}, u32[]{:S(2)}) collective-permute-start(f32[280,128]{1,0:T(8,128)S(1)} %copy-done.9), channel_id=1, source_target_pairs={{0,28},{4,24},{8,20},{12,16},{16,12},{20,8},{24,4},{28,0},{1,29},{... | collective-permute-start | bytes 430088 | tf_op jit(solution)/shard_map/ppermute | solution.py:833
  29.2 1.1 %collective-permute-done.5.rest_6_ = f32[280,128]{1,0:T(8,128)S(1)} collective-permute-done((f32[280,128]{1,0:T(8,128)S(1)}, f32[280,128]{1,0:T(8,128)S(1)}, u32[]{:S(2)}, u32[]{:S(2)}) %collective-permute-start.5) | collective-permute-done | bytes 143392 | tf_op jit(solution)/shard_map/ppermute | solution.py:833
  30.4 3.0 %collective-permute-done.6.rest_7_ = f32[280,128]{1,0:T(8,128)S(1)} collective-permute-done((f32[280,128]{1,0:T(8,128)S(1)}, f32[280,128]{1,0:T(8,128)S(1)}, u32[]{:S(2)}, u32[]{:S(2)}) %collective-permute-start.6) | collective-permute-done | bytes 143392 | tf_op jit(solution)/shard_map/ppermute | solution.py:833
  34.1 1.2 %collective-permute-done.7.rest_1_.refs_5_ = f32[8,16,128]{2,1,0:T(8,128)S(1)} collective-permute-done((f32[8,16,128]{2,1,0:T(8,128)S(1)}, f32[8,16,128]{2,1,0:T(8,128)S(1)}, u32[]{:S(2)}, u32[]{:S(2)}) %collective-permute-start.7) | collective-permute-done | bytes 65568 | tf_op jit(solution)/shard_map/ppermute | solution.py:833
  36.2 3.7 %collective-permute-start.10 = (f32[800,128]{1,0:T(8,128)}, f32[800,128]{1,0:T(8,128)S(1)}, u32[]{:S(2)}, u32[]{:S(2)}) collective-permute-start(f32[800,128]{1,0:T(8,128)} %get-tuple-element.56), channel_id=1, source_target_pairs={{0,8},{4,12},{8,0},{12,4},{16,24},{20,28},{24,16},{28,20},{1,9},{5... | collective-permute-start | bytes 1228808 | tf_op jit(solution)/shard_map/ppermute | solution.py:833
  39.9 1.5 %collective-permute-start.8 = (f32[8,16,128]{2,1,0:T(8,128)S(1)}, f32[8,16,128]{2,1,0:T(8,128)}, u32[]{:S(2)}, u32[]{:S(2)}) collective-permute-start(f32[8,16,128]{2,1,0:T(8,128)S(1)} %collect_taps.1.rest_0_), channel_id=1, source_target_pairs={{0,2},{1,3},{2,0},{3,1},{4,6},{5,7},{6,4},{7,5},{8,10},{9,11},{10,... | collective-permute-start | bytes 196616 | tf_op jit(solution)/shard_map/ppermute | solution.py:833
  41.4 1.9 %collective-permute-start.13 = (f32[272,128]{1,0:T(8,128)}, f32[272,128]{1,0:T(8,128)S(1)}, u32[]{:S(2)}, u32[]{:S(2)}) collective-permute-start(f32[272,128]{1,0:T(8,128)} %get-tuple-element.63), channel_id=1, source_target_pairs={{0,16},{4,20},{8,24},{12,28},{16,0},{20,4},{24,8},{28,12},{1,17},{... | collective-permute-start | bytes 417800 | tf_op jit(solution)/shard_map/ppermute | solution.py:833
  43.3 1.4 %collective-permute-start.14 = (f32[272,128]{1,0:T(8,128)}, f32[272,128]{1,0:T(8,128)S(1)}, u32[]{:S(2)}, u32[]{:S(2)}) collective-permute-start(f32[272,128]{1,0:T(8,128)} %get-tuple-element.64), channel_id=1, source_target_pairs={{0,24},{4,28},{8,16},{12,20},{16,8},{20,12},{24,0},{28,4},{1,25},{... | collective-permute-start | bytes 417800 | tf_op jit(solution)/shard_map/ppermute | solution.py:833
  44.8 1.5 %gated_bins.1 = (f32[512,1024]{1,0:T(8,128)S(1)}, f32[9,8,128]{2,1,0:T(8,128)S(1)}) custom-call(s32[1]{0:T(128)} %bitcast.me_ref, bf16[512,768]{1,0:T(8,128)(2,1)S(1)} %copy-done.1, f32[280,128]{1,0:T(8,128)S(1)} %collective-permute-done.rest_0_, f32[280,128]{1,0:T(8,128)S(1)} %collective-permute-done.1.rest_1_, f32[280,128]{1,0:T(8,128)S(1)} %copy-done.3, ...), custom_call_target="tpu_custom_call" | custom-call | tf_op jit(solution)/shard_map/gated_bins/pallas_call | solution.py:498
  46.3 2.3 %filter_spectra.1.spectra = f32[8,512,128]{2,1,0:T(8,128)S(1)} custom-call(s32[1]{0:T(128)} %bitcast.1.group_ref, f32[8,128]{1,0:T(8,128)S(1)} %copy-done.8, bf16[512,768]{1,0:T(8,128)(2,1)S(1)} %copy-done.1, f32[8,16,128]{2,1,0:T(8,128)S(1)} %collect_taps.1.rest_0_, f32[8,16,128]{2,1,0:T(8,128)S(1)} %collective-permute-done.7.rest_1_.refs_5_, ...), custom_call_target="tpu_custom_call" | custom-call | tf_op jit(solution)/shard_map/filter_spectra/pallas_call | solution.py:453
  48.6 4.3 %collective-permute-done.10.rest_1_.refs_3_.refs_2_.rest_2_ = f32[800,128]{1,0:T(8,128)S(1)} collective-permute-done((f32[800,128]{1,0:T(8,128)}, f32[800,128]{1,0:T(8,128)S(1)}, u32[]{:S(2)}, u32[]{:S(2)}) %collective-permute-start.10) | collective-permute-done | bytes 409632 | tf_op jit(solution)/shard_map/ppermute | solution.py:833
  52.9 3.1 %convolve.1 = (f32[256,128]{1,0:T(8,128)S(1)}, f32[256,128]{1,0:T(8,128)S(1)}, f32[256,128]{1,0:T(8,128)S(1)}, f32[256,128]{1,0:T(8,128)S(1)}, f32[256,128]{1,0:...) custom-call(s32[1]{0:T(128)} %bitcast.me_ref, ...), custom_call_target="tpu_custom_call" | custom-call | tf_op jit(solution)/shard_map/convolve/pallas_call | solution.py:583
  56.0 2.0 %collective-permute-start.11 = (f32[256,128]{1,0:T(8,128)S(1)}, f32[256,128]{1,0:T(8,128)S(1)}, u32[]{:S(2)}, u32[]{:S(2)}) collective-permute-start(f32[256,128]{1,0:T(8,128)S(1)} %get-tuple-element.57), channel_id=1, source_target_pairs={{0,16},{4,20},{8,24},{12,28},{16,0},{20,4},{24,8},{28,12},{1,17},{... | collective-permute-start | bytes 393224 | tf_op jit(solution)/shard_map/ppermute | solution.py:833
  58.0 1.8 %collective-permute-start.12 = (f32[256,128]{1,0:T(8,128)S(1)}, f32[256,128]{1,0:T(8,128)S(1)}, u32[]{:S(2)}, u32[]{:S(2)}) collective-permute-start(f32[256,128]{1,0:T(8,128)S(1)} %get-tuple-element.58), channel_id=1, source_target_pairs={{0,20},{4,16},{8,28},{12,24},{16,4},{20,0},{24,12},{28,8},{1,21},{... | collective-permute-start | bytes 393224 | tf_op jit(solution)/shard_map/ppermute | solution.py:833
  60.5 1.8 %collective-permute-start.16 = (f32[256,128]{1,0:T(8,128)S(1)}, f32[256,128]{1,0:T(8,128)S(1)}, u32[]{:S(2)}, u32[]{:S(2)}) collective-permute-start(f32[256,128]{1,0:T(8,128)S(1)} %get-tuple-element.66), channel_id=1, source_target_pairs={{0,8},{4,12},{8,0},{12,4},{16,24},{20,28},{24,16},{28,20},{1,9},{5... | collective-permute-start | bytes 393224 | tf_op jit(solution)/shard_map/ppermute | solution.py:833
  62.2 1.0 %collective-permute-start.17 = (f32[256,128]{1,0:T(8,128)S(1)}, f32[256,128]{1,0:T(8,128)S(1)}, u32[]{:S(2)}, u32[]{:S(2)}) collective-permute-start(f32[256,128]{1,0:T(8,128)S(1)} %get-tuple-element.67), channel_id=1, source_target_pairs={{0,12},{4,8},{8,4},{12,0},{16,28},{20,24},{24,20},{28,16},{1,13},{... | collective-permute-start | bytes 393224 | tf_op jit(solution)/shard_map/ppermute | solution.py:833
  63.2 5.3 %collective-permute-done.11.refs_5_.rest_0_ = f32[256,128]{1,0:T(8,128)S(1)} collective-permute-done((f32[256,128]{1,0:T(8,128)S(1)}, f32[256,128]{1,0:T(8,128)S(1)}, u32[]{:S(2)}, u32[]{:S(2)}) %collective-permute-start.11) | collective-permute-done | bytes 131104 | tf_op jit(solution)/shard_map/ppermute | solution.py:833
  68.5 1.9 %collective-permute-start.18 = (f32[256,128]{1,0:T(8,128)S(1)}, f32[256,128]{1,0:T(8,128)S(1)}, u32[]{:S(2)}, u32[]{:S(2)}) collective-permute-start(f32[256,128]{1,0:T(8,128)S(1)} %get-tuple-element.70), channel_id=1, source_target_pairs={{0,24},{4,28},{8,16},{12,20},{16,8},{20,12},{24,0},{28,4},{1,25},{... | collective-permute-start | bytes 393224 | tf_op jit(solution)/shard_map/ppermute | solution.py:833
  70.4 2.2 %collective-permute-done.12.rest_1_ = f32[256,128]{1,0:T(8,128)S(1)} collective-permute-done((f32[256,128]{1,0:T(8,128)S(1)}, f32[256,128]{1,0:T(8,128)S(1)}, u32[]{:S(2)}, u32[]{:S(2)}) %collective-permute-start.12) | collective-permute-done | bytes 131104 | tf_op jit(solution)/shard_map/ppermute | solution.py:833
  72.7 1.4 %collective-permute-start.19 = (f32[256,128]{1,0:T(8,128)S(1)}, f32[256,128]{1,0:T(8,128)S(1)}, u32[]{:S(2)}, u32[]{:S(2)}) collective-permute-start(f32[256,128]{1,0:T(8,128)S(1)} %get-tuple-element.71), channel_id=1, source_target_pairs={{0,28},{4,24},{8,20},{12,16},{16,12},{20,8},{24,4},{28,0},{1,29},{... | collective-permute-start | bytes 393224 | tf_op jit(solution)/shard_map/ppermute | solution.py:833
  74.5 1.0 %collective-permute-done.18.rest_6_ = f32[256,128]{1,0:T(8,128)S(1)} collective-permute-done((f32[256,128]{1,0:T(8,128)S(1)}, f32[256,128]{1,0:T(8,128)S(1)}, u32[]{:S(2)}, u32[]{:S(2)}) %collective-permute-start.18) | collective-permute-done | bytes 131104 | tf_op jit(solution)/shard_map/ppermute | solution.py:833
  75.5 4.9 %collective-permute-done.19.rest_7_ = f32[256,128]{1,0:T(8,128)S(1)} collective-permute-done((f32[256,128]{1,0:T(8,128)S(1)}, f32[256,128]{1,0:T(8,128)S(1)}, u32[]{:S(2)}, u32[]{:S(2)}) %collective-permute-start.19) | collective-permute-done | bytes 131104 | tf_op jit(solution)/shard_map/ppermute | solution.py:833
  80.4 2.2 %finish.1 = f32[32,8,1024]{2,1,0:T(8,128)} custom-call(s32[1]{0:T(128)} %bitcast.me_ref, f32[256,128]{1,0:T(8,128)S(1)} %collective-permute-done.11.refs_5_.rest_0_, f32[256,128]{1,0:T(8,128)S(1)} %collective-permute-done.12.rest_1_, f32[256,128]{1,0:T(8,128)S(1)} %get-tuple-element.59.rest_2_, f32[256,128]{1,0:T(8,128)S(1)} %collective-permute-done.15.rest_3_, ...), custom_call_target="tpu_custom_call" | custom-call | tf_op jit(solution)/shard_map/finish/pallas_call | solution.py:818
  (49 shorter events, 2.9 us)
Async XLA Ops:
  0.0 4.2 %copy-start.4 = (f32[3,3,1024]{2,1,0:T(4,128)S(1)}, f32[3,3,1024]{2,1,0:T(4,128)}, u32[]{:S(2)}) copy-start(f32[3,3,1024]{2,1,0:T(4,128)} %taps_in.1) | copy-start | bytes 110596
  4.2 29.8 %copy-start.3 = (f32[280,128]{1,0:T(8,128)S(1)}, f32[280,128]{1,0:T(8,128)}, u32[]{:S(2)}) copy-start(f32[280,128]{1,0:T(8,128)} %get-tuple-element.42.rest_2_) | copy-start | bytes 430084
  5.2 6.7 %copy-start.13 = (f32[280,128]{1,0:T(8,128)S(1)}, f32[280,128]{1,0:T(8,128)}, u32[]{:S(2)}) copy-start(f32[280,128]{1,0:T(8,128)} %get-tuple-element.41) | copy-start | bytes 430084
  5.2 6.7 %copy-start.12 = (f32[280,128]{1,0:T(8,128)S(1)}, f32[280,128]{1,0:T(8,128)}, u32[]{:S(2)}) copy-start(f32[280,128]{1,0:T(8,128)} %get-tuple-element.45) | copy-start | bytes 430084
  5.2 8.5 %copy-start.11 = (f32[280,128]{1,0:T(8,128)S(1)}, f32[280,128]{1,0:T(8,128)}, u32[]{:S(2)}) copy-start(f32[280,128]{1,0:T(8,128)} %get-tuple-element.46) | copy-start | bytes 430084
  5.2 17.6 %copy-start.10 = (f32[280,128]{1,0:T(8,128)S(1)}, f32[280,128]{1,0:T(8,128)}, u32[]{:S(2)}) copy-start(f32[280,128]{1,0:T(8,128)} %get-tuple-element.47) | copy-start | bytes 430084
  5.2 20.0 %copy-start.9 = (f32[280,128]{1,0:T(8,128)S(1)}, f32[280,128]{1,0:T(8,128)}, u32[]{:S(2)}) copy-start(f32[280,128]{1,0:T(8,128)} %get-tuple-element.48) | copy-start | bytes 430084
  6.2 29.1 %copy-start.6 = (f32[128,128]{1,0:T(8,128)}, f32[128,128]{1,0:T(8,128)S(1)}, u32[]{:S(2)}) copy-start(f32[128,128]{1,0:T(8,128)S(1)} %get-tuple-element.51.rest_0_) | copy-start | bytes 196612
  6.2 38.5 %copy-start.1 = (bf16[512,768]{1,0:T(8,128)(2,1)S(1)}, bf16[512,768]{1,0:T(8,128)(2,1)}, u32[]{:S(2)}) copy-start(bf16[512,768]{1,0:T(8,128)(2,1)} %constant.13.clone.forward) | copy-start | bytes 2359300
  6.3 27.7 %collective-permute-start.2 = (f32[1352,128]{1,0:T(8,128)S(1)}, f32[1352,128]{1,0:T(8,128)S(1)}, u32[]{:S(2)}, u32[]{:S(2)}) collective-permute-start(f32[1352,128]{1,0:T(8,128)S(1)} %get-tuple-element.44), channel_id=1, source_target_pairs={{0,4},{4,0},{8,12},{12,8},{16,20},{20,16},{24,28},{28,24},{1,5},{5... | collective-permute-start | bytes 2076680 | tf_op jit(solution)/shard_map/ppermute | solution.py:833
  9.3 13.5 %collective-permute-start = (f32[280,128]{1,0:T(8,128)S(1)}, f32[280,128]{1,0:T(8,128)S(1)}, u32[]{:S(2)}, u32[]{:S(2)}) collective-permute-start(f32[280,128]{1,0:T(8,128)S(1)} %copy-done.14), channel_id=1, source_target_pairs={{0,16},{4,20},{8,24},{12,28},{16,0},{20,4},{24,8},{28,12},{1,17},{... | collective-permute-start | bytes 430088 | tf_op jit(solution)/shard_map/ppermute | solution.py:833
  11.9 13.4 %collective-permute-start.1 = (f32[280,128]{1,0:T(8,128)S(1)}, f32[280,128]{1,0:T(8,128)S(1)}, u32[]{:S(2)}, u32[]{:S(2)}) collective-permute-start(f32[280,128]{1,0:T(8,128)S(1)} %copy-done.13), channel_id=1, source_target_pairs={{0,20},{4,16},{8,28},{12,24},{16,4},{20,0},{24,12},{28,8},{1,21},{... | collective-permute-start | bytes 430088 | tf_op jit(solution)/shard_map/ppermute | solution.py:833
  11.9 17.3 %collective-permute-start.3 = (f32[280,128]{1,0:T(8,128)S(1)}, f32[280,128]{1,0:T(8,128)S(1)}, u32[]{:S(2)}, u32[]{:S(2)}) collective-permute-start(f32[280,128]{1,0:T(8,128)S(1)} %copy-done.12), channel_id=1, source_target_pairs={{0,8},{4,12},{8,0},{12,4},{16,24},{20,28},{24,16},{28,20},{1,9},{5... | collective-permute-start | bytes 430088 | tf_op jit(solution)/shard_map/ppermute | solution.py:833
  13.7 15.5 %collective-permute-start.4 = (f32[280,128]{1,0:T(8,128)S(1)}, f32[280,128]{1,0:T(8,128)S(1)}, u32[]{:S(2)}, u32[]{:S(2)}) collective-permute-start(f32[280,128]{1,0:T(8,128)S(1)} %copy-done.11), channel_id=1, source_target_pairs={{0,12},{4,8},{8,4},{12,0},{16,28},{20,24},{24,20},{28,16},{1,13},{... | collective-permute-start | bytes 430088 | tf_op jit(solution)/shard_map/ppermute | solution.py:833
  22.8 7.6 %collective-permute-start.5 = (f32[280,128]{1,0:T(8,128)S(1)}, f32[280,128]{1,0:T(8,128)S(1)}, u32[]{:S(2)}, u32[]{:S(2)}) collective-permute-start(f32[280,128]{1,0:T(8,128)S(1)} %copy-done.10), channel_id=1, source_target_pairs={{0,24},{4,28},{8,16},{12,20},{16,8},{20,12},{24,0},{28,4},{1,25},{... | collective-permute-start | bytes 430088 | tf_op jit(solution)/shard_map/ppermute | solution.py:833
  25.2 8.1 %collective-permute-start.6 = (f32[280,128]{1,0:T(8,128)S(1)}, f32[280,128]{1,0:T(8,128)S(1)}, u32[]{:S(2)}, u32[]{:S(2)}) collective-permute-start(f32[280,128]{1,0:T(8,128)S(1)} %copy-done.9), channel_id=1, source_target_pairs={{0,28},{4,24},{8,20},{12,16},{16,12},{20,8},{24,4},{28,0},{1,29},{... | collective-permute-start | bytes 430088 | tf_op jit(solution)/shard_map/ppermute | solution.py:833
  34.0 12.3 %copy-start.8 = (f32[8,128]{1,0:T(8,128)S(1)}, f32[8,128]{1,0:T(8,128)}, u32[]{:S(2)}) copy-start(f32[8,128]{1,0:T(8,128)} %get-tuple-element.39.params) | copy-start | bytes 12292
  34.0 1.3 %collective-permute-start.7 = (f32[8,16,128]{2,1,0:T(8,128)S(1)}, f32[8,16,128]{2,1,0:T(8,128)S(1)}, u32[]{:S(2)}, u32[]{:S(2)}) collective-permute-start(f32[8,16,128]{2,1,0:T(8,128)S(1)} %collect_taps.1.rest_0_), channel_id=1, source_target_pairs={{0,1},{1,0},{2,3},{3,2},{4,5},{5,4},{6,7},{7,6},{8,9},{9,8},{10,11... | collective-permute-start | bytes 196616 | tf_op jit(solution)/shard_map/ppermute | solution.py:833
  36.2 16.6 %collective-permute-start.10 = (f32[800,128]{1,0:T(8,128)}, f32[800,128]{1,0:T(8,128)S(1)}, u32[]{:S(2)}, u32[]{:S(2)}) collective-permute-start(f32[800,128]{1,0:T(8,128)} %get-tuple-element.56), channel_id=1, source_target_pairs={{0,8},{4,12},{8,0},{12,4},{16,24},{20,28},{24,16},{28,20},{1,9},{5... | collective-permute-start | bytes 1228808 | tf_op jit(solution)/shard_map/ppermute | solution.py:833
  39.9 6.4 %collective-permute-start.8 = (f32[8,16,128]{2,1,0:T(8,128)S(1)}, f32[8,16,128]{2,1,0:T(8,128)}, u32[]{:S(2)}, u32[]{:S(2)}) collective-permute-start(f32[8,16,128]{2,1,0:T(8,128)S(1)} %collect_taps.1.rest_0_), channel_id=1, source_target_pairs={{0,2},{1,3},{2,0},{3,1},{4,6},{5,7},{6,4},{7,5},{8,10},{9,11},{10,... | collective-permute-start | bytes 196616 | tf_op jit(solution)/shard_map/ppermute | solution.py:833
  41.4 4.9 %collective-permute-start.9 = (f32[8,16,128]{2,1,0:T(8,128)S(1)}, f32[8,16,128]{2,1,0:T(8,128)}, u32[]{:S(2)}, u32[]{:S(2)}) collective-permute-start(f32[8,16,128]{2,1,0:T(8,128)S(1)} %collect_taps.1.rest_0_), channel_id=1, source_target_pairs={{0,3},{1,2},{2,1},{3,0},{4,7},{5,6},{6,5},{7,4},{8,11},{9,10},{10,... | collective-permute-start | bytes 196616 | tf_op jit(solution)/shard_map/ppermute | solution.py:833
  41.4 18.3 %collective-permute-start.13 = (f32[272,128]{1,0:T(8,128)}, f32[272,128]{1,0:T(8,128)S(1)}, u32[]{:S(2)}, u32[]{:S(2)}) collective-permute-start(f32[272,128]{1,0:T(8,128)} %get-tuple-element.63), channel_id=1, source_target_pairs={{0,16},{4,20},{8,24},{12,28},{16,0},{20,4},{24,8},{28,12},{1,17},{... | collective-permute-start | bytes 417800 | tf_op jit(solution)/shard_map/ppermute | solution.py:833
  43.3 16.4 %collective-permute-start.14 = (f32[272,128]{1,0:T(8,128)}, f32[272,128]{1,0:T(8,128)S(1)}, u32[]{:S(2)}, u32[]{:S(2)}) collective-permute-start(f32[272,128]{1,0:T(8,128)} %get-tuple-element.64), channel_id=1, source_target_pairs={{0,24},{4,28},{8,16},{12,20},{16,8},{20,12},{24,0},{28,4},{1,25},{... | collective-permute-start | bytes 417800 | tf_op jit(solution)/shard_map/ppermute | solution.py:833
  46.2 6.6 %copy-start.2 = (bf16[256,1536]{1,0:T(8,128)(2,1)S(1)}, bf16[256,1536]{1,0:T(8,128)(2,1)}, u32[]{:S(2)}) copy-start(bf16[256,1536]{1,0:T(8,128)(2,1)} %constant.14.clone.inverse) | copy-start | bytes 2359300
  46.2 6.6 %copy-start.7 = (f32[128,128]{1,0:T(8,128)S(1)}, f32[128,128]{1,0:T(8,128)}, u32[]{:S(2)}) copy-start(f32[128,128]{1,0:T(8,128)} %copy-done.6) | copy-start | bytes 196612
  56.0 12.5 %collective-permute-start.11 = (f32[256,128]{1,0:T(8,128)S(1)}, f32[256,128]{1,0:T(8,128)S(1)}, u32[]{:S(2)}, u32[]{:S(2)}) collective-permute-start(f32[256,128]{1,0:T(8,128)S(1)} %get-tuple-element.57), channel_id=1, source_target_pairs={{0,16},{4,20},{8,24},{12,28},{16,0},{20,4},{24,8},{28,12},{1,17},{... | collective-permute-start | bytes 393224 | tf_op jit(solution)/shard_map/ppermute | solution.py:833
  58.0 14.7 %collective-permute-start.12 = (f32[256,128]{1,0:T(8,128)S(1)}, f32[256,128]{1,0:T(8,128)S(1)}, u32[]{:S(2)}, u32[]{:S(2)}) collective-permute-start(f32[256,128]{1,0:T(8,128)S(1)} %get-tuple-element.58), channel_id=1, source_target_pairs={{0,20},{4,16},{8,28},{12,24},{16,4},{20,0},{24,12},{28,8},{1,21},{... | collective-permute-start | bytes 393224 | tf_op jit(solution)/shard_map/ppermute | solution.py:833
  59.7 14.7 %collective-permute-start.15 = (f32[256,128]{1,0:T(8,128)S(1)}, f32[256,128]{1,0:T(8,128)S(1)}, u32[]{:S(2)}, u32[]{:S(2)}) collective-permute-start(f32[256,128]{1,0:T(8,128)S(1)} %get-tuple-element.65), channel_id=1, source_target_pairs={{0,4},{4,0},{8,12},{12,8},{16,20},{20,16},{24,28},{28,24},{1,5},{5... | collective-permute-start | bytes 393224 | tf_op jit(solution)/shard_map/ppermute | solution.py:833
  60.5 14.0 %collective-permute-start.16 = (f32[256,128]{1,0:T(8,128)S(1)}, f32[256,128]{1,0:T(8,128)S(1)}, u32[]{:S(2)}, u32[]{:S(2)}) collective-permute-start(f32[256,128]{1,0:T(8,128)S(1)} %get-tuple-element.66), channel_id=1, source_target_pairs={{0,8},{4,12},{8,0},{12,4},{16,24},{20,28},{24,16},{28,20},{1,9},{5... | collective-permute-start | bytes 393224 | tf_op jit(solution)/shard_map/ppermute | solution.py:833
  62.2 12.3 %collective-permute-start.17 = (f32[256,128]{1,0:T(8,128)S(1)}, f32[256,128]{1,0:T(8,128)S(1)}, u32[]{:S(2)}, u32[]{:S(2)}) collective-permute-start(f32[256,128]{1,0:T(8,128)S(1)} %get-tuple-element.67), channel_id=1, source_target_pairs={{0,12},{4,8},{8,4},{12,0},{16,28},{20,24},{24,20},{28,16},{1,13},{... | collective-permute-start | bytes 393224 | tf_op jit(solution)/shard_map/ppermute | solution.py:833
  68.5 7.0 %collective-permute-start.18 = (f32[256,128]{1,0:T(8,128)S(1)}, f32[256,128]{1,0:T(8,128)S(1)}, u32[]{:S(2)}, u32[]{:S(2)}) collective-permute-start(f32[256,128]{1,0:T(8,128)S(1)} %get-tuple-element.70), channel_id=1, source_target_pairs={{0,24},{4,28},{8,16},{12,20},{16,8},{20,12},{24,0},{28,4},{1,25},{... | collective-permute-start | bytes 393224 | tf_op jit(solution)/shard_map/ppermute | solution.py:833
  72.7 7.8 %collective-permute-start.19 = (f32[256,128]{1,0:T(8,128)S(1)}, f32[256,128]{1,0:T(8,128)S(1)}, u32[]{:S(2)}, u32[]{:S(2)}) collective-permute-start(f32[256,128]{1,0:T(8,128)S(1)} %get-tuple-element.71), channel_id=1, source_target_pairs={{0,28},{4,24},{8,20},{12,16},{16,12},{20,8},{24,4},{28,0},{1,29},{... | collective-permute-start | bytes 393224 | tf_op jit(solution)/shard_map/ppermute | solution.py:833
  (3 other events, 9.2 us)
